TPU v7x, 32 devices: a whole 2x2x4 slice. The times are simulated.
32 devices in a mesh: gx: 8 (over z, x), gy: 4 (over y, core).
Axes of the slice: x: 2, y: 2, z: 4, core: 2. Of those that a mesh axis runs over, the one named last changes fastest.
Arguments:
- probes: bfloat16 [64, 64, 64, 128], P(None, 'gx', 'gy'), may hold values from -6 to 6
- permeability: float32 [64, 64, 128], P('gx', 'gy'), may hold values from 0.2 to 5
- absorption: float32 [64, 64, 128], P('gx', 'gy'), may hold values from 0.3 to 3
- sensitivity: float32 [64, 64, 128], P('gx', 'gy'), may hold values from -6 to 6
- observe_weight: float32 [64, 64, 128], P('gx', 'gy'), may hold values from 1 to 10
Outputs:
- q_basis: float32 [64, 64, 64, 128], P(None, 'gx', 'gy')
- r_factor: float32 [64, 64], replicated
All inputs are finite; a program needn't handle non-finite values.
Results may differ from a plain program's by a relative error of at most 0.0003.
Values sent between devices are 32-bit elements; how exact they have to be, the bound alone decides.
No kernel may reach another device: no remote copies, remote signals or barrier semaphores. Data moves between devices by JAX's collectives and lax.ppermute only.
A program may use at most 128 MiB of HBM per device.

v0:
```python
import jax
import jax.numpy as jnp
from jax import lax
from jax.sharding import PartitionSpec as P

SWEEPS = 4


def padded_2(shard, sides, width):
    for axis, dim in sides:
        peers, length = (lax.axis_size(axis), shard.shape[dim])
        up = [(i, (i + 1) % peers) for i in range(peers - 1)]
        down = [(j, i) for i, j in up]
        last = lax.slice_in_dim(shard, length - width, length, axis=dim)
        first = lax.slice_in_dim(shard, 0, width, axis=dim)
        before = lax.ppermute(last, axis, up)
        after = lax.ppermute(first, axis, down)
        shard = jnp.concatenate([before, shard, after], axis=dim)
    return shard


def face_terms(kpad, absorption):
    center = kpad[1:-1, 1:-1]
    x_low = 0.5 * (center + kpad[:-2, 1:-1])
    x_high = 0.5 * (center + kpad[2:, 1:-1])
    y_low = 0.5 * (center + kpad[1:-1, :-2])
    y_high = 0.5 * (center + kpad[1:-1, 2:])
    zpad = jnp.pad(center, ((0, 0), (0, 0), (1, 1)))
    z_low = 0.5 * (center + zpad[:, :, :-2])
    z_high = 0.5 * (center + zpad[:, :, 2:])
    diag = absorption + x_low + x_high + y_low + y_high + z_low + z_high
    return ((x_low, x_high, y_low, y_high, z_low, z_high), diag)


def sweep(field, padded, rhs, coefs, diag):
    x_low, x_high, y_low, y_high, z_low, z_high = coefs
    zpad = jnp.pad(field, ((0, 0), (0, 0), (0, 0), (1, 1)))
    total = x_low * padded[:, :-2, 1:-1] + x_high * padded[:, 2:, 1:-1]
    total = total + y_low * padded[:, 1:-1, :-2] + y_high * padded[:, 1:-1, 2:]
    total = total + z_low * zpad[..., :-2] + z_high * zpad[..., 2:]
    return 0.2 * field + 0.8 * (rhs + total) / diag


def single_solve(rhs, coefs, diag):
    field = 0.8 * rhs / diag
    for step in range(SWEEPS - 1):
        padded = padded_2(field, (("gx", 1), ("gy", 2)), 1)
        field = sweep(field, padded, rhs, coefs, diag)
    return field


def lower_inverse(lower):
    width = lower.shape[0]
    identity = jnp.eye(width, dtype=jnp.float32)

    def row_step(index, inverse):
        row = lax.dynamic_slice_in_dim(lower, index, 1, 0)
        pivot = lax.dynamic_slice(lower, (index, index), (1, 1))
        unit = lax.dynamic_slice_in_dim(identity, index, 1, 0)
        partial_sum = jnp.dot(
            row, inverse, precision=lax.Precision.HIGHEST, preferred_element_type=jnp.float32
        )
        new_row = (unit - partial_sum) / pivot
        return lax.dynamic_update_slice_in_dim(inverse, new_row, index, 0)

    return lax.fori_loop(0, width, row_step, jnp.zeros((width, width), jnp.float32))


def body(probes, permeability, absorption, sensitivity, observe_weight):
    count, width_x, width_y, width_z = probes.shape
    total_cells = width_x * lax.axis_size("gx") * width_y * lax.axis_size("gy") * width_z
    source = sensitivity * probes.astype(jnp.float32)
    kpad = padded_2(permeability, (("gx", 0), ("gy", 1)), 1)
    coefs, diag = face_terms(kpad, absorption)
    forward = single_solve(source, coefs, diag)
    adjoint = single_solve(observe_weight * forward, coefs, diag)
    responses = (sensitivity * adjoint).reshape(count, -1)
    gram = jnp.dot(
        responses, responses.T, precision=lax.Precision.HIGHEST, preferred_element_type=jnp.float32
    ) / float(total_cells)
    summed = lax.psum(gram, ("gx", "gy"))
    r_factor = jnp.linalg.cholesky(summed).T
    inverse = lower_inverse(r_factor.T)
    q_basis = jnp.dot(
        inverse, responses, precision=lax.Precision.HIGHEST, preferred_element_type=jnp.float32
    )
    return (q_basis.reshape(count, width_x, width_y, width_z), r_factor)


def solution(mesh):
    return jax.shard_map(
        body,
        mesh=mesh,
        in_specs=(
            P(None, "gx", "gy", None),
            P("gx", "gy", None),
            P("gx", "gy", None),
            P("gx", "gy", None),
            P("gx", "gy", None),
        ),
        out_specs=(P(None, "gx", "gy", None), P()),
        check_vma=False,
    )
```

profile of v0, /device:TPU:0, one launch (start us, length us, event | category | flops | bytes accessed | tf_op | source)
XLA Modules:
  0.0 463.9 jit_solution(4770731915882500182)
XLA Ops:
  28.3 20.7 %collective-permute-done.4 = f32[64,1,16,128]{3,0,2,1:T(8,128)S(1)} collective-permute-done((f32[64,1,16,128]{3,0,2,1:T(8,128)S(1)}, f32[64,1,16,128]{3,0,2,1:T(8,128)S(1)}, u32[]{:S(2)}, u32[]{:S(2)}) %collective-permute-start.4) | collective-permute-done | bytes 524320 | tf_op jit(solution)/shard_map/ppermute | solution.py:16
  56.2 7.8 %fusion.10 = f32[64,8,16,128]{3,0,2,1:T(8,128)S(1)} fusion(f32[64,8,16,128]{3,0,2,1:T(8,128)S(1)} %multiply_divide_fusion.1, f32[64,10,1,128]{3,0,2,1:T(8,128)S(1)} %collective-permute-done.7, f32[64,1,16,128]{3,0,2,1:T(8,128)S(1)} %collective-permute-done.5, f32[64,1,16,128]{3,0,2,1:T(8,128)S(1)} %collective-permute-done.4, ...), kind=kLoop, calls=%fused_computation.23 | loop fusion | flops 27262976 | bytes 12713984 | tf_op jit(solution)/shard_map/add | solution.py:41
  69.6 18.2 %collective-permute-done.8 = f32[64,1,16,128]{3,0,2,1:T(8,128)S(1)} collective-permute-done((f32[64,1,16,128]{3,0,2,1:T(8,128)S(1)}, f32[64,1,16,128]{3,0,2,1:T(8,128)S(1)}, u32[]{:S(2)}, u32[]{:S(2)}) %collective-permute-start.8) | collective-permute-done | bytes 524320 | tf_op jit(solution)/shard_map/ppermute | solution.py:16
  87.9 6.0 %collective-permute-start.10 = (f32[64,10,1,128]{3,0,2,1:T(8,128)S(1)}, f32[64,10,1,128]{3,0,2,1:T(8,128)S(1)}, u32[]{:S(2)}, u32[]{:S(2)}) collective-permute-start(f32[64,10,1,128]{3,0,2,1:T(8,128)S(1)} %get-tuple-element.115), channel_id=1, source_target_pairs={{0,1},{1,2},{2,3},{4,5},{5,6},{6,7},{8,9},{9,10},{10,11},{12,13},{... | collective-permute-start | bytes 983048 | tf_op jit(solution)/shard_map/ppermute | solution.py:16
  97.4 7.8 %fusion.18 = f32[64,8,16,128]{3,0,2,1:T(8,128)S(1)} fusion(f32[64,8,16,128]{3,0,2,1:T(8,128)S(1)} %fusion.10, f32[64,10,1,128]{3,0,2,1:T(8,128)S(1)} %collective-permute-done.11, f32[64,1,16,128]{3,0,2,1:T(8,128)S(1)} %collective-permute-done.9, f32[64,1,16,128]{3,0,2,1:T(8,128)S(1)} %collective-permute-done.8, ...), kind=kLoop, calls=%fused_computation.31 | loop fusion | flops 27262976 | bytes 12713984 | tf_op jit(solution)/shard_map/add | solution.py:41
  110.8 18.2 %collective-permute-done.12 = f32[64,1,16,128]{3,0,2,1:T(8,128)S(1)} collective-permute-done((f32[64,1,16,128]{3,0,2,1:T(8,128)S(1)}, f32[64,1,16,128]{3,0,2,1:T(8,128)S(1)}, u32[]{:S(2)}, u32[]{:S(2)}) %collective-permute-start.12) | collective-permute-done | bytes 524320 | tf_op jit(solution)/shard_map/ppermute | solution.py:16
  129.0 6.0 %collective-permute-start.14 = (f32[64,10,1,128]{3,0,2,1:T(8,128)S(1)}, f32[64,10,1,128]{3,0,2,1:T(8,128)S(1)}, u32[]{:S(2)}, u32[]{:S(2)}) collective-permute-start(f32[64,10,1,128]{3,0,2,1:T(8,128)S(1)} %get-tuple-element.113), channel_id=1, source_target_pairs={{0,1},{1,2},{2,3},{4,5},{5,6},{6,7},{8,9},{9,10},{10,11},{12,13},{... | collective-permute-start | bytes 983048 | tf_op jit(solution)/shard_map/ppermute | solution.py:16
  138.6 7.9 %multiply_divide_fusion = (f32[64,8,16,128]{3,0,2,1:T(8,128)S(1)}, f32[64,8,16,128]{3,0,2,1:T(8,128)S(1)}) fusion(f32[8,16,128]{2,1,0:T(8,128)S(1)} %get-tuple-element.100, f32[8,16,128]{2,1,0:T(8,128)S(1)} %get-tuple-element.106, f32[64,8,16,128]{3,0,2,1:T(8,128)S(1)} %fusion.18, f32[8,16,128]{2,1,0:T(8,128)S(1)} %get-tuple-element.105, ...), kind=kLoop, calls=%fused_computation.158 | loop fusion | flops 30408704 | bytes 16973824 | tf_op jit(solution)/shard_map/div | solution.py:45
  152.1 18.1 %collective-permute-done.16 = f32[64,1,16,128]{3,0,2,1:T(8,128)S(1)} collective-permute-done((f32[64,1,16,128]{3,0,2,1:T(8,128)S(1)}, f32[64,1,16,128]{3,0,2,1:T(8,128)S(1)}, u32[]{:S(2)}, u32[]{:S(2)}) %collective-permute-start.16) | collective-permute-done | bytes 524320 | tf_op jit(solution)/shard_map/ppermute | solution.py:16
  170.2 6.1 %collective-permute-start.18 = (f32[64,10,1,128]{3,0,2,1:T(8,128)S(1)}, f32[64,10,1,128]{3,0,2,1:T(8,128)S(1)}, u32[]{:S(2)}, u32[]{:S(2)}) collective-permute-start(f32[64,10,1,128]{3,0,2,1:T(8,128)S(1)} %get-tuple-element.111), channel_id=1, source_target_pairs={{0,1},{1,2},{2,3},{4,5},{5,6},{6,7},{8,9},{9,10},{10,11},{12,13},{... | collective-permute-start | bytes 983048 | tf_op jit(solution)/shard_map/ppermute | solution.py:16
  179.9 13.2 %fusion.34 = f32[64,8,16,128]{3,0,2,1:T(8,128)S(1)} fusion(f32[64,8,16,128]{3,0,2,1:T(8,128)S(1)} %get-tuple-element.99, f32[64,8,16,128]{3,0,2,1:T(8,128)} %copy-done.4, f32[64,10,1,128]{3,0,2,1:T(8,128)S(1)} %collective-permute-done.19, f32[64,1,16,128]{3,0,2,1:T(8,128)S(1)} %collective-permute-done.17, f32[64,1,16,128]{3,0,2,1:T(8,128)S(1)} %collective-permute-done.16, ...), kind=kLoop, calls=%fused_computation.47 | loop fusion | flops 25165824 | bytes 14745600 | tf_op jit(solution)/shard_map/add | solution.py:41
  198.6 7.0 %collective-permute-done.20 = f32[64,1,16,128]{3,0,2,1:T(8,128)S(1)} collective-permute-done((f32[64,1,16,128]{3,0,2,1:T(8,128)S(1)}, f32[64,1,16,128]{3,0,2,1:T(8,128)S(1)}, u32[]{:S(2)}, u32[]{:S(2)}) %collective-permute-start.20) | collective-permute-done | bytes 524320 | tf_op jit(solution)/shard_map/ppermute | solution.py:16
  205.6 7.3 %collective-permute-done.21 = f32[64,1,16,128]{3,0,2,1:T(8,128)S(1)} collective-permute-done((f32[64,1,16,128]{3,0,2,1:T(8,128)S(1)}, f32[64,1,16,128]{3,0,2,1:T(8,128)S(1)}, u32[]{:S(2)}, u32[]{:S(2)}) %collective-permute-start.21) | collective-permute-done | bytes 524320 | tf_op jit(solution)/shard_map/ppermute | solution.py:17
  213.0 9.9 %collective-permute-start.22 = (f32[64,10,1,128]{3,0,2,1:T(8,128)S(1)}, f32[64,10,1,128]{3,0,2,1:T(8,128)S(1)}, u32[]{:S(2)}, u32[]{:S(2)}) collective-permute-start(f32[64,10,1,128]{3,0,2,1:T(8,128)S(1)} %get-tuple-element.109), channel_id=1, source_target_pairs={{0,1},{1,2},{2,3},{4,5},{5,6},{6,7},{8,9},{9,10},{10,11},{12,13},{... | collective-permute-start | bytes 983048 | tf_op jit(solution)/shard_map/ppermute | solution.py:16
  226.5 13.2 %fusion.42 = f32[64,8,16,128]{3,0,2,1:T(8,128)S(1)} fusion(f32[64,8,16,128]{3,0,2,1:T(8,128)S(1)} %get-tuple-element.99, f32[64,8,16,128]{3,0,2,1:T(8,128)} %copy-done.3, f32[64,10,1,128]{3,0,2,1:T(8,128)S(1)} %collective-permute-done.23, f32[64,1,16,128]{3,0,2,1:T(8,128)S(1)} %collective-permute-done.21, f32[64,1,16,128]{3,0,2,1:T(8,128)S(1)} %collective-permute-done.20, ...), kind=kLoop, calls=%fused_computation.55 | loop fusion | flops 25165824 | bytes 14745600 | tf_op jit(solution)/shard_map/add | solution.py:41
  245.2 7.0 %collective-permute-done.24 = f32[64,1,16,128]{3,0,2,1:T(8,128)S(1)} collective-permute-done((f32[64,1,16,128]{3,0,2,1:T(8,128)S(1)}, f32[64,1,16,128]{3,0,2,1:T(8,128)S(1)}, u32[]{:S(2)}, u32[]{:S(2)}) %collective-permute-start.24) | collective-permute-done | bytes 524320 | tf_op jit(solution)/shard_map/ppermute | solution.py:16
  252.2 8.4 %collective-permute-done.25 = f32[64,1,16,128]{3,0,2,1:T(8,128)S(1)} collective-permute-done((f32[64,1,16,128]{3,0,2,1:T(8,128)S(1)}, f32[64,1,16,128]{3,0,2,1:T(8,128)S(1)}, u32[]{:S(2)}, u32[]{:S(2)}) %collective-permute-start.25) | collective-permute-done | bytes 524320 | tf_op jit(solution)/shard_map/ppermute | solution.py:17
  260.7 8.8 %collective-permute-start.26 = (f32[64,10,1,128]{3,0,2,1:T(8,128)S(1)}, f32[64,10,1,128]{3,0,2,1:T(8,128)S(1)}, u32[]{:S(2)}, u32[]{:S(2)}) collective-permute-start(f32[64,10,1,128]{3,0,2,1:T(8,128)S(1)} %get-tuple-element.107), channel_id=1, source_target_pairs={{0,1},{1,2},{2,3},{4,5},{5,6},{6,7},{8,9},{9,10},{10,11},{12,13},{... | collective-permute-start | bytes 983048 | tf_op jit(solution)/shard_map/ppermute | solution.py:16
  273.1 14.5 %fusion.97 = f32[64,8,16,128]{3,0,2,1:T(8,128)S(1)} fusion(f32[64,8,16,128]{3,0,2,1:T(8,128)} %copy-done, f32[64,8,16,128]{3,0,2,1:T(8,128)} %copy-done.2, f32[64,10,1,128]{3,0,2,1:T(8,128)S(1)} %collective-permute-done.27, f32[64,1,16,128]{3,0,2,1:T(8,128)S(1)} %collective-permute-done.25, f32[64,1,16,128]{3,0,2,1:T(8,128)S(1)} %collective-permute-done.24, ...), kind=kLoop, calls=%fused_computation.162 | loop fusion | flops 26214400 | bytes 14811136 | tf_op jit(solution)/shard_map/mul | solution.py:77
  293.0 48.9 %psum.7 = f32[64,64]{0,1:T(8,128)S(1)} all-reduce(f32[64,64]{0,1:T(8,128)S(1)} %fusion.98), channel_id=1, replica_groups=mesh['gx'=8,'gy'=4] {'gx','gy'}, use_global_device_ids=true, to_apply=%region_0.1 | all-reduce | flops 4096 | bytes 32768 | tf_op jit(solution)/shard_map/psum | solution.py:81
  341.9 5.8 %cholesky.19 = f32[64,64]{1,0:T(8,128)S(1)} custom-call(f32[64,64]{1,0:T(8,128)S(1)} %fusion.112), custom_call_target="Cholesky" | custom-call | tf_op jit(solution)/shard_map/jit(cholesky)/cholesky | solution.py:82
  349.8 6.6 %copy.29 = f32[64,8,16,128]{3,2,1,0:T(8,128)} copy(f32[64,8,16,128]{3,0,2,1:T(8,128)} %copy-done.1) | data formatting | bytes 8388608 | tf_op jit(solution)/shard_map/mul | solution.py:77
  357.1 90.6 %while.13 = (s32[]{:T(128)}, f32[64,64]{1,0:T(8,128)S(1)}, f32[64,64]{1,0:T(8,128)S(1)}, f32[64,64]{1,0:T(8,128)S(1)}, s32[]{:T(128)}, /*index=5*/s32[]{:T(128)}) while((s32[]{:T(128)}, f32[64,64]{1,0:T(8,128)S(1)}, f32[64,64]{1,0:T(8,128)S(1)}, f32[64,64]{1,0:T(8,128)S(1)}, s32[]{:T(128)}, /*index=5*/s32[]{:T(128)}) %tuple.57), condition=%wide.region_4.5_spmd, body=%wide.region_3.4_spmd.sunk | while | flops 49282 | bytes 36181 | solution.py:66
  453.0 6.0 %fusion.94 = f32[64,8,16,128]{3,0,2,1:T(8,128)S(1)} fusion(f32[8,16,128,64]{2,1,0,3:T(8,128)S(1)} %bitcast.44, f32[64,64]{1,0:T(8,128)S(1)} %get-tuple-element.81), kind=kOutput, calls=%fused_computation.156 | convolution fusion | flops 805306368 | bytes 8404992 | tf_op jit(solution)/shard_map/dot_general | solution.py:84
  (283 shorter events, 187.2 us)
Async XLA Ops:
  1.3 6.2 %collective-permute-start = (f32[1,16,128]{2,1,0:T(8,128)S(1)}, f32[1,16,128]{2,1,0:T(8,128)S(1)}, u32[]{:S(2)}, u32[]{:S(2)}) collective-permute-start(f32[1,16,128]{2,1,0:T(8,128)S(1)} %get-tuple-element.134), channel_id=1, source_target_pairs={{0,4},{4,8},{8,12},{12,16},{16,20},{20,24},{24,28},{1,5},{5,9},{9,... | collective-permute-start | bytes 24584 | tf_op jit(solution)/shard_map/ppermute | solution.py:16
  6.2 5.5 %collective-permute-start.1 = (f32[1,16,128]{2,1,0:T(8,128)S(1)}, f32[1,16,128]{2,1,0:T(8,128)S(1)}, u32[]{:S(2)}, u32[]{:S(2)}) collective-permute-start(f32[1,16,128]{2,1,0:T(8,128)S(1)} %get-tuple-element.133), channel_id=1, source_target_pairs={{4,0},{8,4},{12,8},{16,12},{20,16},{24,20},{28,24},{5,1},{9,5},{13... | collective-permute-start | bytes 24584 | tf_op jit(solution)/shard_map/ppermute | solution.py:17
  13.0 4.8 %collective-permute-start.3 = (f32[10,1,128]{2,1,0:T(1,128)S(1)}, f32[10,1,128]{2,1,0:T(1,128)S(1)}, u32[]{:S(2)}, u32[]{:S(2)}) collective-permute-start(f32[10,1,128]{2,1,0:T(1,128)S(1)} %get-tuple-element.131), channel_id=1, source_target_pairs={{1,0},{2,1},{3,2},{5,4},{6,5},{7,6},{9,8},{10,9},{11,10},{13,12},{... | collective-permute-start | bytes 15368 | tf_op jit(solution)/shard_map/ppermute | solution.py:17
  22.5 26.6 %collective-permute-start.4 = (f32[64,1,16,128]{3,0,2,1:T(8,128)S(1)}, f32[64,1,16,128]{3,0,2,1:T(8,128)S(1)}, u32[]{:S(2)}, u32[]{:S(2)}) collective-permute-start(f32[64,1,16,128]{3,0,2,1:T(8,128)S(1)} %get-tuple-element.129), channel_id=1, source_target_pairs={{0,4},{4,8},{8,12},{12,16},{16,20},{20,24},{24,28},{1,5},{5,9},{9,... | collective-permute-start | bytes 1572872 | tf_op jit(solution)/shard_map/ppermute | solution.py:16
  27.0 22.0 %collective-permute-start.5 = (f32[64,1,16,128]{3,0,2,1:T(8,128)S(1)}, f32[64,1,16,128]{3,0,2,1:T(8,128)S(1)}, u32[]{:S(2)}, u32[]{:S(2)}) collective-permute-start(f32[64,1,16,128]{3,0,2,1:T(8,128)S(1)} %get-tuple-element.130), channel_id=1, source_target_pairs={{4,0},{8,4},{12,8},{16,12},{20,16},{24,20},{28,24},{5,1},{9,5},{13... | collective-permute-start | bytes 1572872 | tf_op jit(solution)/shard_map/ppermute | solution.py:17
  49.1 4.8 %collective-permute-start.6 = (f32[64,10,1,128]{3,0,2,1:T(8,128)S(1)}, f32[64,10,1,128]{3,0,2,1:T(8,128)S(1)}, u32[]{:S(2)}, u32[]{:S(2)}) collective-permute-start(f32[64,10,1,128]{3,0,2,1:T(8,128)S(1)} %get-tuple-element.117), channel_id=1, source_target_pairs={{0,1},{1,2},{2,3},{4,5},{5,6},{6,7},{8,9},{9,10},{10,11},{12,13},{... | collective-permute-start | bytes 983048 | tf_op jit(solution)/shard_map/ppermute | solution.py:16
  52.7 3.5 collective-permute-start.7
  64.1 23.7 %collective-permute-start.8 = (f32[64,1,16,128]{3,0,2,1:T(8,128)S(1)}, f32[64,1,16,128]{3,0,2,1:T(8,128)S(1)}, u32[]{:S(2)}, u32[]{:S(2)}) collective-permute-start(f32[64,1,16,128]{3,0,2,1:T(8,128)S(1)} %get-tuple-element.127), channel_id=1, source_target_pairs={{0,4},{4,8},{8,12},{12,16},{16,20},{20,24},{24,28},{1,5},{5,9},{9,... | collective-permute-start | bytes 1572872 | tf_op jit(solution)/shard_map/ppermute | solution.py:16
  68.3 19.5 %collective-permute-start.9 = (f32[64,1,16,128]{3,0,2,1:T(8,128)S(1)}, f32[64,1,16,128]{3,0,2,1:T(8,128)S(1)}, u32[]{:S(2)}, u32[]{:S(2)}) collective-permute-start(f32[64,1,16,128]{3,0,2,1:T(8,128)S(1)} %get-tuple-element.128), channel_id=1, source_target_pairs={{4,0},{8,4},{12,8},{16,12},{20,16},{24,20},{28,24},{5,1},{9,5},{13... | collective-permute-start | bytes 1572872 | tf_op jit(solution)/shard_map/ppermute | solution.py:17
  87.9 7.3 %collective-permute-start.10 = (f32[64,10,1,128]{3,0,2,1:T(8,128)S(1)}, f32[64,10,1,128]{3,0,2,1:T(8,128)S(1)}, u32[]{:S(2)}, u32[]{:S(2)}) collective-permute-start(f32[64,10,1,128]{3,0,2,1:T(8,128)S(1)} %get-tuple-element.115), channel_id=1, source_target_pairs={{0,1},{1,2},{2,3},{4,5},{5,6},{6,7},{8,9},{9,10},{10,11},{12,13},{... | collective-permute-start | bytes 983048 | tf_op jit(solution)/shard_map/ppermute | solution.py:16
  93.9 3.5 collective-permute-start.11
  105.3 23.7 %collective-permute-start.12 = (f32[64,1,16,128]{3,0,2,1:T(8,128)S(1)}, f32[64,1,16,128]{3,0,2,1:T(8,128)S(1)}, u32[]{:S(2)}, u32[]{:S(2)}) collective-permute-start(f32[64,1,16,128]{3,0,2,1:T(8,128)S(1)} %get-tuple-element.125), channel_id=1, source_target_pairs={{0,4},{4,8},{8,12},{12,16},{16,20},{20,24},{24,28},{1,5},{5,9},{9,... | collective-permute-start | bytes 1572872 | tf_op jit(solution)/shard_map/ppermute | solution.py:16
  109.5 19.5 %collective-permute-start.13 = (f32[64,1,16,128]{3,0,2,1:T(8,128)S(1)}, f32[64,1,16,128]{3,0,2,1:T(8,128)S(1)}, u32[]{:S(2)}, u32[]{:S(2)}) collective-permute-start(f32[64,1,16,128]{3,0,2,1:T(8,128)S(1)} %get-tuple-element.126), channel_id=1, source_target_pairs={{4,0},{8,4},{12,8},{16,12},{20,16},{24,20},{28,24},{5,1},{9,5},{13... | collective-permute-start | bytes 1572872 | tf_op jit(solution)/shard_map/ppermute | solution.py:17
  129.0 7.3 %collective-permute-start.14 = (f32[64,10,1,128]{3,0,2,1:T(8,128)S(1)}, f32[64,10,1,128]{3,0,2,1:T(8,128)S(1)}, u32[]{:S(2)}, u32[]{:S(2)}) collective-permute-start(f32[64,10,1,128]{3,0,2,1:T(8,128)S(1)} %get-tuple-element.113), channel_id=1, source_target_pairs={{0,1},{1,2},{2,3},{4,5},{5,6},{6,7},{8,9},{9,10},{10,11},{12,13},{... | collective-permute-start | bytes 983048 | tf_op jit(solution)/shard_map/ppermute | solution.py:16
  135.1 3.5 collective-permute-start.15
  146.6 23.5 %collective-permute-start.16 = (f32[64,1,16,128]{3,0,2,1:T(8,128)S(1)}, f32[64,1,16,128]{3,0,2,1:T(8,128)S(1)}, u32[]{:S(2)}, u32[]{:S(2)}) collective-permute-start(f32[64,1,16,128]{3,0,2,1:T(8,128)S(1)} %get-tuple-element.123), channel_id=1, source_target_pairs={{0,4},{4,8},{8,12},{12,16},{16,20},{20,24},{24,28},{1,5},{5,9},{9,... | collective-permute-start | bytes 1572872 | tf_op jit(solution)/shard_map/ppermute | solution.py:16
  150.8 19.4 %collective-permute-start.17 = (f32[64,1,16,128]{3,0,2,1:T(8,128)S(1)}, f32[64,1,16,128]{3,0,2,1:T(8,128)S(1)}, u32[]{:S(2)}, u32[]{:S(2)}) collective-permute-start(f32[64,1,16,128]{3,0,2,1:T(8,128)S(1)} %get-tuple-element.124), channel_id=1, source_target_pairs={{4,0},{8,4},{12,8},{16,12},{20,16},{24,20},{28,24},{5,1},{9,5},{13... | collective-permute-start | bytes 1572872 | tf_op jit(solution)/shard_map/ppermute | solution.py:17
  170.2 7.6 %collective-permute-start.18 = (f32[64,10,1,128]{3,0,2,1:T(8,128)S(1)}, f32[64,10,1,128]{3,0,2,1:T(8,128)S(1)}, u32[]{:S(2)}, u32[]{:S(2)}) collective-permute-start(f32[64,10,1,128]{3,0,2,1:T(8,128)S(1)} %get-tuple-element.111), channel_id=1, source_target_pairs={{0,1},{1,2},{2,3},{4,5},{5,6},{6,7},{8,9},{9,10},{10,11},{12,13},{... | collective-permute-start | bytes 983048 | tf_op jit(solution)/shard_map/ppermute | solution.py:16
  193.2 12.4 %collective-permute-start.20 = (f32[64,1,16,128]{3,0,2,1:T(8,128)S(1)}, f32[64,1,16,128]{3,0,2,1:T(8,128)S(1)}, u32[]{:S(2)}, u32[]{:S(2)}) collective-permute-start(f32[64,1,16,128]{3,0,2,1:T(8,128)S(1)} %get-tuple-element.121), channel_id=1, source_target_pairs={{0,4},{4,8},{8,12},{12,16},{16,20},{20,24},{24,28},{1,5},{5,9},{9,... | collective-permute-start | bytes 1572872 | tf_op jit(solution)/shard_map/ppermute | solution.py:16
  197.3 15.6 %collective-permute-start.21 = (f32[64,1,16,128]{3,0,2,1:T(8,128)S(1)}, f32[64,1,16,128]{3,0,2,1:T(8,128)S(1)}, u32[]{:S(2)}, u32[]{:S(2)}) collective-permute-start(f32[64,1,16,128]{3,0,2,1:T(8,128)S(1)} %get-tuple-element.122), channel_id=1, source_target_pairs={{4,0},{8,4},{12,8},{16,12},{20,16},{24,20},{28,24},{5,1},{9,5},{13... | collective-permute-start | bytes 1572872 | tf_op jit(solution)/shard_map/ppermute | solution.py:17
  213.0 11.2 %collective-permute-start.22 = (f32[64,10,1,128]{3,0,2,1:T(8,128)S(1)}, f32[64,10,1,128]{3,0,2,1:T(8,128)S(1)}, u32[]{:S(2)}, u32[]{:S(2)}) collective-permute-start(f32[64,10,1,128]{3,0,2,1:T(8,128)S(1)} %get-tuple-element.109), channel_id=1, source_target_pairs={{0,1},{1,2},{2,3},{4,5},{5,6},{6,7},{8,9},{9,10},{10,11},{12,13},{... | collective-permute-start | bytes 983048 | tf_op jit(solution)/shard_map/ppermute | solution.py:16
  239.8 12.4 %collective-permute-start.24 = (f32[64,1,16,128]{3,0,2,1:T(8,128)S(1)}, f32[64,1,16,128]{3,0,2,1:T(8,128)S(1)}, u32[]{:S(2)}, u32[]{:S(2)}) collective-permute-start(f32[64,1,16,128]{3,0,2,1:T(8,128)S(1)} %get-tuple-element.119), channel_id=1, source_target_pairs={{0,4},{4,8},{8,12},{12,16},{16,20},{20,24},{24,28},{1,5},{5,9},{9,... | collective-permute-start | bytes 1572872 | tf_op jit(solution)/shard_map/ppermute | solution.py:16
  243.9 16.7 %collective-permute-start.25 = (f32[64,1,16,128]{3,0,2,1:T(8,128)S(1)}, f32[64,1,16,128]{3,0,2,1:T(8,128)S(1)}, u32[]{:S(2)}, u32[]{:S(2)}) collective-permute-start(f32[64,1,16,128]{3,0,2,1:T(8,128)S(1)} %get-tuple-element.120), channel_id=1, source_target_pairs={{4,0},{8,4},{12,8},{16,12},{20,16},{24,20},{28,24},{5,1},{9,5},{13... | collective-permute-start | bytes 1572872 | tf_op jit(solution)/shard_map/ppermute | solution.py:17
  260.7 10.4 %collective-permute-start.26 = (f32[64,10,1,128]{3,0,2,1:T(8,128)S(1)}, f32[64,10,1,128]{3,0,2,1:T(8,128)S(1)}, u32[]{:S(2)}, u32[]{:S(2)}) collective-permute-start(f32[64,10,1,128]{3,0,2,1:T(8,128)S(1)} %get-tuple-element.107), channel_id=1, source_target_pairs={{0,1},{1,2},{2,3},{4,5},{5,6},{6,7},{8,9},{9,10},{10,11},{12,13},{... | collective-permute-start | bytes 983048 | tf_op jit(solution)/shard_map/ppermute | solution.py:16
  (12 other events, 281.6 us)
where the time goes:
time: 473 us; the launch traced here: 464 us
  waiting for transfers between devices  125 us (26%)
  starting transfers between devices  90.1 us (19%)
  other arithmetic  77.1 us (16%)
  local copies, waits for them, and re-layouts  60.6 us (13%)
  matrix products  59.4 us (13%)
  blocking collectives  48.9 us (10%)
    ppermute x14, waiting for transfers between devices, padded_2(): before = lax.ppermute(last, axis, up)  89.4 us
    ppermute x14, starting transfers between devices, padded_2(): before = lax.ppermute(last, axis, up)  71.6 us
    dot_general x64, matrix products, row_step(): jnp.dot(row, inverse, precision=lax.Precision.HIGHEST, preferred_element_...  50 us
    psum x1, blocking collectives, body(): summed = lax.psum(gram, ('gx', 'gy'))  48.9 us
    add x4, other arithmetic, sweep(): return 0.2 * field + 0.8 * (rhs + total) / diag  42 us
    dynamic_slice x64, local copies, waits for them, and re-layouts, row_step(): pivot = lax.dynamic_slice(lower, (index, index), (1, 1))  37.6 us
    ppermute x14, waiting for transfers between devices, padded_2(): after = lax.ppermute(first, axis, down)  35.5 us
    ppermute x14, starting transfers between devices, padded_2(): after = lax.ppermute(first, axis, down)  18.5 us
  transfers between devices with their start and end apart: 28, of which 16 were waited for; matrix products, arithmetic and copies ran while one was open for 0% of the time, Pallas kernels for 0%

commit v1 on v0

v1 whole, which is shorter than its diff:
```python
import functools

import jax
import jax.numpy as jnp
from jax import lax
from jax.experimental import pallas as pl
from jax.experimental.pallas import tpu as pltpu
from jax.sharding import PartitionSpec as P

OMEGA = 0.8
KEEP = 1.0 - OMEGA
A0 = 1.0 + KEEP + KEEP**2 + KEEP**3
A1 = 1.0 + 2.0 * KEEP + 3.0 * KEEP**2
A2 = 1.0 + 3.0 * KEEP
A3 = 1.0
DEPTH = 6
HALF = 32
GROUPS = (1, 1, 1, 1)
MIB = 1 << 20


def smem():
    return pl.BlockSpec(memory_space=pltpu.SMEM)


def vmem():
    return pl.BlockSpec(memory_space=pltpu.VMEM)


def prep_kernel(h_ref, mine_ref, theirs_ref, own_ref, send_ref, edge_ref, wide):
    planes, rows = mine_ref.shape[1], mine_ref.shape[2]
    side = h_ref[0]
    for source, target in ((theirs_ref, send_ref), (mine_ref, own_ref)):
        wide[...] = source[...].astype(jnp.float32).reshape(wide.shape)

        def plane(x, carry):
            for y in range(rows):
                target[x, y] = wide[pl.ds(x * rows + y, 8, stride=planes * rows), :]
            return carry

        lax.fori_loop(0, planes, plane, 0)
    edge_ref[...] = own_ref[pl.ds(side * (planes - DEPTH), DEPTH)]


def prep(side, probes, tile):
    planes, rows, depth = probes.shape[1:]
    block = (8, planes, rows, depth)
    per_half = HALF // 8
    whole = jax.ShapeDtypeStruct((planes, rows, 8, depth), jnp.float32)
    edge = jax.ShapeDtypeStruct((DEPTH, rows, 8, depth), jnp.float32)
    return pl.pallas_call(
        prep_kernel,
        grid_spec=pltpu.PrefetchScalarGridSpec(
            num_scalar_prefetch=1,
            grid=(1,),
            in_specs=[
                pl.BlockSpec(block, lambda i, h: (h[0] * per_half + tile, 0, 0, 0)),
                pl.BlockSpec(block, lambda i, h: ((1 - h[0]) * per_half + tile, 0, 0, 0)),
            ],
            out_specs=[
                pl.BlockSpec(whole.shape, lambda i, h: (0, 0, 0, 0)),
                pl.BlockSpec(whole.shape, lambda i, h: (0, 0, 0, 0)),
                pl.BlockSpec(edge.shape, lambda i, h: (0, 0, 0, 0)),
            ],
            scratch_shapes=[pltpu.VMEM((8 * planes * rows, depth), jnp.float32)],
        ),
        out_shape=[whole, whole, edge],
        compiler_params=pltpu.CompilerParams(vmem_limit_bytes=12 * MIB),
        cost_estimate=pl.CostEstimate(flops=0, bytes_accessed=2 * MIB, transcendentals=0),
        name="spread_probes",
    )(side, probes, probes)


def solve_kernel(h_ref, coef, own, recv, e1, e2, ylo, yhi, keep, back, r_s, a_s, b_s):
    planes, rows = own.shape[0], own.shape[1]
    wide_x, wide_y = r_s.shape[0], r_s.shape[1]
    side = h_ref[0]
    top = DEPTH + 2 * planes
    parts = (
        (own, 0, planes, DEPTH + planes * side),
        (recv, planes, planes, DEPTH + planes * (1 - side)),
        (e1, 2 * planes, DEPTH, top * (1 - side)),
        (e2, 2 * planes + DEPTH, DEPTH, top * side),
    )

    def row(which, x, y):
        return coef[which, x, pl.ds(y, 1), :]

    for piece, role, count, place in parts:

        def fill(i, carry, piece=piece, role=role, place=place):
            x = place + i
            for y in range(wide_y):
                if y < DEPTH:
                    value = ylo[role + i, y]
                elif y < DEPTH + rows:
                    value = piece[i, y - DEPTH]
                else:
                    value = yhi[role + i, y - DEPTH - rows]
                r_s[x, y] = value * row(6, x, y)
            return carry

        lax.fori_loop(0, count, fill, 0)

    def stencil(src, r, x, y, scale):
        here = src[x, y]
        total = row(0, x, y) * src[x - 1, y] + row(1, x, y) * src[x + 1, y]
        total = total + row(2, x, y) * src[x, y - 1] + row(3, x, y) * src[x, y + 1]
        total = total + row(4, x, y) * pltpu.roll(here, 1, 1) + row(5, x, y) * pltpu.roll(here, 127, 1)
        return r[x, y] + scale * total

    def sweep(src, dst, r, low, scale, last=None):
        def plane(x, carry):
            for y in range(low, wide_y - low):
                value = stencil(src, r, x, y, scale)
                if last is not None:
                    value = value * row(last, x, y)
                dst[x, y] = value
            return carry

        lax.fori_loop(low, wide_x - low, plane, 0)

    sweep(r_s, a_s, r_s, 1, A3 / A2)
    sweep(a_s, b_s, r_s, 2, A2 / A1)
    sweep(b_s, a_s, r_s, 3, A1 / A0, last=7)
    sweep(a_s, b_s, a_s, 4, A3 / A2)
    sweep(b_s, r_s, a_s, 5, A2 / A1)
    for target, place in ((back, parts[1][3]), (keep, parts[0][3])):

        def out(i, carry, target=target, place=place):
            x = place + i
            for y in range(rows):
                target[i, y] = stencil(r_s, a_s, x, y + DEPTH, A1 / A0) * row(8, x, y + DEPTH)
            return carry

        lax.fori_loop(0, planes, out, 0)


def solve(side, coef, own, recv, e1, e2, ylo, yhi):
    wide_x, wide_y = coef.shape[1], coef.shape[2]
    many, depth = own.shape[2:]
    field = pltpu.VMEM((wide_x, wide_y, many, depth), jnp.float32)
    cells = wide_x * wide_y * many * depth
    return pl.pallas_call(
        solve_kernel,
        in_specs=[smem()] + [vmem()] * 7,
        out_specs=[vmem(), vmem()],
        out_shape=[jax.ShapeDtypeStruct(own.shape, jnp.float32)] * 2,
        scratch_shapes=[field, field, field],
        compiler_params=pltpu.CompilerParams(vmem_limit_bytes=(14 + 14 * many // 8) * MIB),
        cost_estimate=pl.CostEstimate(flops=60 * cells, bytes_accessed=12 * MIB, transcendentals=0),
        name="both_solves",
    )(side, coef, own, recv, e1, e2, ylo, yhi)


def stacked(tiles, rows):
    return jnp.concatenate(
        [jnp.concatenate([t[0, y] for t in tiles], axis=0) for y in range(rows)], axis=1
    )


def split(value):
    high = value.astype(jnp.bfloat16)
    return high, (value - high.astype(jnp.float32)).astype(jnp.bfloat16)


def gram_kernel(scale, h_ref, *refs):
    tiles, out, total = refs[:-2], refs[-2], refs[-1]
    step = pl.program_id(0)

    @pl.when(step == 0)
    def _():
        total[...] = jnp.zeros_like(total)

    both = jnp.concatenate(split(stacked(tiles, tiles[0].shape[1])), axis=0)
    total[...] += lax.dot_general(both, both, (((1,), (1,)), ((), ())), preferred_element_type=jnp.float32)

    @pl.when(step == pl.num_programs(0) - 1)
    def _():
        n = out.shape[0]
        g = total[:n, :n] + total[:n, n:] + total[n:, :n] + total[n:, n:]
        half = n // 2
        turned = jnp.concatenate([g[half:], g[:half]], axis=0)
        turned = jnp.concatenate([turned[:, half:], turned[:, :half]], axis=1)
        out[...] = jnp.where(h_ref[0] == 0, g, turned) * scale


def tile_spec(shape):
    return pl.BlockSpec((1,) + shape[1:], lambda i: (i, 0, 0, 0))


def gram_of(side, tiles, cells):
    count = 8 * len(tiles)
    return pl.pallas_call(
        functools.partial(gram_kernel, 1.0 / cells),
        grid=(tiles[0].shape[0],),
        in_specs=[smem()] + [tile_spec(t.shape) for t in tiles],
        out_specs=pl.BlockSpec((count, count), lambda i: (0, 0)),
        out_shape=jax.ShapeDtypeStruct((count, count), jnp.float32),
        scratch_shapes=[pltpu.VMEM((2 * count, 2 * count), jnp.float32)],
        compiler_params=pltpu.CompilerParams(vmem_limit_bytes=16 * MIB),
        cost_estimate=pl.CostEstimate(flops=0, bytes_accessed=6 * MIB, transcendentals=0),
        name="gram",
    )(side, *tiles)


def factor(gram):
    n = gram.shape[0]
    unit = (lax.broadcasted_iota(jnp.int32, (n, n), 0) == lax.broadcasted_iota(jnp.int32, (n, n), 1)).astype(jnp.float32)
    both = jnp.concatenate([gram, unit], axis=1)
    rows = [both[8 * i : 8 * i + 8] for i in range(n // 8)]
    place = lax.broadcasted_iota(jnp.int32, (8, 2 * n), 0)
    for j in range(n):
        t, s = divmod(j, 8)
        pivot = rows[t][s : s + 1]
        pivot = pivot * lax.rsqrt(pivot[:, j : j + 1])
        lead = pivot[:, j : j + 1]
        for i in range(t, n // 8):
            new = rows[i] - (rows[i][:, j : j + 1] / lead) * pivot
            if i == t:
                new = jnp.where(place > s, new, jnp.where(place == s, pivot, rows[i]))
            rows[i] = new
    done = jnp.concatenate(rows, axis=0)
    return done[:, :n], done[:, n:]


def basis_kernel(h_ref, a_ref, b_ref, *refs):
    tiles, (q_ref, r_ref, left) = refs[:-3], refs[-3:]
    n = r_ref.shape[0]
    rows = tiles[0].shape[1]

    @pl.when(pl.program_id(0) == 0)
    def _():
        upper, inverse = factor(a_ref[...] + b_ref[...])
        i = lax.broadcasted_iota(jnp.int32, (n, n), 0)
        j = lax.broadcasted_iota(jnp.int32, (n, n), 1)
        r_ref[...] = jnp.where(j >= i, upper, 0.0)
        inverse = jnp.where(j <= i, inverse, 0.0)
        turned = jnp.concatenate([inverse[:, n // 2 :], inverse[:, : n // 2]], axis=1)
        high, low = split(jnp.where(h_ref[0] == 0, inverse, turned))
        left[...] = jnp.concatenate([high, high, low, low], axis=1)

    high, low = split(stacked(tiles, rows))
    q = jnp.dot(left[...], jnp.concatenate([high, low, high, low], axis=0), preferred_element_type=jnp.float32)
    depth = q.shape[1] // rows
    flat = q_ref.reshape(n * rows, depth)
    for y in range(rows):
        flat[pl.ds(y, n, stride=rows), :] = q[:, y * depth : (y + 1) * depth]


def basis(side, a, b, tiles):
    n = a.shape[0]
    planes, rows, _, depth = tiles[0].shape
    full = pl.BlockSpec((n, n), lambda i: (0, 0))
    return pl.pallas_call(
        basis_kernel,
        grid=(planes,),
        in_specs=[smem(), full, full] + [tile_spec(t.shape) for t in tiles],
        out_specs=[pl.BlockSpec((n, 1, rows, depth), lambda i: (0, i, 0, 0)), full],
        out_shape=[
            jax.ShapeDtypeStruct((n, planes, rows, depth), jnp.float32),
            jax.ShapeDtypeStruct((n, n), jnp.float32),
        ],
        scratch_shapes=[pltpu.VMEM((n, 4 * n), jnp.bfloat16)],
        compiler_params=pltpu.CompilerParams(vmem_limit_bytes=24 * MIB),
        cost_estimate=pl.CostEstimate(flops=0, bytes_accessed=8 * MIB, transcendentals=0),
        name="basis",
    )(side, a, b, *tiles)


def swap(value):
    return lax.ppermute(value, "gx", [(i, i ^ 1) for i in range(lax.axis_size("gx"))])


def outward(value):
    n = lax.axis_size("gx")
    return lax.ppermute(value, "gx", [(i, i + 2 * (i % 2) * 2 - 2) for i in range(n) if 0 <= i + 4 * (i % 2) - 2 < n])


def inward(value):
    n = lax.axis_size("gx")
    return lax.ppermute(value, "gx", [(i, i + 2 - 4 * (i % 2)) for i in range(n) if 0 <= i + 2 - 4 * (i % 2) < n])


def above(value):
    n = lax.axis_size("gy")
    return lax.ppermute(value, "gy", [(i, i + 1) for i in range(n - 1)])


def below(value):
    n = lax.axis_size("gy")
    return lax.ppermute(value, "gy", [(i + 1, i) for i in range(n - 1)])


def summed(value):
    steps = []
    for axis in ("gy", "gx"):
        n = lax.axis_size(axis)
        assert n & (n - 1) == 0
        shift = 1
        while shift < n:
            steps.append((axis, shift, n))
            shift *= 2
    other = None
    for axis, shift, n in steps:
        if other is not None:
            value = value + other
        other = lax.ppermute(value, axis, [(i, i ^ shift) for i in range(n)])
    return value, other


def coefficients(side, permeability, absorption, sensitivity, observe_weight):
    planes, rows, depth = permeability.shape
    lower = side == 0
    ring = DEPTH + 1
    own = jnp.stack([permeability, absorption, sensitivity, observe_weight])
    recv = swap(own)
    e1 = outward(jnp.where(lower, own[:, :ring], own[:, planes - ring :]))
    e2 = inward(jnp.where(lower, recv[:, planes - ring :], recv[:, :ring]))
    tall = jnp.concatenate(
        [
            jnp.where(lower, e2, e1),
            jnp.where(lower, own, recv),
            jnp.where(lower, recv, own),
            jnp.where(lower, e1, e2),
        ],
        axis=1,
    )
    low = above(tall[:, :, rows - ring :])
    high = below(tall[:, :, :ring])
    k, absorb, sense, weight = jnp.concatenate([low, tall, high], axis=2)

    def shifted(dx, dy):
        return k[1 + dx : k.shape[0] - 1 + dx, 1 + dy : k.shape[1] - 1 + dy]

    mid = shifted(0, 0)
    faces = [0.5 * (mid + shifted(*d)) for d in ((-1, 0), (1, 0), (0, -1), (0, 1))]
    zpad = jnp.pad(mid, ((0, 0), (0, 0), (1, 1)))
    z_low = 0.5 * (mid + zpad[:, :, :-2])
    z_high = 0.5 * (mid + zpad[:, :, 2:])
    diag = absorb[1:-1, 1:-1] + sum(faces) + z_low + z_high

    def inside(axis, length, start, total):
        index = start - DEPTH + lax.broadcasted_iota(jnp.int32, diag.shape, axis)
        return (index >= 0) & (index < total)

    gx, gy = lax.axis_index("gx"), lax.axis_index("gy")
    here = inside(0, planes, (gx - side) * planes, planes * lax.axis_size("gx"))
    here = here & inside(1, rows, gy * rows, rows * lax.axis_size("gy"))
    inv = jnp.where(here, OMEGA / jnp.where(here, diag, 1.0), 0.0)
    z = lax.broadcasted_iota(jnp.int32, diag.shape, 2)
    z_low = jnp.where(z == 0, 0.0, z_low)
    z_high = jnp.where(z == depth - 1, 0.0, z_high)
    sense, weight = sense[1:-1, 1:-1], weight[1:-1, 1:-1]
    return jnp.stack([f * inv for f in faces] + [z_low * inv, z_high * inv, sense * inv, A0 * weight * inv, A0 * sense])


def body(probes, permeability, absorption, sensitivity, observe_weight):
    count, planes, rows, depth = probes.shape
    cells = planes * lax.axis_size("gx") * rows * lax.axis_size("gy") * depth
    side = lax.axis_index("gx") % 2
    flag = side.reshape(1).astype(jnp.int32)
    coef = coefficients(side, permeability, absorption, sensitivity, observe_weight)

    keeps, gots = [], []
    tile = 0
    for many in GROUPS:
        pieces = [prep(flag, probes, tile + i) for i in range(many)]
        tile += many
        own, send, edge = (jnp.concatenate(p, axis=2) if many > 1 else p[0] for p in zip(*pieces))
        recv = swap(send)
        e1 = outward(edge)
        e2 = inward(lax.dynamic_slice_in_dim(recv, (1 - side) * (planes - DEPTH), DEPTH, 0))
        ends = [(p[:, :DEPTH], p[:, rows - DEPTH :]) for p in (own, recv, e1, e2)]
        yhi = below(jnp.concatenate([first for first, _ in ends], axis=0))
        ylo = above(jnp.concatenate([last for _, last in ends], axis=0))
        keep, back = solve(flag, coef, own, recv, e1, e2, ylo, yhi)
        got = swap(back)
        for i in range(many):
            keeps.append(keep[:, :, 8 * i : 8 * i + 8] if many > 1 else keep)
            gots.append(got[:, :, 8 * i : 8 * i + 8] if many > 1 else got)
    tiles = keeps + gots
    a, b = summed(gram_of(flag, tiles, cells))
    q, r = basis(flag, a, b, tiles)
    return (q, r)


def solution(mesh):
    return jax.shard_map(
        body,
        mesh=mesh,
        in_specs=(
            P(None, "gx", "gy", None),
            P("gx", "gy", None),
            P("gx", "gy", None),
            P("gx", "gy", None),
            P("gx", "gy", None),
        ),
        out_specs=(P(None, "gx", "gy", None), P()),
        check_vma=False,
    )
```

time: 473 us -> 251 us (0.53); the launches traced: 464 us -> 250 us
  Pallas kernels: 0 us -> 87.4 us
  other arithmetic: 77.1 us -> 8.81 us
  waiting for transfers between devices: 125 us -> 65.4 us
  matrix products: 59.4 us -> 0 us
  blocking collectives: 48.9 us -> 0 us
  local copies, waits for them, and re-layouts: 60.6 us -> 15.2 us
  starting transfers between devices: 90.1 us -> 71.4 us
    pallas_call x0 -> x10, Pallas kernels: none -> 87.4 us  [the longest x4 64.4 us: solve(): pl.pallas_call(solve_kernel, in_specs=[smem()] + [vmem()] * 7, out_specs=...]
    ppermute x28 -> x34, waiting for transfers between devices: 125 us -> 65.4 us  [the longest x5 22.5 us: outward(): lax.ppermute(value, 'gx', [(i, i + 2 * (i % 2) * 2 - 2) for i in range(n)...]
    dot_general x66 -> x0, matrix products: 59.4 us -> none  [the longest x64 50 us: row_step(): jnp.dot(row, inverse, precision=lax.Precision.HIGHEST, preferred_element_...]
    psum x1 -> x0, blocking collectives: 48.9 us -> none  [body(): summed = lax.psum(gram, ('gx', 'gy'))]
    add x5 -> x4, other arithmetic: 43.2 us -> 0.02 us  [summed(): value = value + other]
    dynamic_slice x64 -> x4, local copies, waits for them, and re-layouts: 37.6 us -> 0.14 us  [body(): lax.dynamic_slice_in_dim(recv, (1 - side) * (planes - DEPTH), DEPTH, 0)]
    ppermute x28 -> x34, starting transfers between devices: 90.1 us -> 71.4 us  [the longest x5 20.4 us: above(): return lax.ppermute(value, 'gy', [(i, i + 1) for i in range(n - 1)])]
    mul x1 -> x0, other arithmetic: 14.5 us -> none  [body(): responses = (sensitivity * adjoint).reshape(count, -1)]
  transfers between devices with their start and end apart: 28 -> 34, of which waited for: 16 -> 14; matrix products, arithmetic and copies ran while one was open for 0% -> 6% of each run, Pallas kernels for 0% -> 28%
where the time goes in v1:
time: 251 us; the launch traced here: 250 us
  Pallas kernels  87.4 us (35%)
  starting transfers between devices  71.4 us (28%)
  waiting for transfers between devices  65.4 us (26%)
  local copies, waits for them, and re-layouts  15.2 us (6%)
  other arithmetic  8.81 us (4%)
    pallas_call x4, Pallas kernels, solve(): pl.pallas_call(solve_kernel, in_specs=[smem()] + [vmem()] * 7, out_specs=...  64.4 us
    ppermute x5, waiting for transfers between devices, outward(): lax.ppermute(value, 'gx', [(i, i + 2 * (i % 2) * 2 - 2) for i in range(n)...  22.5 us
    ppermute x5, starting transfers between devices, above(): return lax.ppermute(value, 'gy', [(i, i + 1) for i in range(n - 1)])  20.4 us
    ppermute x5, waiting for transfers between devices, inward(): lax.ppermute(value, 'gx', [(i, i + 2 - 4 * (i % 2)) for i in range(n) if...  18.3 us
    ppermute x5, starting transfers between devices, inward(): lax.ppermute(value, 'gx', [(i, i + 2 - 4 * (i % 2)) for i in range(n) if...  17.9 us
    pallas_call x1, Pallas kernels, basis(): pl.pallas_call(basis_kernel, grid=(planes,), in_specs=[smem(), full, full...  15.4 us
    ppermute x9, waiting for transfers between devices, swap(): lax.ppermute(value, 'gx', [(i, i ^ 1) for i in range(lax.axis_size('gx'))])  13.6 us
    ppermute x9, starting transfers between devices, swap(): lax.ppermute(value, 'gx', [(i, i ^ 1) for i in range(lax.axis_size('gx'))])  13.1 us
  transfers between devices with their start and end apart: 34, of which 14 were waited for; matrix products, arithmetic and copies ran while one was open for 6% of the time, Pallas kernels for 28%

profile of v1, /device:TPU:0, one launch (start us, length us, event | category | flops | bytes accessed | tf_op | source)
XLA Modules:
  0.0 249.6 jit_solution(11458980957967703228)
XLA Ops:
  2.3 2.9 %collective-permute-start = (f32[4,8,16,128]{3,2,1,0:T(8,128)}, f32[4,8,16,128]{3,2,1,0:T(8,128)}, u32[]{:S(2)}, u32[]{:S(2)}) collective-permute-start(f32[4,8,16,128]{3,2,1,0:T(8,128)} %pad_maximum_fusion.10), channel_id=1, source_target_pairs={{0,4},{4,0},{8,12},{12,8},{16,20},{20,16},{24,28},{28,24},{1,5},{5... | collective-permute-start | bytes 786440 | tf_op jit(solution)/shard_map/ppermute | solution.py:272
  11.6 3.4 %collective-permute-start.20 = (f32[8,16,8,128]{3,2,1,0:T(8,128)}, f32[8,16,8,128]{3,2,1,0:T(8,128)S(1)}, u32[]{:S(2)}, u32[]{:S(2)}) collective-permute-start(f32[8,16,8,128]{3,2,1,0:T(8,128)} %get-tuple-element.35), channel_id=1, source_target_pairs={{0,4},{4,0},{8,12},{12,8},{16,20},{20,16},{24,28},{28,24},{1,5},{5... | collective-permute-start | bytes 1572872 | tf_op jit(solution)/shard_map/ppermute | solution.py:272
  39.6 9.3 %collective-permute-done.16.e1 = f32[6,16,8,128]{3,2,1,0:T(8,128)S(1)} collective-permute-done((f32[6,16,8,128]{3,2,1,0:T(8,128)}, f32[6,16,8,128]{3,2,1,0:T(8,128)S(1)}, u32[]{:S(2)}, u32[]{:S(2)}) %collective-permute-start.16) | collective-permute-done | bytes 393248 | tf_op jit(solution)/shard_map/ppermute | solution.py:277
  50.2 7.1 %collective-permute-done.11.e1 = f32[6,16,8,128]{3,2,1,0:T(8,128)S(1)} collective-permute-done((f32[6,16,8,128]{3,2,1,0:T(8,128)}, f32[6,16,8,128]{3,2,1,0:T(8,128)S(1)}, u32[]{:S(2)}, u32[]{:S(2)}) %collective-permute-start.11) | collective-permute-done | bytes 393248 | tf_op jit(solution)/shard_map/ppermute | solution.py:277
  57.4 6.1 %collective-permute-done.6.e1 = f32[6,16,8,128]{3,2,1,0:T(8,128)S(1)} collective-permute-done((f32[6,16,8,128]{3,2,1,0:T(8,128)}, f32[6,16,8,128]{3,2,1,0:T(8,128)S(1)}, u32[]{:S(2)}, u32[]{:S(2)}) %collective-permute-start.6) | collective-permute-done | bytes 393248 | tf_op jit(solution)/shard_map/ppermute | solution.py:277
  63.5 3.5 %collective-permute-start.1 = (f32[4,7,16,128]{3,2,1,0:T(8,128)S(1)}, f32[4,7,16,128]{3,2,1,0:T(8,128)S(1)}, u32[]{:S(2)}, u32[]{:S(2)}) collective-permute-start(f32[4,7,16,128]{3,2,1,0:T(8,128)S(1)} %slice_select_fusion.1), channel_id=1, source_target_pairs={{0,8},{8,16},{12,4},{16,24},{20,12},{28,20},{1,9},{9,17},{13,5},{1... | collective-permute-start | bytes 688136 | tf_op jit(solution)/shard_map/ppermute | solution.py:282
  67.1 3.4 %collective-permute-done.1 = f32[4,7,16,128]{3,2,1,0:T(8,128)S(1)} collective-permute-done((f32[4,7,16,128]{3,2,1,0:T(8,128)S(1)}, f32[4,7,16,128]{3,2,1,0:T(8,128)S(1)}, u32[]{:S(2)}, u32[]{:S(2)}) %collective-permute-start.1) | collective-permute-done | bytes 229408 | tf_op jit(solution)/shard_map/ppermute | solution.py:282
  74.3 4.5 %collective-permute-start.22 = (f32[6,16,8,128]{3,2,1,0:T(8,128)S(1)}, f32[6,16,8,128]{3,2,1,0:T(8,128)S(1)}, u32[]{:S(2)}, u32[]{:S(2)}) collective-permute-start(f32[6,16,8,128]{3,2,1,0:T(8,128)S(1)} %constant_dynamic-slice_fusion), channel_id=1, source_target_pairs={{0,8},{8,16},{12,4},{16,24},{20,12},{28,20},{1,9},{9,17},{13,5},{1... | collective-permute-start | bytes 1179656 | tf_op jit(solution)/shard_map/ppermute | solution.py:282
  79.0 3.6 %collective-permute-start.17 = (f32[6,16,8,128]{3,2,1,0:T(8,128)S(1)}, f32[6,16,8,128]{3,2,1,0:T(8,128)S(1)}, u32[]{:S(2)}, u32[]{:S(2)}) collective-permute-start(f32[6,16,8,128]{3,2,1,0:T(8,128)S(1)} %constant_dynamic-slice_fusion.1), channel_id=1, source_target_pairs={{0,8},{8,16},{12,4},{16,24},{20,12},{28,20},{1,9},{9,17},{13,5},{1... | collective-permute-start | bytes 1179656 | tf_op jit(solution)/shard_map/ppermute | solution.py:282
  86.4 4.4 %collective-permute-start.7 = (f32[6,16,8,128]{3,2,1,0:T(8,128)S(1)}, f32[6,16,8,128]{3,2,1,0:T(8,128)S(1)}, u32[]{:S(2)}, u32[]{:S(2)}) collective-permute-start(f32[6,16,8,128]{3,2,1,0:T(8,128)S(1)} %constant_dynamic-slice_fusion.3), channel_id=1, source_target_pairs={{0,8},{8,16},{12,4},{16,24},{20,12},{28,20},{1,9},{9,17},{13,5},{1... | collective-permute-start | bytes 1179656 | tf_op jit(solution)/shard_map/ppermute | solution.py:282
  90.9 3.9 %collective-permute-done.17.e2 = f32[6,16,8,128]{3,2,1,0:T(8,128)S(1)} collective-permute-done((f32[6,16,8,128]{3,2,1,0:T(8,128)S(1)}, f32[6,16,8,128]{3,2,1,0:T(8,128)S(1)}, u32[]{:S(2)}, u32[]{:S(2)}) %collective-permute-start.17) | collective-permute-done | bytes 393248 | tf_op jit(solution)/shard_map/ppermute | solution.py:282
  94.8 5.9 %collective-permute-start.23 = (f32[28,6,8,128]{3,2,1,0:T(8,128)S(1)}, f32[28,6,8,128]{3,2,1,0:T(8,128)S(1)}, u32[]{:S(2)}, u32[]{:S(2)}) collective-permute-start(f32[28,6,8,128]{3,2,1,0:T(8,128)S(1)} %pad_maximum_fusion.8), channel_id=1, source_target_pairs={{0,1},{1,2},{2,3},{4,5},{5,6},{6,7},{8,9},{9,10},{10,11},{12,13},{... | collective-permute-start | bytes 2064392 | tf_op jit(solution)/shard_map/ppermute | solution.py:287
  104.6 7.1 %collective-permute-done.7.e2 = f32[6,16,8,128]{3,2,1,0:T(8,128)S(1)} collective-permute-done((f32[6,16,8,128]{3,2,1,0:T(8,128)S(1)}, f32[6,16,8,128]{3,2,1,0:T(8,128)S(1)}, u32[]{:S(2)}, u32[]{:S(2)}) %collective-permute-start.7) | collective-permute-done | bytes 393248 | tf_op jit(solution)/shard_map/ppermute | solution.py:282
  111.7 4.0 %collective-permute-start.18 = (f32[28,6,8,128]{3,2,1,0:T(8,128)S(1)}, f32[28,6,8,128]{3,2,1,0:T(8,128)S(1)}, u32[]{:S(2)}, u32[]{:S(2)}) collective-permute-start(f32[28,6,8,128]{3,2,1,0:T(8,128)S(1)} %pad_maximum_fusion.6), channel_id=1, source_target_pairs={{0,1},{1,2},{2,3},{4,5},{5,6},{6,7},{8,9},{9,10},{10,11},{12,13},{... | collective-permute-start | bytes 2064392 | tf_op jit(solution)/shard_map/ppermute | solution.py:287
  117.3 4.8 %collective-permute-start.13 = (f32[28,6,8,128]{3,2,1,0:T(8,128)S(1)}, f32[28,6,8,128]{3,2,1,0:T(8,128)S(1)}, u32[]{:S(2)}, u32[]{:S(2)}) collective-permute-start(f32[28,6,8,128]{3,2,1,0:T(8,128)S(1)} %pad_maximum_fusion.4), channel_id=1, source_target_pairs={{0,1},{1,2},{2,3},{4,5},{5,6},{6,7},{8,9},{9,10},{10,11},{12,13},{... | collective-permute-start | bytes 2064392 | tf_op jit(solution)/shard_map/ppermute | solution.py:287
  125.3 4.3 %collective-permute-start.8 = (f32[28,6,8,128]{3,2,1,0:T(8,128)S(1)}, f32[28,6,8,128]{3,2,1,0:T(8,128)S(1)}, u32[]{:S(2)}, u32[]{:S(2)}) collective-permute-start(f32[28,6,8,128]{3,2,1,0:T(8,128)S(1)} %pad_maximum_fusion.2), channel_id=1, source_target_pairs={{0,1},{1,2},{2,3},{4,5},{5,6},{6,7},{8,9},{9,10},{10,11},{12,13},{... | collective-permute-start | bytes 2064392 | tf_op jit(solution)/shard_map/ppermute | solution.py:287
  131.3 16.1 %both_solves.7 = (f32[8,16,8,128]{3,2,1,0:T(8,128)S(1)}, f32[8,16,8,128]{3,2,1,0:T(8,128)S(1)}) custom-call(s32[1]{0:T(128)} %bitcast.h_ref, f32[9,28,28,128]{3,2,1,0:T(8,128)S(1)} %bitcast_dynamic-update-slice_fusion.coef, f32[8,16,8,128]{3,2,1,0:T(8,128)S(1)} %copy-done.7, f32[8,16,8,128]{3,2,1,0:T(8,128)S(1)} %collective-permute-done.20.recv, ...), custom_call_target="tpu_custom_call" | custom-call | flops 48168960 | bytes 12582912 | tf_op jit(solution)/shard_map/both_solves/pallas_call | solution.py:144
  148.7 16.1 %both_solves.6 = (f32[8,16,8,128]{3,2,1,0:T(8,128)S(1)}, f32[8,16,8,128]{3,2,1,0:T(8,128)S(1)}) custom-call(s32[1]{0:T(128)} %bitcast.h_ref, f32[9,28,28,128]{3,2,1,0:T(8,128)S(1)} %bitcast_dynamic-update-slice_fusion.coef, f32[8,16,8,128]{3,2,1,0:T(8,128)S(1)} %copy-done.5, f32[8,16,8,128]{3,2,1,0:T(8,128)S(1)} %collective-permute-done.15.recv, ...), custom_call_target="tpu_custom_call" | custom-call | flops 48168960 | bytes 12582912 | tf_op jit(solution)/shard_map/both_solves/pallas_call | solution.py:144
  165.7 16.1 %both_solves.5 = (f32[8,16,8,128]{3,2,1,0:T(8,128)S(1)}, f32[8,16,8,128]{3,2,1,0:T(8,128)S(1)}) custom-call(s32[1]{0:T(128)} %bitcast.h_ref, f32[9,28,28,128]{3,2,1,0:T(8,128)S(1)} %bitcast_dynamic-update-slice_fusion.coef, f32[8,16,8,128]{3,2,1,0:T(8,128)S(1)} %copy-done.3, f32[8,16,8,128]{3,2,1,0:T(8,128)S(1)} %collective-permute-done.10.recv, ...), custom_call_target="tpu_custom_call" | custom-call | flops 48168960 | bytes 12582912 | tf_op jit(solution)/shard_map/both_solves/pallas_call | solution.py:144
  183.1 16.1 %both_solves.4 = (f32[8,16,8,128]{3,2,1,0:T(8,128)S(1)}, f32[8,16,8,128]{3,2,1,0:T(8,128)S(1)}) custom-call(s32[1]{0:T(128)} %bitcast.h_ref, f32[9,28,28,128]{3,2,1,0:T(8,128)S(1)} %bitcast_dynamic-update-slice_fusion.coef, f32[8,16,8,128]{3,2,1,0:T(8,128)S(1)} %copy-done.9, f32[8,16,8,128]{3,2,1,0:T(8,128)S(1)} %collective-permute-done.5.recv, ...), custom_call_target="tpu_custom_call" | custom-call | flops 48168960 | bytes 12582912 | tf_op jit(solution)/shard_map/both_solves/pallas_call | solution.py:144
  200.1 13.6 %collective-permute-done.25.refs_4_ = f32[8,16,8,128]{3,2,1,0:T(8,128)S(1)} collective-permute-done((f32[8,16,8,128]{3,2,1,0:T(8,128)S(1)}, f32[8,16,8,128]{3,2,1,0:T(8,128)S(1)}, u32[]{:S(2)}, u32[]{:S(2)}) %collective-permute-start.25) | collective-permute-done | bytes 524320 | tf_op jit(solution)/shard_map/ppermute | solution.py:272
  222.3 3.2 %collective-permute-done.31 = f32[64,64]{1,0:T(8,128)S(1)} collective-permute-done((f32[64,64]{1,0:T(8,128)S(1)}, f32[64,64]{1,0:T(8,128)S(1)}, u32[]{:S(2)}, u32[]{:S(2)}) %collective-permute-start.31) | collective-permute-done | bytes 16416 | tf_op jit(solution)/shard_map/ppermute | solution.py:308
  229.4 2.7 %collective-permute-start.33 = (f32[64,64]{1,0:T(8,128)S(1)}, f32[64,64]{1,0:T(8,128)S(1)}, u32[]{:S(2)}, u32[]{:S(2)}) collective-permute-start(f32[64,64]{1,0:T(8,128)S(1)} %add.97.a_ref), channel_id=1, source_target_pairs={{0,16},{4,20},{8,24},{12,28},{16,0},{20,4},{24,8},{28,12},{1,17},{... | collective-permute-start | bytes 49160 | tf_op jit(solution)/shard_map/ppermute | solution.py:308
  234.2 15.4 %basis.1 = (f32[64,8,16,128]{3,2,1,0:T(8,128)}, f32[64,64]{1,0:T(8,128)}) custom-call(s32[1]{0:T(128)} %bitcast.h_ref, f32[64,64]{1,0:T(8,128)S(1)} %add.97.a_ref, f32[64,64]{1,0:T(8,128)S(1)} %collective-permute-done.33.b_ref, f32[8,16,8,128]{3,2,1,0:T(8,128)S(1)} %get-tuple-element.25.refs_0_, f32[8,16,8,128]{3,2,1,0:T(8,128)S(1)} %get-tuple-element.29.refs_1_, ...), custom_call_target="tpu_custom_call" | custom-call | bytes 8388608 | tf_op jit(solution)/shard_map/basis/pallas_call | solution.py:255
  (152 shorter events, 70.5 us)
Async XLA Ops:
  2.3 32.5 %collective-permute-start = (f32[4,8,16,128]{3,2,1,0:T(8,128)}, f32[4,8,16,128]{3,2,1,0:T(8,128)}, u32[]{:S(2)}, u32[]{:S(2)}) collective-permute-start(f32[4,8,16,128]{3,2,1,0:T(8,128)} %pad_maximum_fusion.10), channel_id=1, source_target_pairs={{0,4},{4,0},{8,12},{12,8},{16,20},{20,16},{24,28},{28,24},{1,5},{5... | collective-permute-start | bytes 786440 | tf_op jit(solution)/shard_map/ppermute | solution.py:272
  7.0 60.0 %collective-permute-start.2 = (f32[4,7,16,128]{3,2,1,0:T(8,128)}, f32[4,7,16,128]{3,2,1,0:T(8,128)}, u32[]{:S(2)}, u32[]{:S(2)}) collective-permute-start(f32[4,7,16,128]{3,2,1,0:T(8,128)} %slice_select_fusion), channel_id=1, source_target_pairs={{4,12},{8,0},{12,20},{16,8},{20,28},{24,16},{5,13},{9,1},{13,21},{... | collective-permute-start | bytes 688136 | tf_op jit(solution)/shard_map/ppermute | solution.py:277
  11.6 61.3 %collective-permute-start.20 = (f32[8,16,8,128]{3,2,1,0:T(8,128)}, f32[8,16,8,128]{3,2,1,0:T(8,128)S(1)}, u32[]{:S(2)}, u32[]{:S(2)}) collective-permute-start(f32[8,16,8,128]{3,2,1,0:T(8,128)} %get-tuple-element.35), channel_id=1, source_target_pairs={{0,4},{4,0},{8,12},{12,8},{16,20},{20,16},{24,28},{28,24},{1,5},{5... | collective-permute-start | bytes 1572872 | tf_op jit(solution)/shard_map/ppermute | solution.py:272
  15.1 23.2 %collective-permute-start.21 = (f32[6,16,8,128]{3,2,1,0:T(8,128)}, f32[6,16,8,128]{3,2,1,0:T(8,128)S(1)}, u32[]{:S(2)}, u32[]{:S(2)}) collective-permute-start(f32[6,16,8,128]{3,2,1,0:T(8,128)} %get-tuple-element.36), channel_id=1, source_target_pairs={{4,12},{8,0},{12,20},{16,8},{20,28},{24,16},{5,13},{9,1},{13,21},{... | collective-permute-start | bytes 1179656 | tf_op jit(solution)/shard_map/ppermute | solution.py:277
  19.5 54.8 %collective-permute-start.15 = (f32[8,16,8,128]{3,2,1,0:T(8,128)}, f32[8,16,8,128]{3,2,1,0:T(8,128)S(1)}, u32[]{:S(2)}, u32[]{:S(2)}) collective-permute-start(f32[8,16,8,128]{3,2,1,0:T(8,128)} %get-tuple-element.31), channel_id=1, source_target_pairs={{0,4},{4,0},{8,12},{12,8},{16,20},{20,16},{24,28},{28,24},{1,5},{5... | collective-permute-start | bytes 1572872 | tf_op jit(solution)/shard_map/ppermute | solution.py:272
  38.3 19.1 %collective-permute-start.11 = (f32[6,16,8,128]{3,2,1,0:T(8,128)}, f32[6,16,8,128]{3,2,1,0:T(8,128)S(1)}, u32[]{:S(2)}, u32[]{:S(2)}) collective-permute-start(f32[6,16,8,128]{3,2,1,0:T(8,128)} %copy-done.13), channel_id=1, source_target_pairs={{4,12},{8,0},{12,20},{16,8},{20,28},{24,16},{5,13},{9,1},{13,21},{... | collective-permute-start | bytes 1179656 | tf_op jit(solution)/shard_map/ppermute | solution.py:277
  57.4 21.6 %collective-permute-start.10 = (f32[8,16,8,128]{3,2,1,0:T(8,128)}, f32[8,16,8,128]{3,2,1,0:T(8,128)S(1)}, u32[]{:S(2)}, u32[]{:S(2)}) collective-permute-start(f32[8,16,8,128]{3,2,1,0:T(8,128)} %copy-done.10), channel_id=1, source_target_pairs={{0,4},{4,0},{8,12},{12,8},{16,20},{20,16},{24,28},{28,24},{1,5},{5... | collective-permute-start | bytes 1572872 | tf_op jit(solution)/shard_map/ppermute | solution.py:272
  67.0 15.7 %collective-permute-start.5 = (f32[8,16,8,128]{3,2,1,0:T(8,128)S(1)}, f32[8,16,8,128]{3,2,1,0:T(8,128)S(1)}, u32[]{:S(2)}, u32[]{:S(2)}) collective-permute-start(f32[8,16,8,128]{3,2,1,0:T(8,128)S(1)} %copy-done.12), channel_id=1, source_target_pairs={{0,4},{4,0},{8,12},{12,8},{16,20},{20,16},{24,28},{28,24},{1,5},{5... | collective-permute-start | bytes 1572872 | tf_op jit(solution)/shard_map/ppermute | solution.py:272
  71.6 44.4 %collective-permute-start.3 = (f32[4,30,7,128]{3,2,1,0:T(8,128)S(1)}, f32[4,30,7,128]{3,2,1,0:T(8,128)S(1)}, u32[]{:S(2)}, u32[]{:S(2)}) collective-permute-start(f32[4,30,7,128]{3,2,1,0:T(8,128)S(1)} %get-tuple-element.48), channel_id=1, source_target_pairs={{0,1},{1,2},{2,3},{4,5},{5,6},{6,7},{8,9},{9,10},{10,11},{12,13},{... | collective-permute-start | bytes 1290248 | tf_op jit(solution)/shard_map/ppermute | solution.py:287
  72.9 44.3 %collective-permute-start.4 = (f32[4,30,7,128]{3,2,1,0:T(8,128)S(1)}, f32[4,30,7,128]{3,2,1,0:T(8,128)S(1)}, u32[]{:S(2)}, u32[]{:S(2)}) collective-permute-start(f32[4,30,7,128]{3,2,1,0:T(8,128)S(1)} %get-tuple-element.49), channel_id=1, source_target_pairs={{1,0},{2,1},{3,2},{5,4},{6,5},{7,6},{9,8},{10,9},{11,10},{13,12},{... | collective-permute-start | bytes 1290248 | tf_op jit(solution)/shard_map/ppermute | solution.py:292
  79.0 15.8 %collective-permute-start.17 = (f32[6,16,8,128]{3,2,1,0:T(8,128)S(1)}, f32[6,16,8,128]{3,2,1,0:T(8,128)S(1)}, u32[]{:S(2)}, u32[]{:S(2)}) collective-permute-start(f32[6,16,8,128]{3,2,1,0:T(8,128)S(1)} %constant_dynamic-slice_fusion.1), channel_id=1, source_target_pairs={{0,8},{8,16},{12,4},{16,24},{20,12},{28,20},{1,9},{9,17},{13,5},{1... | collective-permute-start | bytes 1179656 | tf_op jit(solution)/shard_map/ppermute | solution.py:282
  82.7 20.6 %collective-permute-start.12 = (f32[6,16,8,128]{3,2,1,0:T(8,128)S(1)}, f32[6,16,8,128]{3,2,1,0:T(8,128)S(1)}, u32[]{:S(2)}, u32[]{:S(2)}) collective-permute-start(f32[6,16,8,128]{3,2,1,0:T(8,128)S(1)} %constant_dynamic-slice_fusion.2), channel_id=1, source_target_pairs={{0,8},{8,16},{12,4},{16,24},{20,12},{28,20},{1,9},{9,17},{13,5},{1... | collective-permute-start | bytes 1179656 | tf_op jit(solution)/shard_map/ppermute | solution.py:282
  86.4 25.3 %collective-permute-start.7 = (f32[6,16,8,128]{3,2,1,0:T(8,128)S(1)}, f32[6,16,8,128]{3,2,1,0:T(8,128)S(1)}, u32[]{:S(2)}, u32[]{:S(2)}) collective-permute-start(f32[6,16,8,128]{3,2,1,0:T(8,128)S(1)} %constant_dynamic-slice_fusion.3), channel_id=1, source_target_pairs={{0,8},{8,16},{12,4},{16,24},{20,12},{28,20},{1,9},{9,17},{13,5},{1... | collective-permute-start | bytes 1179656 | tf_op jit(solution)/shard_map/ppermute | solution.py:282
  94.8 29.1 %collective-permute-start.23 = (f32[28,6,8,128]{3,2,1,0:T(8,128)S(1)}, f32[28,6,8,128]{3,2,1,0:T(8,128)S(1)}, u32[]{:S(2)}, u32[]{:S(2)}) collective-permute-start(f32[28,6,8,128]{3,2,1,0:T(8,128)S(1)} %pad_maximum_fusion.8), channel_id=1, source_target_pairs={{0,1},{1,2},{2,3},{4,5},{5,6},{6,7},{8,9},{9,10},{10,11},{12,13},{... | collective-permute-start | bytes 2064392 | tf_op jit(solution)/shard_map/ppermute | solution.py:287
  103.3 22.0 %collective-permute-start.24 = (f32[28,6,8,128]{3,2,1,0:T(8,128)S(1)}, f32[28,6,8,128]{3,2,1,0:T(8,128)S(1)}, u32[]{:S(2)}, u32[]{:S(2)}) collective-permute-start(f32[28,6,8,128]{3,2,1,0:T(8,128)S(1)} %pad_maximum_fusion.9), channel_id=1, source_target_pairs={{1,0},{2,1},{3,2},{5,4},{6,5},{7,6},{9,8},{10,9},{11,10},{13,12},{... | collective-permute-start | bytes 2064392 | tf_op jit(solution)/shard_map/ppermute | solution.py:292
  111.7 17.9 %collective-permute-start.18 = (f32[28,6,8,128]{3,2,1,0:T(8,128)S(1)}, f32[28,6,8,128]{3,2,1,0:T(8,128)S(1)}, u32[]{:S(2)}, u32[]{:S(2)}) collective-permute-start(f32[28,6,8,128]{3,2,1,0:T(8,128)S(1)} %pad_maximum_fusion.6), channel_id=1, source_target_pairs={{0,1},{1,2},{2,3},{4,5},{5,6},{6,7},{8,9},{9,10},{10,11},{12,13},{... | collective-permute-start | bytes 2064392 | tf_op jit(solution)/shard_map/ppermute | solution.py:287
  116.0 31.4 %collective-permute-start.19 = (f32[28,6,8,128]{3,2,1,0:T(8,128)S(1)}, f32[28,6,8,128]{3,2,1,0:T(8,128)S(1)}, u32[]{:S(2)}, u32[]{:S(2)}) collective-permute-start(f32[28,6,8,128]{3,2,1,0:T(8,128)S(1)} %pad_maximum_fusion.7), channel_id=1, source_target_pairs={{1,0},{2,1},{3,2},{5,4},{6,5},{7,6},{9,8},{10,9},{11,10},{13,12},{... | collective-permute-start | bytes 2064392 | tf_op jit(solution)/shard_map/ppermute | solution.py:292
  117.3 47.6 %collective-permute-start.13 = (f32[28,6,8,128]{3,2,1,0:T(8,128)S(1)}, f32[28,6,8,128]{3,2,1,0:T(8,128)S(1)}, u32[]{:S(2)}, u32[]{:S(2)}) collective-permute-start(f32[28,6,8,128]{3,2,1,0:T(8,128)S(1)} %pad_maximum_fusion.4), channel_id=1, source_target_pairs={{0,1},{1,2},{2,3},{4,5},{5,6},{6,7},{8,9},{9,10},{10,11},{12,13},{... | collective-permute-start | bytes 2064392 | tf_op jit(solution)/shard_map/ppermute | solution.py:287
  124.0 41.7 %collective-permute-start.14 = (f32[28,6,8,128]{3,2,1,0:T(8,128)S(1)}, f32[28,6,8,128]{3,2,1,0:T(8,128)S(1)}, u32[]{:S(2)}, u32[]{:S(2)}) collective-permute-start(f32[28,6,8,128]{3,2,1,0:T(8,128)S(1)} %pad_maximum_fusion.5), channel_id=1, source_target_pairs={{1,0},{2,1},{3,2},{5,4},{6,5},{7,6},{9,8},{10,9},{11,10},{13,12},{... | collective-permute-start | bytes 2064392 | tf_op jit(solution)/shard_map/ppermute | solution.py:292
  125.3 57.9 %collective-permute-start.8 = (f32[28,6,8,128]{3,2,1,0:T(8,128)S(1)}, f32[28,6,8,128]{3,2,1,0:T(8,128)S(1)}, u32[]{:S(2)}, u32[]{:S(2)}) collective-permute-start(f32[28,6,8,128]{3,2,1,0:T(8,128)S(1)} %pad_maximum_fusion.2), channel_id=1, source_target_pairs={{0,1},{1,2},{2,3},{4,5},{5,6},{6,7},{8,9},{9,10},{10,11},{12,13},{... | collective-permute-start | bytes 2064392 | tf_op jit(solution)/shard_map/ppermute | solution.py:287
  129.6 53.6 %collective-permute-start.9 = (f32[28,6,8,128]{3,2,1,0:T(8,128)S(1)}, f32[28,6,8,128]{3,2,1,0:T(8,128)S(1)}, u32[]{:S(2)}, u32[]{:S(2)}) collective-permute-start(f32[28,6,8,128]{3,2,1,0:T(8,128)S(1)} %pad_maximum_fusion.3), channel_id=1, source_target_pairs={{1,0},{2,1},{3,2},{5,4},{6,5},{7,6},{9,8},{10,9},{11,10},{13,12},{... | collective-permute-start | bytes 2064392 | tf_op jit(solution)/shard_map/ppermute | solution.py:292
  147.4 52.7 %collective-permute-start.28 = (f32[8,16,8,128]{3,2,1,0:T(8,128)S(1)}, f32[8,16,8,128]{3,2,1,0:T(8,128)S(1)}, u32[]{:S(2)}, u32[]{:S(2)}) collective-permute-start(f32[8,16,8,128]{3,2,1,0:T(8,128)S(1)} %get-tuple-element.41), channel_id=1, source_target_pairs={{0,4},{4,0},{8,12},{12,8},{16,20},{20,16},{24,28},{28,24},{1,5},{5... | collective-permute-start | bytes 1572872 | tf_op jit(solution)/shard_map/ppermute | solution.py:272
  164.9 35.2 %collective-permute-start.27 = (f32[8,16,8,128]{3,2,1,0:T(8,128)S(1)}, f32[8,16,8,128]{3,2,1,0:T(8,128)S(1)}, u32[]{:S(2)}, u32[]{:S(2)}) collective-permute-start(f32[8,16,8,128]{3,2,1,0:T(8,128)S(1)} %get-tuple-element.40), channel_id=1, source_target_pairs={{0,4},{4,0},{8,12},{12,8},{16,20},{20,16},{24,28},{28,24},{1,5},{5... | collective-permute-start | bytes 1572872 | tf_op jit(solution)/shard_map/ppermute | solution.py:272
  181.8 18.3 %collective-permute-start.26 = (f32[8,16,8,128]{3,2,1,0:T(8,128)S(1)}, f32[8,16,8,128]{3,2,1,0:T(8,128)S(1)}, u32[]{:S(2)}, u32[]{:S(2)}) collective-permute-start(f32[8,16,8,128]{3,2,1,0:T(8,128)S(1)} %get-tuple-element.39), channel_id=1, source_target_pairs={{0,4},{4,0},{8,12},{12,8},{16,20},{20,16},{24,28},{28,24},{1,5},{5... | collective-permute-start | bytes 1572872 | tf_op jit(solution)/shard_map/ppermute | solution.py:272
  (32 other events, 344.3 us)

commit v2 on v1

v2 whole, which is shorter than its diff:
```python
import functools

import jax
import jax.numpy as jnp
from jax import lax
from jax.experimental import pallas as pl
from jax.experimental.pallas import tpu as pltpu
from jax.sharding import PartitionSpec as P

OMEGA = 0.8
KEEP = 1.0 - OMEGA
A0 = 1.0 + KEEP + KEEP**2 + KEEP**3
A1 = 1.0 + 2.0 * KEEP + 3.0 * KEEP**2
A2 = 1.0 + 3.0 * KEEP
A3 = 1.0
DEPTH = 6
RING = DEPTH + 1
EDGE = 8
MIB = 1 << 20


def smem():
    return pl.BlockSpec(memory_space=pltpu.SMEM)


def vmem():
    return pl.BlockSpec(memory_space=pltpu.VMEM)


def prep_kernel(h_ref, mine_ref, theirs_ref, *refs):
    maps, (own_ref, send_ref, edge_ref, wide) = refs[:-4], refs[-4:]
    planes, rows, many, depth = own_ref.shape
    side = h_ref[0]
    cells = planes * rows
    send = send_ref.at[pl.ds(0, cells * many)].reshape(own_ref.shape)
    for source, target in ((theirs_ref, send), (mine_ref, own_ref)):
        wide[...] = source[...].astype(jnp.float32).reshape(wide.shape)

        def plane(x, carry):
            for y in range(rows):
                target[x, y] = wide[pl.ds(x * rows + y, many, stride=cells), :]
            return carry

        lax.fori_loop(0, planes, plane, 0)
    edge = DEPTH * rows * many
    edge_ref[:edge] = own_ref[pl.ds(side * (planes - DEPTH), DEPTH)].reshape(edge, depth)
    for i, ref in enumerate(maps):
        at, ring = cells * many + i * cells, RING * rows
        send_ref[at : at + cells] = ref[...].reshape(cells, depth)
        part = ref[pl.ds(side * (planes - RING), RING)].reshape(ring, depth)
        edge_ref[edge + i * ring : edge + (i + 1) * ring] = part


def prep(side, probes, tile, maps):
    planes, rows, depth = probes.shape[1:]
    block = (8, planes, rows, depth)
    own = (planes, rows, 8, depth)
    send = (planes * rows * (8 + len(maps)), depth)
    edge = ((DEPTH * 8 + RING * len(maps)) * rows, depth)
    return pl.pallas_call(
        prep_kernel,
        grid_spec=pltpu.PrefetchScalarGridSpec(
            num_scalar_prefetch=1,
            grid=(1,),
            in_specs=[
                pl.BlockSpec(block, lambda i, h: (2 * tile + h[0], 0, 0, 0)),
                pl.BlockSpec(block, lambda i, h: (2 * tile + 1 - h[0], 0, 0, 0)),
            ]
            + [pl.BlockSpec(m.shape, lambda i, h: (0, 0, 0)) for m in maps],
            out_specs=[
                pl.BlockSpec(own, lambda i, h: (0, 0, 0, 0)),
                pl.BlockSpec(send, lambda i, h: (0, 0)),
                pl.BlockSpec(edge, lambda i, h: (0, 0)),
            ],
            scratch_shapes=[pltpu.VMEM((8 * planes * rows, depth), jnp.float32)],
        ),
        out_shape=[jax.ShapeDtypeStruct(s, jnp.float32) for s in (own, send, edge)],
        compiler_params=pltpu.CompilerParams(vmem_limit_bytes=16 * MIB),
        cost_estimate=pl.CostEstimate(flops=0, bytes_accessed=2 * MIB, transcendentals=0),
        name="spread_probes",
    )(side, probes, probes, *maps)


def spread(coef, which, x, y, many):
    return coef[which, x, pl.ds(y, many, stride=0), :]


def solve_kernel(h_ref, coef, own, recv, e1, e2, ylo, yhi, keep, back, r_s, a_s, b_s):
    planes, rows = own.shape[0], own.shape[1]
    wide_x, wide_y = r_s.shape[0], r_s.shape[1]
    side = h_ref[0]
    top = DEPTH + 2 * planes
    parts = (
        (own, 0, planes, DEPTH + planes * side),
        (recv, planes, planes, DEPTH + planes * (1 - side)),
        (e1, 2 * planes, DEPTH, top * (1 - side)),
        (e2, 2 * planes + DEPTH, DEPTH, top * side),
    )

    def row(which, x, y):
        return spread(coef, which, x, y, own.shape[2])

    for piece, role, count, place in parts:

        def fill(i, carry, piece=piece, role=role, place=place):
            x = place + i
            for y in range(wide_y):
                if y < DEPTH:
                    value = ylo[role + i, y]
                elif y < DEPTH + rows:
                    value = piece[i, y - DEPTH]
                else:
                    value = yhi[role + i, y - DEPTH - rows]
                r_s[x, y] = value * row(6, x, y)
            return carry

        lax.fori_loop(0, count, fill, 0)

    def stencil(src, r, x, low, scale):
        here = [src[x, y] for y in range(low - 1, wide_y - low + 1)]
        for y in range(low, wide_y - low):
            k = y - low + 1
            total = row(0, x, y) * src[x - 1, y] + row(1, x, y) * src[x + 1, y]
            total = total + row(2, x, y) * here[k - 1] + row(3, x, y) * here[k + 1]
            total = total + row(4, x, y) * pltpu.roll(here[k], 1, 1) + row(5, x, y) * pltpu.roll(here[k], 127, 1)
            yield y, r[x, y] + scale * total

    def sweep(src, dst, r, low, scale, last=None):
        def plane(x, carry):
            for y, value in stencil(src, r, x, low, scale):
                dst[x, y] = value if last is None else value * row(last, x, y)
            return carry

        lax.fori_loop(low, wide_x - low, plane, 0)

    sweep(r_s, a_s, r_s, 1, A3 / A2)
    sweep(a_s, b_s, r_s, 2, A2 / A1)
    sweep(b_s, a_s, r_s, 3, A1 / A0, last=7)
    sweep(a_s, b_s, a_s, 4, A3 / A2)
    sweep(b_s, r_s, a_s, 5, A2 / A1)
    for target, place in ((back, parts[1][3]), (keep, parts[0][3])):

        def out(i, carry, target=target, place=place):
            x = place + i
            for y, value in stencil(r_s, a_s, x, DEPTH, A1 / A0):
                target[i, y - DEPTH] = value * row(8, x, y)
            return carry

        lax.fori_loop(0, planes, out, 0)


def solve(side, coef, own, recv, e1, e2, ylo, yhi):
    wide_x, wide_y = coef.shape[1], coef.shape[2]
    many, depth = own.shape[2:]
    field = pltpu.VMEM((wide_x, wide_y, many, depth), jnp.float32)
    cells = wide_x * wide_y * many * depth
    return pl.pallas_call(
        solve_kernel,
        in_specs=[smem()] + [vmem()] * 7,
        out_specs=[vmem(), vmem()],
        out_shape=[jax.ShapeDtypeStruct(own.shape, jnp.float32)] * 2,
        scratch_shapes=[field, field, field],
        compiler_params=pltpu.CompilerParams(vmem_limit_bytes=(14 + 14 * many // 8) * MIB),
        cost_estimate=pl.CostEstimate(flops=60 * cells, bytes_accessed=12 * MIB, transcendentals=0),
        name="both_solves",
    )(side, coef, own, recv, e1, e2, ylo, yhi)


def stacked(side, tiles, rows):
    columns = []
    for y in range(rows):
        parts = []
        for keep, got in zip(tiles[0::2], tiles[1::2]):
            a, b = keep[0, y], got[0, y]
            parts += [jnp.where(side == 0, a, b), jnp.where(side == 0, b, a)]
        columns.append(jnp.concatenate(parts, axis=0))
    return jnp.concatenate(columns, axis=1)


def split(value):
    high = value.astype(jnp.bfloat16)
    return high, (value - high.astype(jnp.float32)).astype(jnp.bfloat16)


def gram_kernel(scale, h_ref, *refs):
    tiles, out, total = refs[:-2], refs[-2], refs[-1]
    step = pl.program_id(0)

    @pl.when(step == 0)
    def _():
        total[...] = jnp.zeros_like(total)

    both = jnp.concatenate(split(stacked(h_ref[0], tiles, tiles[0].shape[1])), axis=0)
    total[...] += lax.dot_general(both, both, (((1,), (1,)), ((), ())), preferred_element_type=jnp.float32)

    @pl.when(step == pl.num_programs(0) - 1)
    def _():
        n = out.shape[0]
        g = total[:n, :n] + total[:n, n:] + total[n:, :n] + total[n:, n:]
        out[...] = g * scale


def tile_spec(shape):
    return pl.BlockSpec((1,) + shape[1:], lambda i: (i, 0, 0, 0))


def gram_of(side, tiles, cells):
    count = 8 * len(tiles)
    return pl.pallas_call(
        functools.partial(gram_kernel, 1.0 / cells),
        grid=(tiles[0].shape[0],),
        in_specs=[smem()] + [tile_spec(t.shape) for t in tiles],
        out_specs=pl.BlockSpec((count, count), lambda i: (0, 0)),
        out_shape=jax.ShapeDtypeStruct((count, count), jnp.float32),
        scratch_shapes=[pltpu.VMEM((2 * count, 2 * count), jnp.float32)],
        compiler_params=pltpu.CompilerParams(vmem_limit_bytes=16 * MIB),
        cost_estimate=pl.CostEstimate(flops=0, bytes_accessed=6 * MIB, transcendentals=0),
        name="gram",
    )(side, *tiles)


def factor(gram):
    n = gram.shape[0]
    i = lax.broadcasted_iota(jnp.int32, (n, n), 0)
    j = lax.broadcasted_iota(jnp.int32, (n, n), 1)
    both = jnp.concatenate([gram, (i == j).astype(jnp.float32)], axis=1)
    rows = [both[8 * t : 8 * t + 8] for t in range(n // 8)]
    place = lax.broadcasted_iota(jnp.int32, (8, 2 * n), 0)
    for c in range(0, n, 2):
        t, s = divmod(c, 8)
        first, second = rows[t][s : s + 1], rows[t][s + 1 : s + 2]
        a, b, d = first[:, c : c + 1], first[:, c + 1 : c + 2], second[:, c + 1 : c + 2]
        inv = 1.0 / (a * d - b * b)
        w1 = (d * first - b * second) * inv
        w2 = (a * second - b * first) * inv
        fixed = jnp.where(place == s + 1, second - (b / a) * first, rows[t])
        for k in range(t, n // 8):
            new = rows[k] - (rows[k][:, c : c + 1] * w1 + rows[k][:, c + 1 : c + 2] * w2)
            rows[k] = jnp.where(place > s + 1, new, fixed) if k == t else new
    done = jnp.concatenate(rows, axis=0)
    size = jnp.sum(jnp.where(i == j, done[:, :n], 0.0), axis=1, keepdims=True)
    done = done * lax.rsqrt(size)
    return done[:, :n], done[:, n:]


def basis_kernel(h_ref, a_ref, b_ref, *refs):
    tiles, (q_ref, r_ref, left) = refs[:-3], refs[-3:]
    n = r_ref.shape[0]
    rows = tiles[0].shape[1]

    @pl.when(pl.program_id(0) == 0)
    def _():
        upper, inverse = factor(a_ref[...] + b_ref[...])
        i = lax.broadcasted_iota(jnp.int32, (n, n), 0)
        j = lax.broadcasted_iota(jnp.int32, (n, n), 1)
        r_ref[...] = jnp.where(j >= i, upper, 0.0)
        inverse = jnp.where(j <= i, inverse, 0.0)
        high, low = split(inverse)
        left[...] = jnp.concatenate([high, high, low, low], axis=1)

    high, low = split(stacked(h_ref[0], tiles, rows))
    q = jnp.dot(left[...], jnp.concatenate([high, low, high, low], axis=0), preferred_element_type=jnp.float32)
    depth = q.shape[1] // rows
    flat = q_ref.reshape(n * rows, depth)
    for y in range(rows):
        flat[pl.ds(y, n, stride=rows), :] = q[:, y * depth : (y + 1) * depth]


def basis(side, a, b, tiles):
    n = a.shape[0]
    planes, rows, _, depth = tiles[0].shape
    full = pl.BlockSpec((n, n), lambda i: (0, 0))
    return pl.pallas_call(
        basis_kernel,
        grid=(planes,),
        in_specs=[smem(), full, full] + [tile_spec(t.shape) for t in tiles],
        out_specs=[pl.BlockSpec((n, 1, rows, depth), lambda i: (0, i, 0, 0)), full],
        out_shape=[
            jax.ShapeDtypeStruct((n, planes, rows, depth), jnp.float32),
            jax.ShapeDtypeStruct((n, n), jnp.float32),
        ],
        scratch_shapes=[pltpu.VMEM((n, 4 * n), jnp.bfloat16)],
        compiler_params=pltpu.CompilerParams(vmem_limit_bytes=24 * MIB),
        cost_estimate=pl.CostEstimate(flops=0, bytes_accessed=8 * MIB, transcendentals=0),
        name="basis",
    )(side, a, b, *tiles)


def swap(value):
    return lax.ppermute(value, "gx", [(i, i ^ 1) for i in range(lax.axis_size("gx"))])


def outward(value):
    n = lax.axis_size("gx")
    return lax.ppermute(value, "gx", [(i, i + 2 * (i % 2) * 2 - 2) for i in range(n) if 0 <= i + 4 * (i % 2) - 2 < n])


def inward(value):
    n = lax.axis_size("gx")
    return lax.ppermute(value, "gx", [(i, i + 2 - 4 * (i % 2)) for i in range(n) if 0 <= i + 2 - 4 * (i % 2) < n])


def above(value):
    n = lax.axis_size("gy")
    return lax.ppermute(value, "gy", [(i, i + 1) for i in range(n - 1)])


def below(value):
    n = lax.axis_size("gy")
    return lax.ppermute(value, "gy", [(i + 1, i) for i in range(n - 1)])


def summed(value):
    steps = []
    for axis in ("gy", "gx"):
        n = lax.axis_size(axis)
        assert n & (n - 1) == 0
        shift = 1
        while shift < n:
            steps.append((axis, shift, n))
            shift *= 2
    other = None
    for axis, shift, n in steps:
        if other is not None:
            value = value + other
        other = lax.ppermute(value, axis, [(i, i ^ shift) for i in range(n)])
    return value, other


def coefficients(side, ext, planes, rows):
    cut = EDGE - DEPTH
    k, absorb, sense, weight = ext
    depth = k.shape[2]

    def shifted(value, dx, dy):
        return value[1 + dx : value.shape[0] - 1 + dx, cut + dy : value.shape[1] - cut + dy]

    mid = shifted(k, 0, 0)
    faces = [0.5 * (mid + shifted(k, *d)) for d in ((-1, 0), (1, 0), (0, -1), (0, 1))]
    zpad = jnp.pad(mid, ((0, 0), (0, 0), (1, 1)))
    z_low = 0.5 * (mid + zpad[:, :, :-2])
    z_high = 0.5 * (mid + zpad[:, :, 2:])
    diag = shifted(absorb, 0, 0) + sum(faces) + z_low + z_high

    def inside(axis, start, total):
        index = start - DEPTH + lax.broadcasted_iota(jnp.int32, diag.shape, axis)
        return (index >= 0) & (index < total)

    gx, gy = lax.axis_index("gx"), lax.axis_index("gy")
    here = inside(0, (gx - side) * planes, planes * lax.axis_size("gx"))
    here = here & inside(1, gy * rows, rows * lax.axis_size("gy"))
    inv = jnp.where(here, OMEGA / jnp.where(here, diag, 1.0), 0.0)
    z = lax.broadcasted_iota(jnp.int32, diag.shape, 2)
    z_low = jnp.where(z == 0, 0.0, z_low)
    z_high = jnp.where(z == depth - 1, 0.0, z_high)
    sense, weight = shifted(sense, 0, 0), shifted(weight, 0, 0)
    return jnp.stack([f * inv for f in faces] + [z_low * inv, z_high * inv, sense * inv, A0 * weight * inv, A0 * sense])


def rows_of(*values):
    parts = [v.reshape(-1, v.shape[-1]) for v in values]
    return parts[0] if len(parts) == 1 else jnp.concatenate(parts, axis=0)


def parts_of(flat, *shapes):
    out, at = [], 0
    for shape in shapes:
        size = 1
        for n in shape[:-1]:
            size *= n
        out.append(flat[at : at + size].reshape(shape))
        at += size
    return out


def body(probes, permeability, absorption, sensitivity, observe_weight):
    count, planes, rows, depth = probes.shape
    cells = planes * lax.axis_size("gx") * rows * lax.axis_size("gy") * depth
    side = lax.axis_index("gx") % 2
    lower = side == 0
    flag = side.reshape(1).astype(jnp.int32)
    maps = (permeability, absorption, sensitivity, observe_weight)
    tall = 2 * planes + 2 * DEPTH

    tiles = []
    coef = turn = None
    for tile in range(count // 16):
        mine = maps if tile == 0 else ()
        own, send, edge = prep(flag, probes, tile, mine)
        if turn is not None:
            send, turn = lax.optimization_barrier((send, turn))
        recv_rows = swap(send)
        e1_rows = outward(edge)
        block, halo = (planes, rows, 8, depth), (DEPTH, rows, 8, depth)
        four, ring = (len(maps), planes, rows, depth), (len(maps), RING, rows, depth)
        recv, *recv_maps = parts_of(recv_rows, block, *([four] if mine else []))
        inner = [lax.dynamic_slice_in_dim(recv, (1 - side) * (planes - DEPTH), DEPTH, 0)]
        for value in recv_maps:
            inner.append(lax.dynamic_slice_in_dim(value, (1 - side) * (planes - RING), RING, 1))
        e2_rows = inward(rows_of(*inner))
        e1, *e1_maps = parts_of(e1_rows, halo, *([ring] if mine else []))
        e2, *e2_maps = parts_of(e2_rows, halo, *([ring] if mine else []))
        turn = e1
        low = [jnp.concatenate([p[:, rows - DEPTH :] for p in (own, recv, e1, e2)], axis=0)]
        high = [jnp.concatenate([p[:, :DEPTH] for p in (own, recv, e1, e2)], axis=0)]
        if mine:
            own_maps = jnp.stack(maps)
            wide = jnp.concatenate(
                [
                    jnp.where(lower, e2_maps[0], e1_maps[0]),
                    jnp.where(lower, own_maps, recv_maps[0]),
                    jnp.where(lower, recv_maps[0], own_maps),
                    jnp.where(lower, e1_maps[0], e2_maps[0]),
                ],
                axis=1,
            )
            low.append(wide[:, :, rows - EDGE :])
            high.append(wide[:, :, :EDGE])
        shapes = [v.shape for v in low]
        ylo, *map_low = parts_of(above(rows_of(*low)), *shapes)
        yhi, *map_high = parts_of(below(rows_of(*high)), *shapes)
        if mine:
            coef = coefficients(side, jnp.concatenate([map_low[0], wide, map_high[0]], axis=2), planes, rows)
        keep, back = solve(flag, coef, own, recv, e1, e2, ylo, yhi)
        tiles += [keep, swap(back)]
    a, b = summed(gram_of(flag, tiles, cells))
    q, r = basis(flag, a, b, tiles)
    return (q, r)


def solution(mesh):
    return jax.shard_map(
        body,
        mesh=mesh,
        in_specs=(
            P(None, "gx", "gy", None),
            P("gx", "gy", None),
            P("gx", "gy", None),
            P("gx", "gy", None),
            P("gx", "gy", None),
        ),
        out_specs=(P(None, "gx", "gy", None), P()),
        check_vma=False,
    )
```

time: 251 us -> 239 us (0.952)
  Pallas kernels: 87.4 us -> 80.6 us
  other arithmetic: 8.81 us -> 3.4 us
  starting transfers between devices: 71.4 us -> 76.7 us
  waiting for transfers between devices: 65.4 us -> 61.8 us
    ppermute x5, starting transfers between devices: 6.95 us -> 24.7 us  [summed(): other = lax.ppermute(value, axis, [(i, i ^ shift) for i in range(n)])]
    ppermute x5 -> x4, starting transfers between devices: 20.4 us -> 13.2 us  [above(): return lax.ppermute(value, 'gy', [(i, i + 1) for i in range(n - 1)])]
    ppermute x5 -> x4, waiting for transfers between devices: 18.3 us -> 12.4 us  [inward(): lax.ppermute(value, 'gx', [(i, i + 2 - 4 * (i % 2)) for i in range(n) if...]
    pallas_call x1, Pallas kernels: 15.4 us -> 10.4 us  [basis(): pl.pallas_call(basis_kernel, grid=(planes,), in_specs=[smem(), full, full...]
    ppermute x5 -> x4, waiting for transfers between devices: 0.01 us -> 4.29 us  [below(): return lax.ppermute(value, 'gy', [(i + 1, i) for i in range(n - 1)])]
    select_n x4 -> x2, other arithmetic: 4.9 us -> 1.02 us  [the longest x1 0.97 us: body(): jnp.where(lower, e2_maps[0], e1_maps[0])]
    pallas_call x4, Pallas kernels: 64.4 us -> 60.9 us  [solve(): pl.pallas_call(solve_kernel, in_specs=[smem()] + [vmem()] * 7, out_specs=...]
    ppermute x5 -> x4, starting transfers between devices: 17.9 us -> 14.8 us  [inward(): lax.ppermute(value, 'gx', [(i, i + 2 - 4 * (i % 2)) for i in range(n) if...]
  transfers between devices with their start and end apart: 34 -> 29, of which waited for: 14 -> 13; matrix products, arithmetic and copies ran while one was open for 6% -> 4% of each run, Pallas kernels for 28% -> 28%
where the time goes in v2:
time: 239 us; the launch traced here: 238 us
  Pallas kernels  80.6 us (34%)
  starting transfers between devices  76.7 us (32%)
  waiting for transfers between devices  61.8 us (26%)
  local copies, waits for them, and re-layouts  13.7 us (6%)
  other arithmetic  3.4 us (1%)
    pallas_call x4, Pallas kernels, solve(): pl.pallas_call(solve_kernel, in_specs=[smem()] + [vmem()] * 7, out_specs=...  60.9 us
    ppermute x5, starting transfers between devices, summed(): other = lax.ppermute(value, axis, [(i, i ^ shift) for i in range(n)])  24.7 us
    ppermute x4, waiting for transfers between devices, outward(): lax.ppermute(value, 'gx', [(i, i + 2 * (i % 2) * 2 - 2) for i in range(n)...  21.4 us
    ppermute x4, starting transfers between devices, inward(): lax.ppermute(value, 'gx', [(i, i + 2 - 4 * (i % 2)) for i in range(n) if...  14.8 us
    ppermute x8, starting transfers between devices, swap(): lax.ppermute(value, 'gx', [(i, i ^ 1) for i in range(lax.axis_size('gx'))])  13.5 us
    ppermute x8, waiting for transfers between devices, swap(): lax.ppermute(value, 'gx', [(i, i ^ 1) for i in range(lax.axis_size('gx'))])  13.3 us
    ppermute x4, starting transfers between devices, above(): return lax.ppermute(value, 'gy', [(i, i + 1) for i in range(n - 1)])  13.2 us
    ppermute x4, waiting for transfers between devices, inward(): lax.ppermute(value, 'gx', [(i, i + 2 - 4 * (i % 2)) for i in range(n) if...  12.4 us
  transfers between devices with their start and end apart: 29, of which 13 were waited for; matrix products, arithmetic and copies ran while one was open for 4% of the time, Pallas kernels for 28%

profile of v2, /device:TPU:0, one launch (start us, length us, event | category | flops | bytes accessed | tf_op | source)
XLA Modules:
  0.0 237.7 jit_solution(10309615163136010704)
XLA Ops:
  8.8 5.9 %collective-permute-start = (f32[1536,128]{1,0:T(8,128)}, f32[1536,128]{1,0:T(8,128)}, u32[]{:S(2)}, u32[]{:S(2)}) collective-permute-start(f32[1536,128]{1,0:T(8,128)} %get-tuple-element.26), channel_id=1, source_target_pairs={{0,4},{4,0},{8,12},{12,8},{16,20},{20,16},{24,28},{28,24},{1,5},{5... | collective-permute-start | bytes 2359304 | tf_op jit(solution)/shard_map/ppermute | solution.py:290
  28.2 7.8 %collective-permute-done.7 = f32[768,128]{1,0:T(8,128)S(1)} collective-permute-done((f32[768,128]{1,0:T(8,128)}, f32[768,128]{1,0:T(8,128)S(1)}, u32[]{:S(2)}, u32[]{:S(2)}) %collective-permute-start.7) | collective-permute-done | bytes 393248 | tf_op jit(solution)/shard_map/ppermute | solution.py:295
  37.2 7.2 %collective-permute-done.13 = f32[768,128]{1,0:T(8,128)S(1)} collective-permute-done((f32[768,128]{1,0:T(8,128)}, f32[768,128]{1,0:T(8,128)S(1)}, u32[]{:S(2)}, u32[]{:S(2)}) %collective-permute-start.13) | collective-permute-done | bytes 393248 | tf_op jit(solution)/shard_map/ppermute | solution.py:295
  45.6 6.4 %collective-permute-done.19 = f32[768,128]{1,0:T(8,128)S(1)} collective-permute-done((f32[768,128]{1,0:T(8,128)}, f32[768,128]{1,0:T(8,128)S(1)}, u32[]{:S(2)}, u32[]{:S(2)}) %collective-permute-start.19) | collective-permute-done | bytes 393248 | tf_op jit(solution)/shard_map/ppermute | solution.py:295
  56.2 4.3 %collective-permute-start.2 = (f32[1216,128]{1,0:T(8,128)S(1)}, f32[1216,128]{1,0:T(8,128)S(1)}, u32[]{:S(2)}, u32[]{:S(2)}) collective-permute-start(f32[1216,128]{1,0:T(8,128)S(1)} %pad_maximum_fusion.12), channel_id=1, source_target_pairs={{0,8},{8,16},{12,4},{16,24},{20,12},{28,20},{1,9},{9,17},{13,5},{1... | collective-permute-start | bytes 1867784 | tf_op jit(solution)/shard_map/ppermute | solution.py:300
  60.7 3.5 %collective-permute-start.14 = (f32[768,128]{1,0:T(8,128)S(1)}, f32[768,128]{1,0:T(8,128)S(1)}, u32[]{:S(2)}, u32[]{:S(2)}) collective-permute-start(f32[768,128]{1,0:T(8,128)S(1)} %bitcast.135), channel_id=1, source_target_pairs={{0,8},{8,16},{12,4},{16,24},{20,12},{28,20},{1,9},{9,17},{13,5},{1... | collective-permute-start | bytes 1179656 | tf_op jit(solution)/shard_map/ppermute | solution.py:300
  64.3 3.5 %collective-permute-start.20 = (f32[768,128]{1,0:T(8,128)S(1)}, f32[768,128]{1,0:T(8,128)S(1)}, u32[]{:S(2)}, u32[]{:S(2)}) collective-permute-start(f32[768,128]{1,0:T(8,128)S(1)} %bitcast.134), channel_id=1, source_target_pairs={{0,8},{8,16},{12,4},{16,24},{20,12},{28,20},{1,9},{9,17},{13,5},{1... | collective-permute-start | bytes 1179656 | tf_op jit(solution)/shard_map/ppermute | solution.py:300
  67.8 3.2 %collective-permute-done.6 = f32[1024,128]{1,0:T(8,128)S(1)} collective-permute-done((f32[1024,128]{1,0:T(8,128)}, f32[1024,128]{1,0:T(8,128)S(1)}, u32[]{:S(2)}, u32[]{:S(2)}) %collective-permute-start.6) | collective-permute-done | bytes 524320 | tf_op jit(solution)/shard_map/ppermute | solution.py:290
  71.0 3.5 %collective-permute-start.8 = (f32[768,128]{1,0:T(8,128)S(1)}, f32[768,128]{1,0:T(8,128)S(1)}, u32[]{:S(2)}, u32[]{:S(2)}) collective-permute-start(f32[768,128]{1,0:T(8,128)S(1)} %bitcast.133), channel_id=1, source_target_pairs={{0,8},{8,16},{12,4},{16,24},{20,12},{28,20},{1,9},{9,17},{13,5},{1... | collective-permute-start | bytes 1179656 | tf_op jit(solution)/shard_map/ppermute | solution.py:300
  74.5 8.8 %collective-permute-done.14 = f32[768,128]{1,0:T(8,128)S(1)} collective-permute-done((f32[768,128]{1,0:T(8,128)S(1)}, f32[768,128]{1,0:T(8,128)S(1)}, u32[]{:S(2)}, u32[]{:S(2)}) %collective-permute-start.14) | collective-permute-done | bytes 393248 | tf_op jit(solution)/shard_map/ppermute | solution.py:300
  86.3 3.2 %collective-permute-start.3 = (f32[2304,128]{1,0:T(8,128)S(1)}, f32[2304,128]{1,0:T(8,128)S(1)}, u32[]{:S(2)}, u32[]{:S(2)}) collective-permute-start(f32[2304,128]{1,0:T(8,128)S(1)} %pad_maximum_fusion.1), channel_id=1, source_target_pairs={{0,1},{1,2},{2,3},{4,5},{5,6},{6,7},{8,9},{9,10},{10,11},{12,13},{... | collective-permute-start | bytes 3538952 | tf_op jit(solution)/shard_map/ppermute | solution.py:305
  89.7 3.0 %collective-permute-start.15 = (f32[1344,128]{1,0:T(8,128)S(1)}, f32[1344,128]{1,0:T(8,128)S(1)}, u32[]{:S(2)}, u32[]{:S(2)}) collective-permute-start(f32[1344,128]{1,0:T(8,128)S(1)} %bitcast.127), channel_id=1, source_target_pairs={{0,1},{1,2},{2,3},{4,5},{5,6},{6,7},{8,9},{9,10},{10,11},{12,13},{... | collective-permute-start | bytes 2064392 | tf_op jit(solution)/shard_map/ppermute | solution.py:305
  94.2 3.6 %collective-permute-done.8 = f32[768,128]{1,0:T(8,128)S(1)} collective-permute-done((f32[768,128]{1,0:T(8,128)S(1)}, f32[768,128]{1,0:T(8,128)S(1)}, u32[]{:S(2)}, u32[]{:S(2)}) %collective-permute-start.8) | collective-permute-done | bytes 393248 | tf_op jit(solution)/shard_map/ppermute | solution.py:300
  100.7 5.6 %collective-permute-start.9 = (f32[1344,128]{1,0:T(8,128)S(1)}, f32[1344,128]{1,0:T(8,128)S(1)}, u32[]{:S(2)}, u32[]{:S(2)}) collective-permute-start(f32[1344,128]{1,0:T(8,128)S(1)} %bitcast.132), channel_id=1, source_target_pairs={{0,1},{1,2},{2,3},{4,5},{5,6},{6,7},{8,9},{9,10},{10,11},{12,13},{... | collective-permute-start | bytes 2064392 | tf_op jit(solution)/shard_map/ppermute | solution.py:305
  109.9 15.2 %both_solves.4 = (f32[8,16,8,128]{3,2,1,0:T(8,128)S(1)}, f32[8,16,8,128]{3,2,1,0:T(8,128)S(1)}) custom-call(s32[1]{0:T(128)} %bitcast.h_ref, f32[9,28,28,128]{3,2,1,0:T(8,128)S(1)} %bitcast_dynamic-update-slice_fusion.coef, f32[8,16,8,128]{3,2,1,0:T(8,128)S(1)} %get-tuple-element.25.own, f32[8,16,8,128]{3,2,1,0:T(8,128)S(1)} %bitcast.75, ...), custom_call_target="tpu_custom_call" | custom-call | flops 48168960 | bytes 12582912 | tf_op jit(solution)/shard_map/both_solves/pallas_call | solution.py:157
  125.2 4.3 %collective-permute-done.10 = f32[1344,128]{1,0:T(8,128)S(1)} collective-permute-done((f32[1344,128]{1,0:T(8,128)S(1)}, f32[1344,128]{1,0:T(8,128)S(1)}, u32[]{:S(2)}, u32[]{:S(2)}) %collective-permute-start.10) | collective-permute-done | bytes 688160 | tf_op jit(solution)/shard_map/ppermute | solution.py:310
  130.9 15.2 %both_solves.5 = (f32[8,16,8,128]{3,2,1,0:T(8,128)S(1)}, f32[8,16,8,128]{3,2,1,0:T(8,128)S(1)}) custom-call(s32[1]{0:T(128)} %bitcast.h_ref, f32[9,28,28,128]{3,2,1,0:T(8,128)S(1)} %bitcast_dynamic-update-slice_fusion.coef, f32[8,16,8,128]{3,2,1,0:T(8,128)S(1)} %get-tuple-element.30.own, f32[8,16,8,128]{3,2,1,0:T(8,128)S(1)} %bitcast.84, ...), custom_call_target="tpu_custom_call" | custom-call | flops 48168960 | bytes 12582912 | tf_op jit(solution)/shard_map/both_solves/pallas_call | solution.py:157
  146.8 15.2 %both_solves.6 = (f32[8,16,8,128]{3,2,1,0:T(8,128)S(1)}, f32[8,16,8,128]{3,2,1,0:T(8,128)S(1)}) custom-call(s32[1]{0:T(128)} %bitcast.h_ref, f32[9,28,28,128]{3,2,1,0:T(8,128)S(1)} %bitcast_dynamic-update-slice_fusion.coef, f32[8,16,8,128]{3,2,1,0:T(8,128)S(1)} %get-tuple-element.36.own, f32[8,16,8,128]{3,2,1,0:T(8,128)S(1)} %bitcast.81, ...), custom_call_target="tpu_custom_call" | custom-call | flops 48168960 | bytes 12582912 | tf_op jit(solution)/shard_map/both_solves/pallas_call | solution.py:157
  163.5 15.2 %both_solves.7 = (f32[8,16,8,128]{3,2,1,0:T(8,128)S(1)}, f32[8,16,8,128]{3,2,1,0:T(8,128)S(1)}) custom-call(s32[1]{0:T(128)} %bitcast.h_ref, f32[9,28,28,128]{3,2,1,0:T(8,128)S(1)} %bitcast_dynamic-update-slice_fusion.coef, f32[8,16,8,128]{3,2,1,0:T(8,128)S(1)} %get-tuple-element.42.own, f32[8,16,8,128]{3,2,1,0:T(8,128)S(1)} %bitcast.78, ...), custom_call_target="tpu_custom_call" | custom-call | flops 48168960 | bytes 12582912 | tf_op jit(solution)/shard_map/both_solves/pallas_call | solution.py:157
  179.4 10.0 %collective-permute-done.23.refs_7_ = f32[8,16,8,128]{3,2,1,0:T(8,128)S(1)} collective-permute-done((f32[8,16,8,128]{3,2,1,0:T(8,128)S(1)}, f32[8,16,8,128]{3,2,1,0:T(8,128)S(1)}, u32[]{:S(2)}, u32[]{:S(2)}) %collective-permute-start.23) | collective-permute-done | bytes 524320 | tf_op jit(solution)/shard_map/ppermute | solution.py:290
  192.1 10.7 %collective-permute-start.24 = (f32[64,64]{1,0:T(8,128)S(1)}, f32[64,64]{1,0:T(8,128)S(1)}, u32[]{:S(2)}, u32[]{:S(2)}) collective-permute-start(f32[64,64]{1,0:T(8,128)S(1)} %gram.1), channel_id=1, source_target_pairs={{0,1},{1,0},{2,3},{3,2},{4,5},{5,4},{6,7},{7,6},{8,9},{9,8},{10,11... | collective-permute-start | bytes 49160 | tf_op jit(solution)/shard_map/ppermute | solution.py:326
  203.8 9.1 %collective-permute-start.25 = (f32[64,64]{1,0:T(8,128)S(1)}, f32[64,64]{1,0:T(8,128)S(1)}, u32[]{:S(2)}, u32[]{:S(2)}) collective-permute-start(f32[64,64]{1,0:T(8,128)S(1)} %add.99), channel_id=1, source_target_pairs={{0,2},{1,3},{2,0},{3,1},{4,6},{5,7},{6,4},{7,5},{8,10},{9,11},{10,... | collective-permute-start | bytes 49160 | tf_op jit(solution)/shard_map/ppermute | solution.py:326
  215.3 3.3 %collective-permute-done.26 = f32[64,64]{1,0:T(8,128)S(1)} collective-permute-done((f32[64,64]{1,0:T(8,128)S(1)}, f32[64,64]{1,0:T(8,128)S(1)}, u32[]{:S(2)}, u32[]{:S(2)}) %collective-permute-start.26) | collective-permute-done | bytes 16416 | tf_op jit(solution)/shard_map/ppermute | solution.py:326
  227.4 10.4 %basis.1 = (f32[64,8,16,128]{3,2,1,0:T(8,128)}, f32[64,64]{1,0:T(8,128)}) custom-call(s32[1]{0:T(128)} %bitcast.h_ref, f32[64,64]{1,0:T(8,128)S(1)} %add.102.a_ref, f32[64,64]{1,0:T(8,128)S(1)} %collective-permute-done.28.b_ref, f32[8,16,8,128]{3,2,1,0:T(8,128)S(1)} %get-tuple-element.28.refs_0_, f32[8,16,8,128]{3,2,1,0:T(8,128)S(1)} %collective-permute-done.5.refs_1_, ...), custom_call_target="tpu_custom_call" | custom-call | bytes 8388608 | tf_op jit(solution)/shard_map/basis/pallas_call | solution.py:273
  (146 shorter events, 58.0 us)
Async XLA Ops:
  7.5 44.5 %collective-permute-start.1 = (f32[1216,128]{1,0:T(8,128)}, f32[1216,128]{1,0:T(8,128)}, u32[]{:S(2)}, u32[]{:S(2)}) collective-permute-start(f32[1216,128]{1,0:T(8,128)} %get-tuple-element.27), channel_id=1, source_target_pairs={{4,12},{8,0},{12,20},{16,8},{20,28},{24,16},{5,13},{9,1},{13,21},{... | collective-permute-start | bytes 1867784 | tf_op jit(solution)/shard_map/ppermute | solution.py:295
  8.8 45.1 %collective-permute-start = (f32[1536,128]{1,0:T(8,128)}, f32[1536,128]{1,0:T(8,128)}, u32[]{:S(2)}, u32[]{:S(2)}) collective-permute-start(f32[1536,128]{1,0:T(8,128)} %get-tuple-element.26), channel_id=1, source_target_pairs={{0,4},{4,0},{8,12},{12,8},{16,20},{20,16},{24,28},{28,24},{1,5},{5... | collective-permute-start | bytes 2359304 | tf_op jit(solution)/shard_map/ppermute | solution.py:290
  17.2 18.8 %collective-permute-start.7 = (f32[768,128]{1,0:T(8,128)}, f32[768,128]{1,0:T(8,128)S(1)}, u32[]{:S(2)}, u32[]{:S(2)}) collective-permute-start(f32[768,128]{1,0:T(8,128)} %get-tuple-element.33), channel_id=1, source_target_pairs={{4,12},{8,0},{12,20},{16,8},{20,28},{24,16},{5,13},{9,1},{13,21},{... | collective-permute-start | bytes 1179656 | tf_op jit(solution)/shard_map/ppermute | solution.py:295
  20.8 23.5 %collective-permute-start.13 = (f32[768,128]{1,0:T(8,128)}, f32[768,128]{1,0:T(8,128)S(1)}, u32[]{:S(2)}, u32[]{:S(2)}) collective-permute-start(f32[768,128]{1,0:T(8,128)} %get-tuple-element.39), channel_id=1, source_target_pairs={{4,12},{8,0},{12,20},{16,8},{20,28},{24,16},{5,13},{9,1},{13,21},{... | collective-permute-start | bytes 1179656 | tf_op jit(solution)/shard_map/ppermute | solution.py:295
  23.7 28.3 %collective-permute-start.19 = (f32[768,128]{1,0:T(8,128)}, f32[768,128]{1,0:T(8,128)S(1)}, u32[]{:S(2)}, u32[]{:S(2)}) collective-permute-start(f32[768,128]{1,0:T(8,128)} %get-tuple-element.45), channel_id=1, source_target_pairs={{4,12},{8,0},{12,20},{16,8},{20,28},{24,16},{5,13},{9,1},{13,21},{... | collective-permute-start | bytes 1179656 | tf_op jit(solution)/shard_map/ppermute | solution.py:295
  36.0 24.6 %collective-permute-start.12 = (f32[1024,128]{1,0:T(8,128)}, f32[1024,128]{1,0:T(8,128)S(1)}, u32[]{:S(2)}, u32[]{:S(2)}) collective-permute-start(f32[1024,128]{1,0:T(8,128)} %copy-done.11), channel_id=1, source_target_pairs={{0,4},{4,0},{8,12},{12,8},{16,20},{20,16},{24,28},{28,24},{1,5},{5... | collective-permute-start | bytes 1572872 | tf_op jit(solution)/shard_map/ppermute | solution.py:290
  44.4 19.8 %collective-permute-start.18 = (f32[1024,128]{1,0:T(8,128)}, f32[1024,128]{1,0:T(8,128)S(1)}, u32[]{:S(2)}, u32[]{:S(2)}) collective-permute-start(f32[1024,128]{1,0:T(8,128)} %copy-done.10), channel_id=1, source_target_pairs={{0,4},{4,0},{8,12},{12,8},{16,20},{20,16},{24,28},{28,24},{1,5},{5... | collective-permute-start | bytes 1572872 | tf_op jit(solution)/shard_map/ppermute | solution.py:290
  53.0 18.0 %collective-permute-start.6 = (f32[1024,128]{1,0:T(8,128)}, f32[1024,128]{1,0:T(8,128)S(1)}, u32[]{:S(2)}, u32[]{:S(2)}) collective-permute-start(f32[1024,128]{1,0:T(8,128)} %copy-done.9), channel_id=1, source_target_pairs={{0,4},{4,0},{8,12},{12,8},{16,20},{20,16},{24,28},{28,24},{1,5},{5... | collective-permute-start | bytes 1572872 | tf_op jit(solution)/shard_map/ppermute | solution.py:290
  56.2 27.2 %collective-permute-start.2 = (f32[1216,128]{1,0:T(8,128)S(1)}, f32[1216,128]{1,0:T(8,128)S(1)}, u32[]{:S(2)}, u32[]{:S(2)}) collective-permute-start(f32[1216,128]{1,0:T(8,128)S(1)} %pad_maximum_fusion.12), channel_id=1, source_target_pairs={{0,8},{8,16},{12,4},{16,24},{20,12},{28,20},{1,9},{9,17},{13,5},{1... | collective-permute-start | bytes 1867784 | tf_op jit(solution)/shard_map/ppermute | solution.py:300
  60.7 22.7 %collective-permute-start.14 = (f32[768,128]{1,0:T(8,128)S(1)}, f32[768,128]{1,0:T(8,128)S(1)}, u32[]{:S(2)}, u32[]{:S(2)}) collective-permute-start(f32[768,128]{1,0:T(8,128)S(1)} %bitcast.135), channel_id=1, source_target_pairs={{0,8},{8,16},{12,4},{16,24},{20,12},{28,20},{1,9},{9,17},{13,5},{1... | collective-permute-start | bytes 1179656 | tf_op jit(solution)/shard_map/ppermute | solution.py:300
  64.3 28.5 %collective-permute-start.20 = (f32[768,128]{1,0:T(8,128)S(1)}, f32[768,128]{1,0:T(8,128)S(1)}, u32[]{:S(2)}, u32[]{:S(2)}) collective-permute-start(f32[768,128]{1,0:T(8,128)S(1)} %bitcast.134), channel_id=1, source_target_pairs={{0,8},{8,16},{12,4},{16,24},{20,12},{28,20},{1,9},{9,17},{13,5},{1... | collective-permute-start | bytes 1179656 | tf_op jit(solution)/shard_map/ppermute | solution.py:300
  71.0 26.8 %collective-permute-start.8 = (f32[768,128]{1,0:T(8,128)S(1)}, f32[768,128]{1,0:T(8,128)S(1)}, u32[]{:S(2)}, u32[]{:S(2)}) collective-permute-start(f32[768,128]{1,0:T(8,128)S(1)} %bitcast.133), channel_id=1, source_target_pairs={{0,8},{8,16},{12,4},{16,24},{20,12},{28,20},{1,9},{9,17},{13,5},{1... | collective-permute-start | bytes 1179656 | tf_op jit(solution)/shard_map/ppermute | solution.py:300
  84.8 14.5 %collective-permute-start.4 = (f32[2304,128]{1,0:T(8,128)S(1)}, f32[2304,128]{1,0:T(8,128)S(1)}, u32[]{:S(2)}, u32[]{:S(2)}) collective-permute-start(f32[2304,128]{1,0:T(8,128)S(1)} %pad_maximum_fusion.2), channel_id=1, source_target_pairs={{1,0},{2,1},{3,2},{5,4},{6,5},{7,6},{9,8},{10,9},{11,10},{13,12},{... | collective-permute-start | bytes 3538952 | tf_op jit(solution)/shard_map/ppermute | solution.py:310
  86.3 14.3 %collective-permute-start.3 = (f32[2304,128]{1,0:T(8,128)S(1)}, f32[2304,128]{1,0:T(8,128)S(1)}, u32[]{:S(2)}, u32[]{:S(2)}) collective-permute-start(f32[2304,128]{1,0:T(8,128)S(1)} %pad_maximum_fusion.1), channel_id=1, source_target_pairs={{0,1},{1,2},{2,3},{4,5},{5,6},{6,7},{8,9},{9,10},{10,11},{12,13},{... | collective-permute-start | bytes 3538952 | tf_op jit(solution)/shard_map/ppermute | solution.py:305
  89.7 56.5 %collective-permute-start.15 = (f32[1344,128]{1,0:T(8,128)S(1)}, f32[1344,128]{1,0:T(8,128)S(1)}, u32[]{:S(2)}, u32[]{:S(2)}) collective-permute-start(f32[1344,128]{1,0:T(8,128)S(1)} %bitcast.127), channel_id=1, source_target_pairs={{0,1},{1,2},{2,3},{4,5},{5,6},{6,7},{8,9},{9,10},{10,11},{12,13},{... | collective-permute-start | bytes 2064392 | tf_op jit(solution)/shard_map/ppermute | solution.py:305
  92.8 54.0 %collective-permute-start.16 = (f32[1344,128]{1,0:T(8,128)S(1)}, f32[1344,128]{1,0:T(8,128)S(1)}, u32[]{:S(2)}, u32[]{:S(2)}) collective-permute-start(f32[1344,128]{1,0:T(8,128)S(1)} %bitcast.129), channel_id=1, source_target_pairs={{1,0},{2,1},{3,2},{5,4},{6,5},{7,6},{9,8},{10,9},{11,10},{13,12},{... | collective-permute-start | bytes 2064392 | tf_op jit(solution)/shard_map/ppermute | solution.py:310
  97.8 65.7 %collective-permute-start.21 = (f32[1344,128]{1,0:T(8,128)S(1)}, f32[1344,128]{1,0:T(8,128)S(1)}, u32[]{:S(2)}, u32[]{:S(2)}) collective-permute-start(f32[1344,128]{1,0:T(8,128)S(1)} %bitcast.128), channel_id=1, source_target_pairs={{0,1},{1,2},{2,3},{4,5},{5,6},{6,7},{8,9},{9,10},{10,11},{12,13},{... | collective-permute-start | bytes 2064392 | tf_op jit(solution)/shard_map/ppermute | solution.py:305
  99.3 64.2 %collective-permute-start.22 = (f32[1344,128]{1,0:T(8,128)S(1)}, f32[1344,128]{1,0:T(8,128)S(1)}, u32[]{:S(2)}, u32[]{:S(2)}) collective-permute-start(f32[1344,128]{1,0:T(8,128)S(1)} %bitcast.130), channel_id=1, source_target_pairs={{1,0},{2,1},{3,2},{5,4},{6,5},{7,6},{9,8},{10,9},{11,10},{13,12},{... | collective-permute-start | bytes 2064392 | tf_op jit(solution)/shard_map/ppermute | solution.py:310
  108.2 21.2 %collective-permute-start.10 = (f32[1344,128]{1,0:T(8,128)S(1)}, f32[1344,128]{1,0:T(8,128)S(1)}, u32[]{:S(2)}, u32[]{:S(2)}) collective-permute-start(f32[1344,128]{1,0:T(8,128)S(1)} %bitcast.131), channel_id=1, source_target_pairs={{1,0},{2,1},{3,2},{5,4},{6,5},{7,6},{9,8},{10,9},{11,10},{13,12},{... | collective-permute-start | bytes 2064392 | tf_op jit(solution)/shard_map/ppermute | solution.py:310
  129.4 50.0 %collective-permute-start.5 = (f32[8,16,8,128]{3,2,1,0:T(8,128)S(1)}, f32[8,16,8,128]{3,2,1,0:T(8,128)S(1)}, u32[]{:S(2)}, u32[]{:S(2)}) collective-permute-start(f32[8,16,8,128]{3,2,1,0:T(8,128)S(1)} %get-tuple-element.29), channel_id=1, source_target_pairs={{0,4},{4,0},{8,12},{12,8},{16,20},{20,16},{24,28},{28,24},{1,5},{5... | collective-permute-start | bytes 1572872 | tf_op jit(solution)/shard_map/ppermute | solution.py:290
  146.1 33.3 %collective-permute-start.11 = (f32[8,16,8,128]{3,2,1,0:T(8,128)S(1)}, f32[8,16,8,128]{3,2,1,0:T(8,128)S(1)}, u32[]{:S(2)}, u32[]{:S(2)}) collective-permute-start(f32[8,16,8,128]{3,2,1,0:T(8,128)S(1)} %get-tuple-element.35), channel_id=1, source_target_pairs={{0,4},{4,0},{8,12},{12,8},{16,20},{20,16},{24,28},{28,24},{1,5},{5... | collective-permute-start | bytes 1572872 | tf_op jit(solution)/shard_map/ppermute | solution.py:290
  162.0 17.4 %collective-permute-start.17 = (f32[8,16,8,128]{3,2,1,0:T(8,128)S(1)}, f32[8,16,8,128]{3,2,1,0:T(8,128)S(1)}, u32[]{:S(2)}, u32[]{:S(2)}) collective-permute-start(f32[8,16,8,128]{3,2,1,0:T(8,128)S(1)} %get-tuple-element.41), channel_id=1, source_target_pairs={{0,4},{4,0},{8,12},{12,8},{16,20},{20,16},{24,28},{28,24},{1,5},{5... | collective-permute-start | bytes 1572872 | tf_op jit(solution)/shard_map/ppermute | solution.py:290
  192.1 11.6 %collective-permute-start.24 = (f32[64,64]{1,0:T(8,128)S(1)}, f32[64,64]{1,0:T(8,128)S(1)}, u32[]{:S(2)}, u32[]{:S(2)}) collective-permute-start(f32[64,64]{1,0:T(8,128)S(1)} %gram.1), channel_id=1, source_target_pairs={{0,1},{1,0},{2,3},{3,2},{4,5},{5,4},{6,7},{7,6},{8,9},{9,8},{10,11... | collective-permute-start | bytes 49160 | tf_op jit(solution)/shard_map/ppermute | solution.py:326
  203.8 10.9 %collective-permute-start.25 = (f32[64,64]{1,0:T(8,128)S(1)}, f32[64,64]{1,0:T(8,128)S(1)}, u32[]{:S(2)}, u32[]{:S(2)}) collective-permute-start(f32[64,64]{1,0:T(8,128)S(1)} %add.99), channel_id=1, source_target_pairs={{0,2},{1,3},{2,0},{3,1},{4,6},{5,7},{6,4},{7,5},{8,10},{9,11},{10,... | collective-permute-start | bytes 49160 | tf_op jit(solution)/shard_map/ppermute | solution.py:326
  (25 other events, 257.9 us)

commit v3 on v2

--- a/solution.py
+++ b/solution.py
@@ -16,6 +16,7 @@
 DEPTH = 6
 RING = DEPTH + 1
 EDGE = 8
+GROUPS = (2, 2)
 MIB = 1 << 20
 
 
@@ -86,49 +87,66 @@
 
 
 def solve_kernel(h_ref, coef, own, recv, e1, e2, ylo, yhi, keep, back, r_s, a_s, b_s):
-    planes, rows = own.shape[0], own.shape[1]
-    wide_x, wide_y = r_s.shape[0], r_s.shape[1]
+    tiles, planes, rows, many, depth = own.shape
+    wide_x, wide_y = r_s.shape[1], r_s.shape[2]
     side = h_ref[0]
     top = DEPTH + 2 * planes
+
+    def fields(ref, n, m):
+        return ref.at[pl.ds(0, tiles * n * m * many)].reshape(tiles, n, m, many, depth)
+
+    ylo, yhi = fields(ylo, wide_x, DEPTH), fields(yhi, wide_x, DEPTH)
     parts = (
         (own, 0, planes, DEPTH + planes * side),
-        (recv, planes, planes, DEPTH + planes * (1 - side)),
-        (e1, 2 * planes, DEPTH, top * (1 - side)),
-        (e2, 2 * planes + DEPTH, DEPTH, top * side),
+        (fields(recv, planes, rows), planes, planes, DEPTH + planes * (1 - side)),
+        (fields(e1, DEPTH, rows), 2 * planes, DEPTH, top * (1 - side)),
+        (fields(e2, DEPTH, rows), 2 * planes + DEPTH, DEPTH, top * side),
     )
 
     def row(which, x, y):
-        return spread(coef, which, x, y, own.shape[2])
+        return spread(coef, which, x, y, many)
 
     for piece, role, count, place in parts:
 
         def fill(i, carry, piece=piece, role=role, place=place):
             x = place + i
             for y in range(wide_y):
-                if y < DEPTH:
-                    value = ylo[role + i, y]
-                elif y < DEPTH + rows:
-                    value = piece[i, y - DEPTH]
-                else:
-                    value = yhi[role + i, y - DEPTH - rows]
-                r_s[x, y] = value * row(6, x, y)
+                scale = row(6, x, y)
+                for t in range(tiles):
+                    if y < DEPTH:
+                        value = ylo[t, role + i, y]
+                    elif y < DEPTH + rows:
+                        value = piece[t, i, y - DEPTH]
+                    else:
+                        value = yhi[t, role + i, y - DEPTH - rows]
+                    r_s[t, x, y] = value * scale
             return carry
 
         lax.fori_loop(0, count, fill, 0)
 
-    def stencil(src, r, x, low, scale):
-        here = [src[x, y] for y in range(low - 1, wide_y - low + 1)]
+    def stencil(src, r, x, low, scale, last=None):
+        span = range(tiles)
+        prev = [src[t, x, low - 1] for t in span]
+        here = [src[t, x, low] for t in span]
         for y in range(low, wide_y - low):
-            k = y - low + 1
-            total = row(0, x, y) * src[x - 1, y] + row(1, x, y) * src[x + 1, y]
-            total = total + row(2, x, y) * here[k - 1] + row(3, x, y) * here[k + 1]
-            total = total + row(4, x, y) * pltpu.roll(here[k], 1, 1) + row(5, x, y) * pltpu.roll(here[k], 127, 1)
-            yield y, r[x, y] + scale * total
+            after = [src[t, x, y + 1] for t in span]
+            c = [row(k, x, y) for k in range(6)]
+            end = None if last is None else row(last, x, y)
+            values = []
+            for t in span:
+                total = c[0] * src[t, x - 1, y] + c[1] * src[t, x + 1, y]
+                total = total + (c[2] * prev[t] + c[3] * after[t])
+                total = total + (c[4] * pltpu.roll(here[t], 1, 1) + c[5] * pltpu.roll(here[t], 127, 1))
+                value = r[t, x, y] + scale * total
+                values.append(value if end is None else value * end)
+            yield y, values
+            prev, here = here, after
 
     def sweep(src, dst, r, low, scale, last=None):
         def plane(x, carry):
-            for y, value in stencil(src, r, x, low, scale):
-                dst[x, y] = value if last is None else value * row(last, x, y)
+            for y, values in stencil(src, r, x, low, scale, last):
+                for t, value in enumerate(values):
+                    dst[t, x, y] = value
             return carry
 
         lax.fori_loop(low, wide_x - low, plane, 0)
@@ -141,29 +159,29 @@
     for target, place in ((back, parts[1][3]), (keep, parts[0][3])):
 
         def out(i, carry, target=target, place=place):
-            x = place + i
-            for y, value in stencil(r_s, a_s, x, DEPTH, A1 / A0):
-                target[i, y - DEPTH] = value * row(8, x, y)
+            for y, values in stencil(r_s, a_s, place + i, DEPTH, A1 / A0, last=8):
+                for t, value in enumerate(values):
+                    target[t, i, y - DEPTH] = value
             return carry
 
         lax.fori_loop(0, planes, out, 0)
 
 
-def solve(side, coef, own, recv, e1, e2, ylo, yhi):
-    wide_x, wide_y = coef.shape[1], coef.shape[2]
-    many, depth = own.shape[2:]
-    field = pltpu.VMEM((wide_x, wide_y, many, depth), jnp.float32)
-    cells = wide_x * wide_y * many * depth
+def solve(side, coef, own, *messages):
+    tiles, _, _, many, depth = own.shape
+    wide_x, wide_y = coef.shape[1:3]
+    field = pltpu.VMEM((tiles, wide_x, wide_y, many, depth), jnp.float32)
+    cells = tiles * wide_x * wide_y * many * depth
     return pl.pallas_call(
         solve_kernel,
         in_specs=[smem()] + [vmem()] * 7,
         out_specs=[vmem(), vmem()],
         out_shape=[jax.ShapeDtypeStruct(own.shape, jnp.float32)] * 2,
         scratch_shapes=[field, field, field],
-        compiler_params=pltpu.CompilerParams(vmem_limit_bytes=(14 + 14 * many // 8) * MIB),
+        compiler_params=pltpu.CompilerParams(vmem_limit_bytes=(14 + 14 * tiles) * MIB),
         cost_estimate=pl.CostEstimate(flops=60 * cells, bytes_accessed=12 * MIB, transcendentals=0),
         name="both_solves",
-    )(side, coef, own, recv, e1, e2, ylo, yhi)
+    )(side, coef, own, *messages)
 
 
 def stacked(side, tiles, rows):
@@ -171,7 +189,7 @@
     for y in range(rows):
         parts = []
         for keep, got in zip(tiles[0::2], tiles[1::2]):
-            a, b = keep[0, y], got[0, y]
+            a, b = keep[0, 0, y], got[0, 0, y]
             parts += [jnp.where(side == 0, a, b), jnp.where(side == 0, b, a)]
         columns.append(jnp.concatenate(parts, axis=0))
     return jnp.concatenate(columns, axis=1)
@@ -190,7 +208,7 @@
     def _():
         total[...] = jnp.zeros_like(total)
 
-    both = jnp.concatenate(split(stacked(h_ref[0], tiles, tiles[0].shape[1])), axis=0)
+    both = jnp.concatenate(split(stacked(h_ref[0], tiles, tiles[0].shape[2])), axis=0)
     total[...] += lax.dot_general(both, both, (((1,), (1,)), ((), ())), preferred_element_type=jnp.float32)
 
     @pl.when(step == pl.num_programs(0) - 1)
@@ -200,16 +218,26 @@
         out[...] = g * scale
 
 
-def tile_spec(shape):
-    return pl.BlockSpec((1,) + shape[1:], lambda i: (i, 0, 0, 0))
-
-
-def gram_of(side, tiles, cells):
+def tile_specs(groups):
+    return [
+        pl.BlockSpec((1, 1) + g.shape[2:], lambda i, t=t: (t, i, 0, 0, 0))
+        for keep, got in groups
+        for t in range(keep.shape[0])
+        for g in (keep, got)
+    ]
+
+
+def tile_args(groups):
+    return [g for keep, got in groups for t in range(keep.shape[0]) for g in (keep, got)]
+
+
+def gram_of(side, groups, cells):
+    tiles = tile_args(groups)
     count = 8 * len(tiles)
     return pl.pallas_call(
         functools.partial(gram_kernel, 1.0 / cells),
-        grid=(tiles[0].shape[0],),
-        in_specs=[smem()] + [tile_spec(t.shape) for t in tiles],
+        grid=(tiles[0].shape[1],),
+        in_specs=[smem()] + tile_specs(groups),
         out_specs=pl.BlockSpec((count, count), lambda i: (0, 0)),
         out_shape=jax.ShapeDtypeStruct((count, count), jnp.float32),
         scratch_shapes=[pltpu.VMEM((2 * count, 2 * count), jnp.float32)],
@@ -246,7 +274,7 @@
 def basis_kernel(h_ref, a_ref, b_ref, *refs):
     tiles, (q_ref, r_ref, left) = refs[:-3], refs[-3:]
     n = r_ref.shape[0]
-    rows = tiles[0].shape[1]
+    rows = tiles[0].shape[2]
 
     @pl.when(pl.program_id(0) == 0)
     def _():
@@ -266,14 +294,15 @@
         flat[pl.ds(y, n, stride=rows), :] = q[:, y * depth : (y + 1) * depth]
 
 
-def basis(side, a, b, tiles):
+def basis(side, a, b, groups):
     n = a.shape[0]
-    planes, rows, _, depth = tiles[0].shape
+    tiles = tile_args(groups)
+    _, planes, rows, _, depth = tiles[0].shape
     full = pl.BlockSpec((n, n), lambda i: (0, 0))
     return pl.pallas_call(
         basis_kernel,
         grid=(planes,),
-        in_specs=[smem(), full, full] + [tile_spec(t.shape) for t in tiles],
+        in_specs=[smem(), full, full] + tile_specs(groups),
         out_specs=[pl.BlockSpec((n, 1, rows, depth), lambda i: (0, i, 0, 0)), full],
         out_shape=[
             jax.ShapeDtypeStruct((n, planes, rows, depth), jnp.float32),
@@ -362,15 +391,15 @@
     return parts[0] if len(parts) == 1 else jnp.concatenate(parts, axis=0)
 
 
-def parts_of(flat, *shapes):
-    out, at = [], 0
-    for shape in shapes:
-        size = 1
-        for n in shape[:-1]:
-            size *= n
-        out.append(flat[at : at + size].reshape(shape))
-        at += size
-    return out
+def fields_of(flat, *shape):
+    size = 1
+    for n in shape[:-1]:
+        size *= n
+    return flat[:size].reshape(shape)
+
+
+def maps_of(flat, skip, *shape):
+    return flat[skip:].reshape(shape)
 
 
 def body(probes, permeability, absorption, sensitivity, observe_weight):
@@ -381,50 +410,55 @@
     flag = side.reshape(1).astype(jnp.int32)
     maps = (permeability, absorption, sensitivity, observe_weight)
     tall = 2 * planes + 2 * DEPTH
-
-    tiles = []
+    assert 16 * sum(GROUPS) == count
+
+    groups = []
     coef = turn = None
-    for tile in range(count // 16):
+    tile = 0
+    for size in GROUPS:
         mine = maps if tile == 0 else ()
-        own, send, edge = prep(flag, probes, tile, mine)
+        owns, sends, edges = zip(*[prep(flag, probes, tile + t, mine if t == size - 1 else ()) for t in range(size)])
+        tile += size
+        own, send, edge = jnp.stack(owns), rows_of(*sends), rows_of(*edges)
         if turn is not None:
-            send, turn = lax.optimization_barrier((send, turn))
-        recv_rows = swap(send)
-        e1_rows = outward(edge)
-        block, halo = (planes, rows, 8, depth), (DEPTH, rows, 8, depth)
-        four, ring = (len(maps), planes, rows, depth), (len(maps), RING, rows, depth)
-        recv, *recv_maps = parts_of(recv_rows, block, *([four] if mine else []))
-        inner = [lax.dynamic_slice_in_dim(recv, (1 - side) * (planes - DEPTH), DEPTH, 0)]
-        for value in recv_maps:
-            inner.append(lax.dynamic_slice_in_dim(value, (1 - side) * (planes - RING), RING, 1))
-        e2_rows = inward(rows_of(*inner))
-        e1, *e1_maps = parts_of(e1_rows, halo, *([ring] if mine else []))
-        e2, *e2_maps = parts_of(e2_rows, halo, *([ring] if mine else []))
-        turn = e1
-        low = [jnp.concatenate([p[:, rows - DEPTH :] for p in (own, recv, e1, e2)], axis=0)]
-        high = [jnp.concatenate([p[:, :DEPTH] for p in (own, recv, e1, e2)], axis=0)]
+            send, edge, turn = lax.optimization_barrier((send, edge, turn))
+        recv = swap(send)
+        e1 = outward(edge)
+        turn = recv
+        block, halo = (size, planes, rows, 8, depth), (size, DEPTH, rows, 8, depth)
+        recv_f = fields_of(recv, *block)
+        inner = [lax.dynamic_slice_in_dim(recv_f, (1 - side) * (planes - DEPTH), DEPTH, 1)]
         if mine:
-            own_maps = jnp.stack(maps)
+            recv_m = maps_of(recv, size * planes * rows * 8, len(maps), planes, rows, depth)
+            inner.append(lax.dynamic_slice_in_dim(recv_m, (1 - side) * (planes - RING), RING, 1))
+        e2 = inward(rows_of(*inner))
+        whole = (own, recv_f, fields_of(e1, *halo), fields_of(e2, *halo))
+        low = [jnp.concatenate([p[:, :, rows - DEPTH :] for p in whole], axis=1)]
+        high = [jnp.concatenate([p[:, :, :DEPTH] for p in whole], axis=1)]
+        if mine:
+            own_m = jnp.stack(maps)
+            skip = size * DEPTH * rows * 8
+            e1_m, e2_m = (maps_of(e, skip, len(maps), RING, rows, depth) for e in (e1, e2))
             wide = jnp.concatenate(
                 [
-                    jnp.where(lower, e2_maps[0], e1_maps[0]),
-                    jnp.where(lower, own_maps, recv_maps[0]),
-                    jnp.where(lower, recv_maps[0], own_maps),
-                    jnp.where(lower, e1_maps[0], e2_maps[0]),
+                    jnp.where(lower, e2_m, e1_m),
+                    jnp.where(lower, own_m, recv_m),
+                    jnp.where(lower, recv_m, own_m),
+                    jnp.where(lower, e1_m, e2_m),
                 ],
                 axis=1,
             )
             low.append(wide[:, :, rows - EDGE :])
             high.append(wide[:, :, :EDGE])
-        shapes = [v.shape for v in low]
-        ylo, *map_low = parts_of(above(rows_of(*low)), *shapes)
-        yhi, *map_high = parts_of(below(rows_of(*high)), *shapes)
+        ylo, yhi = above(rows_of(*low)), below(rows_of(*high))
         if mine:
-            coef = coefficients(side, jnp.concatenate([map_low[0], wide, map_high[0]], axis=2), planes, rows)
+            skip = size * tall * DEPTH * 8
+            ends = [maps_of(y, skip, len(maps), tall + 2, EDGE, depth) for y in (ylo, yhi)]
+            coef = coefficients(side, jnp.concatenate([ends[0], wide, ends[1]], axis=2), planes, rows)
         keep, back = solve(flag, coef, own, recv, e1, e2, ylo, yhi)
-        tiles += [keep, swap(back)]
-    a, b = summed(gram_of(flag, tiles, cells))
-    q, r = basis(flag, a, b, tiles)
+        groups.append((keep, swap(back)))
+    a, b = summed(gram_of(flag, groups, cells))
+    q, r = basis(flag, a, b, groups)
     return (q, r)
 
 

time: 239 us -> 219 us (0.916)
  starting transfers between devices: 76.7 us -> 32.5 us
  waiting for transfers between devices: 61.8 us -> 84 us
  Pallas kernels: 80.6 us -> 65 us
  other arithmetic: 3.4 us -> 18.5 us
  local copies, waits for them, and re-layouts: 13.7 us -> 17 us
    ppermute x8 -> x4, waiting for transfers between devices: 13.3 us -> 42.9 us  [swap(): lax.ppermute(value, 'gx', [(i, i ^ 1) for i in range(lax.axis_size('gx'))])]
    ppermute x4 -> x2, waiting for transfers between devices: 21.4 us -> 0.01 us  [outward(): lax.ppermute(value, 'gx', [(i, i + 2 * (i % 2) * 2 - 2) for i in range(n)...]
    ppermute x4 -> x2, waiting for transfers between devices: 12.4 us -> 30.4 us  [inward(): lax.ppermute(value, 'gx', [(i, i + 2 - 4 * (i % 2)) for i in range(n) if...]
    ppermute x5, starting transfers between devices: 24.7 us -> 7.74 us  [summed(): other = lax.ppermute(value, axis, [(i, i ^ shift) for i in range(n)])]
    pallas_call x4 -> x2, Pallas kernels: 60.9 us -> 48.7 us  [solve(): pl.pallas_call(solve_kernel, in_specs=[smem()] + [vmem()] * 7, out_specs=...]
    concatenate x3 -> x7, other arithmetic: 0.2 us -> 10.3 us  [rows_of(): return parts[0] if len(parts) == 1 else jnp.concatenate(parts, axis=0)]
    ppermute x8 -> x4, starting transfers between devices: 13.5 us -> 5.57 us  [swap(): lax.ppermute(value, 'gx', [(i, i ^ 1) for i in range(lax.axis_size('gx'))])]
    ppermute x4 -> x2, starting transfers between devices: 13.2 us -> 5.79 us  [above(): return lax.ppermute(value, 'gy', [(i, i + 1) for i in range(n - 1)])]
  transfers between devices with their start and end apart: 29 -> 17, of which waited for: 13 -> 9; matrix products, arithmetic and copies ran while one was open for 4% -> 10% of each run, Pallas kernels for 28% -> 23%
where the time goes in v3:
time: 219 us; the launch traced here: 218 us
  waiting for transfers between devices  84 us (38%)
  Pallas kernels  65 us (30%)
  starting transfers between devices  32.5 us (15%)
  other arithmetic  18.5 us (8%)
  local copies, waits for them, and re-layouts  17 us (8%)
    pallas_call x2, Pallas kernels, solve(): pl.pallas_call(solve_kernel, in_specs=[smem()] + [vmem()] * 7, out_specs=...  48.7 us
    ppermute x4, waiting for transfers between devices, swap(): lax.ppermute(value, 'gx', [(i, i ^ 1) for i in range(lax.axis_size('gx'))])  42.9 us
    ppermute x2, waiting for transfers between devices, inward(): lax.ppermute(value, 'gx', [(i, i + 2 - 4 * (i % 2)) for i in range(n) if...  30.4 us
    unnamed x78, local copies, waits for them, and re-layouts  11.7 us
    ppermute x5, waiting for transfers between devices, summed(): other = lax.ppermute(value, axis, [(i, i ^ shift) for i in range(n)])  10.7 us
    pallas_call x1, Pallas kernels, basis(): pl.pallas_call(basis_kernel, grid=(planes,), in_specs=[smem(), full, full...  10.4 us
    concatenate x7, other arithmetic, rows_of(): return parts[0] if len(parts) == 1 else jnp.concatenate(parts, axis=0)  10.3 us
    ppermute x2, starting transfers between devices, inward(): lax.ppermute(value, 'gx', [(i, i + 2 - 4 * (i % 2)) for i in range(n) if...  8.25 us
  transfers between devices with their start and end apart: 17, of which 9 were waited for; matrix products, arithmetic and copies ran while one was open for 10% of the time, Pallas kernels for 23%

profile of v3, /device:TPU:0, one launch (start us, length us, event | category | flops | bytes accessed | tf_op | source)
XLA Modules:
  0.0 218.4 jit_solution(15375693840745677342)
XLA Ops:
  0.7 1.6 copy-done
  5.9 2.9 %collective-permute-start = (f32[2560,128]{1,0:T(8,128)}, f32[2560,128]{1,0:T(8,128)S(1)}, u32[]{:S(2)}, u32[]{:S(2)}) collective-permute-start(f32[2560,128]{1,0:T(8,128)} %pad_maximum_fusion.9), channel_id=1, source_target_pairs={{0,4},{4,0},{8,12},{12,8},{16,20},{20,16},{24,28},{28,24},{1,5},{5... | collective-permute-start | bytes 3932168 | tf_op jit(solution)/shard_map/ppermute | solution.py:319
  17.6 2.3 %pad_maximum_fusion.10 = f32[2048,128]{1,0:T(8,128)} fusion(f32[1024,128]{1,0:T(8,128)} %copy-done.14, f32[1024,128]{1,0:T(8,128)} %copy-done.15), kind=kLoop, calls=%fused_computation.20 | loop fusion | flops 262144 | bytes 2097152 | tf_op jit(solution)/shard_map/concatenate | solution.py:391
  19.9 17.9 %collective-permute-done.recv = f32[2560,128]{1,0:T(8,128)S(1)} collective-permute-done((f32[2560,128]{1,0:T(8,128)}, f32[2560,128]{1,0:T(8,128)S(1)}, u32[]{:S(2)}, u32[]{:S(2)}) %collective-permute-start) | collective-permute-done | bytes 1310752 | tf_op jit(solution)/shard_map/ppermute | solution.py:319
  39.9 3.8 %collective-permute-start.2 = (f32[1984,128]{1,0:T(8,128)}, f32[1984,128]{1,0:T(8,128)S(1)}, u32[]{:S(2)}, u32[]{:S(2)}) collective-permute-start(f32[1984,128]{1,0:T(8,128)} %pad_maximum_fusion.12), channel_id=1, source_target_pairs={{0,8},{8,16},{12,4},{16,24},{20,12},{28,20},{1,9},{9,17},{13,5},{1... | collective-permute-start | bytes 3047432 | tf_op jit(solution)/shard_map/ppermute | solution.py:329
  44.8 2.1 pad_maximum_fusion.14
  49.8 15.0 %collective-permute-done.2.e2 = f32[1984,128]{1,0:T(8,128)S(1)} collective-permute-done((f32[1984,128]{1,0:T(8,128)}, f32[1984,128]{1,0:T(8,128)S(1)}, u32[]{:S(2)}, u32[]{:S(2)}) %collective-permute-start.2) | collective-permute-done | bytes 1015840 | tf_op jit(solution)/shard_map/ppermute | solution.py:329
  72.2 4.4 %collective-permute-start.3 = (f32[3648,128]{1,0:T(8,128)}, f32[3648,128]{1,0:T(8,128)}, u32[]{:S(2)}, u32[]{:S(2)}) collective-permute-start(f32[3648,128]{1,0:T(8,128)} %pad_maximum_fusion.1), channel_id=1, source_target_pairs={{0,1},{1,2},{2,3},{4,5},{5,6},{6,7},{8,9},{9,10},{10,11},{12,13},{... | collective-permute-start | bytes 5603336 | tf_op jit(solution)/shard_map/ppermute | solution.py:334
  78.1 4.5 %collective-permute-start.8 = (f32[1536,128]{1,0:T(8,128)S(1)}, f32[1536,128]{1,0:T(8,128)S(1)}, u32[]{:S(2)}, u32[]{:S(2)}) collective-permute-start(f32[1536,128]{1,0:T(8,128)S(1)} %bitcast.90), channel_id=1, source_target_pairs={{0,8},{8,16},{12,4},{16,24},{20,12},{28,20},{1,9},{9,17},{13,5},{1... | collective-permute-start | bytes 2359304 | tf_op jit(solution)/shard_map/ppermute | solution.py:329
  84.0 15.4 %collective-permute-done.8.e2 = f32[1536,128]{1,0:T(8,128)S(1)} collective-permute-done((f32[1536,128]{1,0:T(8,128)S(1)}, f32[1536,128]{1,0:T(8,128)S(1)}, u32[]{:S(2)}, u32[]{:S(2)}) %collective-permute-start.8) | collective-permute-done | bytes 786464 | tf_op jit(solution)/shard_map/ppermute | solution.py:329
  108.7 2.0 copy-done.24
  110.7 25.0 %both_solves.2 = (f32[2,8,16,8,128]{4,3,2,1,0:T(8,128)S(1)}, f32[2,8,16,8,128]{4,3,2,1,0:T(8,128)S(1)}) custom-call(s32[1]{0:T(128)} %bitcast.h_ref, f32[9,28,28,128]{3,2,1,0:T(8,128)} %copy-done.24, f32[2,8,16,8,128]{4,3,2,1,0:T(8,128)S(1)} %pad_maximum_fusion.3.own, f32[2560,128]{1,0:T(8,128)S(1)} %collective-permute-done.recv, ...), custom_call_target="tpu_custom_call" | custom-call | flops 96337920 | bytes 12582912 | tf_op jit(solution)/shard_map/both_solves/pallas_call | solution.py:175
  135.7 2.5 %collective-permute-start.5 = (f32[2,8,16,8,128]{4,3,2,1,0:T(8,128)S(1)}, f32[2,8,16,8,128]{4,3,2,1,0:T(8,128)S(1)}, u32[]{:S(2)}, u32[]{:S(2)}) collective-permute-start(f32[2,8,16,8,128]{4,3,2,1,0:T(8,128)S(1)} %get-tuple-element.27), channel_id=1, source_target_pairs={{0,4},{4,0},{8,12},{12,8},{16,20},{20,16},{24,28},{28,24},{1,5},{5... | collective-permute-start | bytes 3145736 | tf_op jit(solution)/shard_map/ppermute | solution.py:319
  138.2 23.7 %both_solves.3 = (f32[2,8,16,8,128]{4,3,2,1,0:T(8,128)S(1)}, f32[2,8,16,8,128]{4,3,2,1,0:T(8,128)S(1)}) custom-call(s32[1]{0:T(128)} %bitcast.h_ref, f32[9,28,28,128]{3,2,1,0:T(8,128)} %copy-done.24, f32[2,8,16,8,128]{4,3,2,1,0:T(8,128)S(1)} %pad_maximum_fusion.4.own, f32[2048,128]{1,0:T(8,128)S(1)} %collective-permute-done.6.recv, ...), custom_call_target="tpu_custom_call" | custom-call | flops 96337920 | bytes 12582912 | tf_op jit(solution)/shard_map/both_solves/pallas_call | solution.py:175
  162.0 24.9 %collective-permute-done.11.refs_5_.refs_7_ = f32[2,8,16,8,128]{4,3,2,1,0:T(8,128)S(1)} collective-permute-done((f32[2,8,16,8,128]{4,3,2,1,0:T(8,128)S(1)}, f32[2,8,16,8,128]{4,3,2,1,0:T(8,128)S(1)}, u32[]{:S(2)}, u32[]{:S(2)}) %collective-permute-start.11) | collective-permute-done | bytes 1048608 | tf_op jit(solution)/shard_map/ppermute | solution.py:319
  186.9 2.7 %gram.1 = f32[64,64]{1,0:T(8,128)S(1)} custom-call(s32[1]{0:T(128)} %bitcast.h_ref, f32[2,8,16,8,128]{4,3,2,1,0:T(8,128)S(1)} %get-tuple-element.26.refs_0_.refs_2_, f32[2,8,16,8,128]{4,3,2,1,0:T(8,128)S(1)} %collective-permute-done.5.refs_1_.refs_3_, f32[2,8,16,8,128]{4,3,2,1,0:T(8,128)S(1)} %get-tuple-element.26.refs_0_.refs_2_, ...), custom_call_target="tpu_custom_call" | custom-call | bytes 6291456 | tf_op jit(solution)/shard_map/gram/pallas_call | solution.py:237
  191.4 2.1 collective-permute-start.13
  193.5 1.9 collective-permute-done.13
  195.7 3.6 %collective-permute-done.14 = f32[64,64]{1,0:T(8,128)S(1)} collective-permute-done((f32[64,64]{1,0:T(8,128)S(1)}, f32[64,64]{1,0:T(8,128)S(1)}, u32[]{:S(2)}, u32[]{:S(2)}) %collective-permute-start.14) | collective-permute-done | bytes 16416 | tf_op jit(solution)/shard_map/ppermute | solution.py:355
  199.3 1.6 collective-permute-start.15
  200.9 2.3 %collective-permute-done.15 = f32[64,64]{1,0:T(8,128)S(1)} collective-permute-done((f32[64,64]{1,0:T(8,128)S(1)}, f32[64,64]{1,0:T(8,128)S(1)}, u32[]{:S(2)}, u32[]{:S(2)}) %collective-permute-start.15) | collective-permute-done | bytes 16416 | tf_op jit(solution)/shard_map/ppermute | solution.py:355
  203.2 2.8 %collective-permute-start.16 = (f32[64,64]{1,0:T(8,128)S(1)}, f32[64,64]{1,0:T(8,128)S(1)}, u32[]{:S(2)}, u32[]{:S(2)}) collective-permute-start(f32[64,64]{1,0:T(8,128)S(1)} %add.100.a_ref), channel_id=1, source_target_pairs={{0,16},{4,20},{8,24},{12,28},{16,0},{20,4},{24,8},{28,12},{1,17},{... | collective-permute-start | bytes 49160 | tf_op jit(solution)/shard_map/ppermute | solution.py:355
  206.0 2.0 collective-permute-done.16.b_ref
  208.0 10.4 %basis.1 = (f32[64,8,16,128]{3,2,1,0:T(8,128)}, f32[64,64]{1,0:T(8,128)}) custom-call(s32[1]{0:T(128)} %bitcast.h_ref, f32[64,64]{1,0:T(8,128)S(1)} %add.100.a_ref, f32[64,64]{1,0:T(8,128)S(1)} %collective-permute-done.16.b_ref, f32[2,8,16,8,128]{4,3,2,1,0:T(8,128)S(1)} %get-tuple-element.26.refs_0_.refs_2_, ...), custom_call_target="tpu_custom_call" | custom-call | bytes 8388608 | tf_op jit(solution)/shard_map/basis/pallas_call | solution.py:302
  (148 shorter events, 39.7 us)
Async XLA Ops:
  4.8 6.4 %copy-start.1 = (bf16[64,8,16,128]{3,2,1,0:T(8,128)(2,1)S(1)}, bf16[64,8,16,128]{3,2,1,0:T(8,128)(2,1)}, u32[]{:S(2)}) copy-start(bf16[64,8,16,128]{3,2,1,0:T(8,128)(2,1)} %theirs_ref.7) | copy-start | bytes 6291460
  5.9 31.9 %collective-permute-start = (f32[2560,128]{1,0:T(8,128)}, f32[2560,128]{1,0:T(8,128)S(1)}, u32[]{:S(2)}, u32[]{:S(2)}) collective-permute-start(f32[2560,128]{1,0:T(8,128)} %pad_maximum_fusion.9), channel_id=1, source_target_pairs={{0,4},{4,0},{8,12},{12,8},{16,20},{20,16},{24,28},{28,24},{1,5},{5... | collective-permute-start | bytes 3932168 | tf_op jit(solution)/shard_map/ppermute | solution.py:319
  9.9 37.0 %collective-permute-start.1 = (f32[1984,128]{1,0:T(8,128)}, f32[1984,128]{1,0:T(8,128)}, u32[]{:S(2)}, u32[]{:S(2)}) collective-permute-start(f32[1984,128]{1,0:T(8,128)} %pad_maximum_fusion.11), channel_id=1, source_target_pairs={{4,12},{8,0},{12,20},{16,8},{20,28},{24,16},{5,13},{9,1},{13,21},{... | collective-permute-start | bytes 3047432 | tf_op jit(solution)/shard_map/ppermute | solution.py:324
  38.6 5.1 %copy-start.5 = (f32[8,16,8,128]{3,2,1,0:T(8,128)S(1)}, f32[8,16,8,128]{3,2,1,0:T(8,128)}, u32[]{:S(2)}) copy-start(f32[8,16,8,128]{3,2,1,0:T(8,128)} %copy-done.4) | copy-start | bytes 1572868
  38.6 5.1 %copy-start.8 = (f32[8,16,8,128]{3,2,1,0:T(8,128)S(1)}, f32[8,16,8,128]{3,2,1,0:T(8,128)}, u32[]{:S(2)}) copy-start(f32[8,16,8,128]{3,2,1,0:T(8,128)} %copy-done.7) | copy-start | bytes 1572868
  39.9 24.9 %collective-permute-start.2 = (f32[1984,128]{1,0:T(8,128)}, f32[1984,128]{1,0:T(8,128)S(1)}, u32[]{:S(2)}, u32[]{:S(2)}) collective-permute-start(f32[1984,128]{1,0:T(8,128)} %pad_maximum_fusion.12), channel_id=1, source_target_pairs={{0,8},{8,16},{12,4},{16,24},{20,12},{28,20},{1,9},{9,17},{13,5},{1... | collective-permute-start | bytes 3047432 | tf_op jit(solution)/shard_map/ppermute | solution.py:329
  48.2 29.8 %collective-permute-start.6 = (f32[2048,128]{1,0:T(8,128)}, f32[2048,128]{1,0:T(8,128)S(1)}, u32[]{:S(2)}, u32[]{:S(2)}) collective-permute-start(f32[2048,128]{1,0:T(8,128)} %pad_maximum_fusion.10), channel_id=1, source_target_pairs={{0,4},{4,0},{8,12},{12,8},{16,20},{20,16},{24,28},{28,24},{1,5},{5... | collective-permute-start | bytes 3145736 | tf_op jit(solution)/shard_map/ppermute | solution.py:319
  48.3 34.5 %collective-permute-start.7 = (f32[1536,128]{1,0:T(8,128)}, f32[1536,128]{1,0:T(8,128)}, u32[]{:S(2)}, u32[]{:S(2)}) collective-permute-start(f32[1536,128]{1,0:T(8,128)} %pad_maximum_fusion.14), channel_id=1, source_target_pairs={{4,12},{8,0},{12,20},{16,8},{20,28},{24,16},{5,13},{9,1},{13,21},{... | collective-permute-start | bytes 2359304 | tf_op jit(solution)/shard_map/ppermute | solution.py:324
  49.7 16.5 %copy-start.27 = (f32[4,8,16,128]{3,2,1,0:T(8,128)}, f32[4,8,16,128]{3,2,1,0:T(8,128)S(1)}, u32[]{:S(2)}) copy-start(f32[4,8,16,128]{3,2,1,0:T(8,128)S(1)} %get-tuple-element.64) | copy-start | bytes 786436
  49.7 16.5 %copy-start.29 = (f32[4,8,16,128]{3,2,1,0:T(8,128)}, f32[4,8,16,128]{3,2,1,0:T(8,128)S(1)}, u32[]{:S(2)}) copy-start(f32[4,8,16,128]{3,2,1,0:T(8,128)S(1)} %get-tuple-element.65) | copy-start | bytes 786436
  69.5 35.0 %collective-permute-start.4 = (f32[3648,128]{1,0:T(8,128)}, f32[3648,128]{1,0:T(8,128)}, u32[]{:S(2)}, u32[]{:S(2)}) collective-permute-start(f32[3648,128]{1,0:T(8,128)} %pad_maximum_fusion.2), channel_id=1, source_target_pairs={{1,0},{2,1},{3,2},{5,4},{6,5},{7,6},{9,8},{10,9},{11,10},{13,12},{... | collective-permute-start | bytes 5603336 | tf_op jit(solution)/shard_map/ppermute | solution.py:339
  72.2 10.3 %copy-start.6 = (f32[8,16,8,128]{3,2,1,0:T(8,128)S(1)}, f32[8,16,8,128]{3,2,1,0:T(8,128)}, u32[]{:S(2)}) copy-start(f32[8,16,8,128]{3,2,1,0:T(8,128)} %copy-done.4) | copy-start | bytes 1572868
  72.2 10.3 %copy-start.9 = (f32[8,16,8,128]{3,2,1,0:T(8,128)S(1)}, f32[8,16,8,128]{3,2,1,0:T(8,128)}, u32[]{:S(2)}) copy-start(f32[8,16,8,128]{3,2,1,0:T(8,128)} %copy-done.7) | copy-start | bytes 1572868
  72.2 33.4 %collective-permute-start.3 = (f32[3648,128]{1,0:T(8,128)}, f32[3648,128]{1,0:T(8,128)}, u32[]{:S(2)}, u32[]{:S(2)}) collective-permute-start(f32[3648,128]{1,0:T(8,128)} %pad_maximum_fusion.1), channel_id=1, source_target_pairs={{0,1},{1,2},{2,3},{4,5},{5,6},{6,7},{8,9},{9,10},{10,11},{12,13},{... | collective-permute-start | bytes 5603336 | tf_op jit(solution)/shard_map/ppermute | solution.py:334
  78.1 21.3 %collective-permute-start.8 = (f32[1536,128]{1,0:T(8,128)S(1)}, f32[1536,128]{1,0:T(8,128)S(1)}, u32[]{:S(2)}, u32[]{:S(2)}) collective-permute-start(f32[1536,128]{1,0:T(8,128)S(1)} %bitcast.90), channel_id=1, source_target_pairs={{0,8},{8,16},{12,4},{16,24},{20,12},{28,20},{1,9},{9,17},{13,5},{1... | collective-permute-start | bytes 2359304 | tf_op jit(solution)/shard_map/ppermute | solution.py:329
  100.6 37.6 %collective-permute-start.9 = (f32[2688,128]{1,0:T(8,128)}, f32[2688,128]{1,0:T(8,128)S(1)}, u32[]{:S(2)}, u32[]{:S(2)}) collective-permute-start(f32[2688,128]{1,0:T(8,128)} %bitcast.40), channel_id=1, source_target_pairs={{0,1},{1,2},{2,3},{4,5},{5,6},{6,7},{8,9},{9,10},{10,11},{12,13},{... | collective-permute-start | bytes 4128776 | tf_op jit(solution)/shard_map/ppermute | solution.py:334
  103.2 34.9 %collective-permute-start.10 = (f32[2688,128]{1,0:T(8,128)}, f32[2688,128]{1,0:T(8,128)S(1)}, u32[]{:S(2)}, u32[]{:S(2)}) collective-permute-start(f32[2688,128]{1,0:T(8,128)} %bitcast.41), channel_id=1, source_target_pairs={{1,0},{2,1},{3,2},{5,4},{6,5},{7,6},{9,8},{10,9},{11,10},{13,12},{... | collective-permute-start | bytes 4128776 | tf_op jit(solution)/shard_map/ppermute | solution.py:339
  135.7 26.3 %collective-permute-start.5 = (f32[2,8,16,8,128]{4,3,2,1,0:T(8,128)S(1)}, f32[2,8,16,8,128]{4,3,2,1,0:T(8,128)S(1)}, u32[]{:S(2)}, u32[]{:S(2)}) collective-permute-start(f32[2,8,16,8,128]{4,3,2,1,0:T(8,128)S(1)} %get-tuple-element.27), channel_id=1, source_target_pairs={{0,4},{4,0},{8,12},{12,8},{16,20},{20,16},{24,28},{28,24},{1,5},{5... | collective-permute-start | bytes 3145736 | tf_op jit(solution)/shard_map/ppermute | solution.py:319
  161.9 25.0 %collective-permute-start.11 = (f32[2,8,16,8,128]{4,3,2,1,0:T(8,128)S(1)}, f32[2,8,16,8,128]{4,3,2,1,0:T(8,128)S(1)}, u32[]{:S(2)}, u32[]{:S(2)}) collective-permute-start(f32[2,8,16,8,128]{4,3,2,1,0:T(8,128)S(1)} %get-tuple-element.37), channel_id=1, source_target_pairs={{0,4},{4,0},{8,12},{12,8},{16,20},{20,16},{24,28},{28,24},{1,5},{5... | collective-permute-start | bytes 3145736 | tf_op jit(solution)/shard_map/ppermute | solution.py:319
  189.6 1.8 collective-permute-start.12
  191.4 4.0 %collective-permute-start.13 = (f32[64,64]{1,0:T(8,128)S(1)}, f32[64,64]{1,0:T(8,128)S(1)}, u32[]{:S(2)}, u32[]{:S(2)}) collective-permute-start(f32[64,64]{1,0:T(8,128)S(1)} %add.97), channel_id=1, source_target_pairs={{0,2},{1,3},{2,0},{3,1},{4,6},{5,7},{6,4},{7,5},{8,10},{9,11},{10,... | collective-permute-start | bytes 49160 | tf_op jit(solution)/shard_map/ppermute | solution.py:355
  195.4 3.9 %collective-permute-start.14 = (f32[64,64]{1,0:T(8,128)S(1)}, f32[64,64]{1,0:T(8,128)S(1)}, u32[]{:S(2)}, u32[]{:S(2)}) collective-permute-start(f32[64,64]{1,0:T(8,128)S(1)} %add.98), channel_id=1, source_target_pairs={{0,4},{4,0},{8,12},{12,8},{16,20},{20,16},{24,28},{28,24},{1,5},{5... | collective-permute-start | bytes 49160 | tf_op jit(solution)/shard_map/ppermute | solution.py:355
  199.3 3.9 %collective-permute-start.15 = (f32[64,64]{1,0:T(8,128)S(1)}, f32[64,64]{1,0:T(8,128)S(1)}, u32[]{:S(2)}, u32[]{:S(2)}) collective-permute-start(f32[64,64]{1,0:T(8,128)S(1)} %add.99), channel_id=1, source_target_pairs={{0,8},{4,12},{8,0},{12,4},{16,24},{20,28},{24,16},{28,20},{1,9},{5... | collective-permute-start | bytes 49160 | tf_op jit(solution)/shard_map/ppermute | solution.py:355
  203.2 4.8 %collective-permute-start.16 = (f32[64,64]{1,0:T(8,128)S(1)}, f32[64,64]{1,0:T(8,128)S(1)}, u32[]{:S(2)}, u32[]{:S(2)}) collective-permute-start(f32[64,64]{1,0:T(8,128)S(1)} %add.100.a_ref), channel_id=1, source_target_pairs={{0,16},{4,20},{8,24},{12,28},{16,0},{20,4},{24,8},{28,12},{1,17},{... | collective-permute-start | bytes 49160 | tf_op jit(solution)/shard_map/ppermute | solution.py:355
  (32 other events, 75.3 us)

commit v4 on v3

--- a/solution.py
+++ b/solution.py
@@ -16,7 +16,7 @@
 DEPTH = 6
 RING = DEPTH + 1
 EDGE = 8
-GROUPS = (2, 2)
+GROUPS = (1, 1, 1, 1)
 MIB = 1 << 20
 
 
@@ -82,37 +82,162 @@
     )(side, probes, probes, *maps)
 
 
+def fields_of(ref, *shape):
+    size = 1
+    for n in shape[:-1]:
+        size *= n
+    return ref.at[pl.ds(0, size)].reshape(shape)
+
+
+def maps_of(ref, skip, *shape):
+    size = 1
+    for n in shape[:-1]:
+        size *= n
+    return ref.at[pl.ds(skip, size)].reshape(shape)
+
+
+def map_parts(side, tiles, many, maps, recv, e1, e2):
+    planes, rows, depth = maps[0].shape
+    recv = maps_of(recv, tiles * planes * rows * many, len(maps), planes, rows, depth)
+    e1, e2 = (maps_of(e, tiles * DEPTH * rows * many, len(maps), RING, rows, depth) for e in (e1, e2))
+    top = RING + 2 * planes
+    return (
+        (maps, planes, RING + planes * side),
+        ([recv.at[i] for i in range(len(maps))], planes, RING + planes * (1 - side)),
+        ([e1.at[i] for i in range(len(maps))], RING, top * (1 - side)),
+        ([e2.at[i] for i in range(len(maps))], RING, top * side),
+    )
+
+
+def border_kernel(h_ref, own, recv, e1, e2, *refs):
+    maps, (low, high) = refs[1:-2], refs[-2:]
+    tiles, planes, rows, many, depth = own.shape
+    wide = 2 * planes + 2 * DEPTH
+    shape = (tiles, wide, DEPTH, many, depth)
+    low_f, high_f = fields_of(low, *shape), fields_of(high, *shape)
+    halo = (tiles, DEPTH, rows, many, depth)
+    at = 0
+    for piece in (own, fields_of(recv, *own.shape), fields_of(e1, *halo), fields_of(e2, *halo)):
+        for t in range(tiles):
+            for i in range(piece.shape[1]):
+                low_f[t, at + i] = piece[t, i, rows - DEPTH :]
+                high_f[t, at + i] = piece[t, i, :DEPTH]
+        at += piece.shape[1]
+    if maps:
+        shape = (len(maps), 2 * planes + 2 * RING, EDGE, depth)
+        skip = tiles * wide * DEPTH * many
+        low_m, high_m = maps_of(low, skip, *shape), maps_of(high, skip, *shape)
+        for pieces, count, place in map_parts(h_ref[0], tiles, many, maps, recv, e1, e2):
+            for i, piece in enumerate(pieces):
+                low_m[i, pl.ds(place, count)] = piece[:, rows - EDGE :]
+                high_m[i, pl.ds(place, count)] = piece[:, :EDGE]
+
+
+def border(side, own, recv, e1, e2, after, maps):
+    tiles, planes, rows, many, depth = own.shape
+    count = tiles * (2 * planes + 2 * DEPTH) * DEPTH * many + len(maps) * (2 * planes + 2 * RING) * EDGE
+    message = jax.ShapeDtypeStruct((count, depth), jnp.float32)
+    return pl.pallas_call(
+        border_kernel,
+        in_specs=[smem()] + [vmem()] * 4 + [pl.BlockSpec(memory_space=pl.ANY)] + [vmem()] * len(maps),
+        out_specs=[vmem(), vmem()],
+        out_shape=[message, message],
+        compiler_params=pltpu.CompilerParams(vmem_limit_bytes=12 * MIB),
+        cost_estimate=pl.CostEstimate(flops=0, bytes_accessed=2 * MIB, transcendentals=0),
+        name="border_rows",
+    )(side, own, recv, e1, e2, after, *maps)
+
+
+def coef_kernel(total_x, total_y, tiles, many, h_ref, at_ref, recv, e1, e2, ylo, yhi, *refs):
+    maps, (out, ext, root) = refs[:-3], refs[-3:]
+    wide_x, wide_y, depth = root.shape
+    rows = maps[0].shape[1]
+    skip = tiles * (wide_x - 2) * DEPTH * many
+    low, high = (maps_of(y, skip, len(maps), wide_x, EDGE, depth) for y in (ylo, yhi))
+    for pieces, count, place in map_parts(h_ref[0], tiles, many, maps, recv, e1, e2):
+        for i, piece in enumerate(pieces):
+            ext[i, pl.ds(place, count), EDGE : EDGE + rows] = piece[...]
+    for i in range(len(maps)):
+        ext[i, :, :EDGE] = low[i]
+        ext[i, :, EDGE + rows :] = high[i]
+    y = at_ref[1] + lax.broadcasted_iota(jnp.int32, (wide_y, depth), 0)
+    z = lax.broadcasted_iota(jnp.int32, (wide_y, depth), 1)
+    inside = (y >= 0) & (y < total_y)
+    root[0] = jnp.zeros((wide_y, depth), jnp.float32)
+    root[wide_x - 1] = jnp.zeros((wide_y, depth), jnp.float32)
+
+    def roots(x, carry):
+        k = ext[0, x]
+        beside = ext[0, x - 1] + ext[0, x + 1] + pltpu.roll(k, 1, 0) + pltpu.roll(k, wide_y - 1, 0)
+        beside = beside + jnp.where(z == 0, 0.0, pltpu.roll(k, 1, 1))
+        beside = beside + jnp.where(z == depth - 1, 0.0, pltpu.roll(k, depth - 1, 1))
+        diag = ext[1, x] + 0.5 * (6.0 * k + beside)
+        here = inside & (at_ref[0] + x >= 0) & (at_ref[0] + x < total_x)
+        root[x] = jnp.where(here, lax.rsqrt(jnp.where(here, diag, 1.0)), 0.0)
+        return carry
+
+    lax.fori_loop(1, wide_x - 1, roots, 0)
+
+    def plane(x, carry):
+        k, inv = ext[0, x], root[x]
+        half = 0.5 * OMEGA * inv
+        out[0, x] = half * root[x + 1] * (k + ext[0, x + 1])
+        out[1, x] = half * pltpu.roll(inv, wide_y - 1, 0) * (k + pltpu.roll(k, wide_y - 1, 0))
+        up = half * pltpu.roll(inv, depth - 1, 1) * (k + pltpu.roll(k, depth - 1, 1))
+        out[2, x] = jnp.where(z == depth - 1, 0.0, up)
+        out[3, x] = OMEGA * inv * ext[2, x]
+        out[4, x] = (OMEGA * A0) * inv * inv * ext[3, x]
+        out[5, x] = A0 * inv * ext[2, x]
+        return carry
+
+    lax.fori_loop(1, wide_x - 1, plane, 0)
+
+
+def coefficients(side, at, totals, own, recv, e1, e2, ylo, yhi, maps):
+    tiles, planes, rows, many, depth = own.shape
+    wide = (2 * planes + 2 * RING, rows + 2 * EDGE, depth)
+    return pl.pallas_call(
+        functools.partial(coef_kernel, *totals, tiles, many),
+        in_specs=[smem(), smem()] + [vmem()] * (5 + len(maps)),
+        out_specs=vmem(),
+        out_shape=jax.ShapeDtypeStruct((6,) + wide, jnp.float32),
+        scratch_shapes=[pltpu.VMEM((len(maps),) + wide, jnp.float32), pltpu.VMEM(wide, jnp.float32)],
+        compiler_params=pltpu.CompilerParams(vmem_limit_bytes=20 * MIB),
+        cost_estimate=pl.CostEstimate(flops=0, bytes_accessed=4 * MIB, transcendentals=0),
+        name="coefficients",
+    )(side, at, recv, e1, e2, ylo, yhi, *maps)
+
+
 def spread(coef, which, x, y, many):
     return coef[which, x, pl.ds(y, many, stride=0), :]
 
 
-def solve_kernel(h_ref, coef, own, recv, e1, e2, ylo, yhi, keep, back, r_s, a_s, b_s):
+def solve_kernel(h_ref, after, coef, own, recv, e1, e2, ylo, yhi, keep, back, r_s, a_s, b_s):
     tiles, planes, rows, many, depth = own.shape
     wide_x, wide_y = r_s.shape[1], r_s.shape[2]
     side = h_ref[0]
     top = DEPTH + 2 * planes
-
-    def fields(ref, n, m):
-        return ref.at[pl.ds(0, tiles * n * m * many)].reshape(tiles, n, m, many, depth)
-
-    ylo, yhi = fields(ylo, wide_x, DEPTH), fields(yhi, wide_x, DEPTH)
+    span = range(tiles)
+    border_shape = (tiles, wide_x, DEPTH, many, depth)
+    ylo, yhi = fields_of(ylo, *border_shape), fields_of(yhi, *border_shape)
+    halo = (tiles, DEPTH, rows, many, depth)
     parts = (
         (own, 0, planes, DEPTH + planes * side),
-        (fields(recv, planes, rows), planes, planes, DEPTH + planes * (1 - side)),
-        (fields(e1, DEPTH, rows), 2 * planes, DEPTH, top * (1 - side)),
-        (fields(e2, DEPTH, rows), 2 * planes + DEPTH, DEPTH, top * side),
+        (fields_of(recv, *own.shape), planes, planes, DEPTH + planes * (1 - side)),
+        (fields_of(e1, *halo), 2 * planes, DEPTH, top * (1 - side)),
+        (fields_of(e2, *halo), 2 * planes + DEPTH, DEPTH, top * side),
     )
 
     def row(which, x, y):
-        return spread(coef, which, x, y, many)
+        return spread(coef, which, x + RING - DEPTH, y + EDGE - DEPTH, many)
 
     for piece, role, count, place in parts:
 
         def fill(i, carry, piece=piece, role=role, place=place):
             x = place + i
             for y in range(wide_y):
-                scale = row(6, x, y)
-                for t in range(tiles):
+                scale = row(3, x, y)
+                for t in span:
                     if y < DEPTH:
                         value = ylo[t, role + i, y]
                     elif y < DEPTH + rows:
@@ -125,63 +250,71 @@
         lax.fori_loop(0, count, fill, 0)
 
     def stencil(src, r, x, low, scale, last=None):
-        span = range(tiles)
-        prev = [src[t, x, low - 1] for t in span]
-        here = [src[t, x, low] for t in span]
+        both = (x, x + 1)
+        prev = [[src[t, p, low - 1] for t in span] for p in both]
+        here = [[src[t, p, low] for t in span] for p in both]
+        cy_prev = [row(1, p, low - 1) for p in both]
         for y in range(low, wide_y - low):
-            after = [src[t, x, y + 1] for t in span]
-            c = [row(k, x, y) for k in range(6)]
-            end = None if last is None else row(last, x, y)
+            after = [[src[t, p, y + 1] for t in span] for p in both]
+            cx = [row(0, x + k, y) for k in (-1, 0, 1)]
+            cy = [row(1, p, y) for p in both]
             values = []
-            for t in span:
-                total = c[0] * src[t, x - 1, y] + c[1] * src[t, x + 1, y]
-                total = total + (c[2] * prev[t] + c[3] * after[t])
-                total = total + (c[4] * pltpu.roll(here[t], 1, 1) + c[5] * pltpu.roll(here[t], 127, 1))
-                value = r[t, x, y] + scale * total
-                values.append(value if end is None else value * end)
+            for k, p in enumerate(both):
+                cz = row(2, p, y)
+                end = None if last is None else row(last, p, y)
+                for t in span:
+                    f = here[k][t]
+                    before = src[t, x - 1, y] if k == 0 else here[0][t]
+                    beyond = here[1][t] if k == 0 else src[t, x + 2, y]
+                    total = cx[k] * before + cx[k + 1] * beyond
+                    total = total + (cy_prev[k] * prev[k][t] + cy[k] * after[k][t])
+                    total = total + (pltpu.roll(cz * f, 1, 1) + cz * pltpu.roll(f, depth - 1, 1))
+                    value = r[t, p, y] + scale * total
+                    values.append((t, k, value if end is None else value * end))
             yield y, values
-            prev, here = here, after
+            prev, here, cy_prev = here, after, cy
 
     def sweep(src, dst, r, low, scale, last=None):
-        def plane(x, carry):
+        def pair(i, carry):
+            x = low + 2 * i
             for y, values in stencil(src, r, x, low, scale, last):
-                for t, value in enumerate(values):
-                    dst[t, x, y] = value
+                for t, k, value in values:
+                    dst[t, x + k, y] = value
             return carry
 
-        lax.fori_loop(low, wide_x - low, plane, 0)
+        lax.fori_loop(0, (wide_x - 2 * low) // 2, pair, 0)
 
     sweep(r_s, a_s, r_s, 1, A3 / A2)
     sweep(a_s, b_s, r_s, 2, A2 / A1)
-    sweep(b_s, a_s, r_s, 3, A1 / A0, last=7)
+    sweep(b_s, a_s, r_s, 3, A1 / A0, last=4)
     sweep(a_s, b_s, a_s, 4, A3 / A2)
     sweep(b_s, r_s, a_s, 5, A2 / A1)
     for target, place in ((back, parts[1][3]), (keep, parts[0][3])):
 
         def out(i, carry, target=target, place=place):
-            for y, values in stencil(r_s, a_s, place + i, DEPTH, A1 / A0, last=8):
-                for t, value in enumerate(values):
-                    target[t, i, y - DEPTH] = value
+            for y, values in stencil(r_s, a_s, place + 2 * i, DEPTH, A1 / A0, last=5):
+                for t, k, value in values:
+                    target[t, 2 * i + k, y - DEPTH] = value
             return carry
 
-        lax.fori_loop(0, planes, out, 0)
-
-
-def solve(side, coef, own, *messages):
-    tiles, _, _, many, depth = own.shape
-    wide_x, wide_y = coef.shape[1:3]
-    field = pltpu.VMEM((tiles, wide_x, wide_y, many, depth), jnp.float32)
-    cells = tiles * wide_x * wide_y * many * depth
+        lax.fori_loop(0, planes // 2, out, 0)
+
+
+def solve(side, after, coef, own, *messages):
+    tiles, planes, rows, many, depth = own.shape
+    wide = (2 * planes + 2 * DEPTH, rows + 2 * DEPTH)
+    field = pltpu.VMEM((tiles,) + wide + (many, depth), jnp.float32)
+    cells = tiles * wide[0] * wide[1] * many * depth
     return pl.pallas_call(
         solve_kernel,
-        in_specs=[smem()] + [vmem()] * 7,
+        in_specs=[smem(), pl.BlockSpec(memory_space=pl.ANY)] + [vmem()] * 7,
         out_specs=[vmem(), vmem()],
         out_shape=[jax.ShapeDtypeStruct(own.shape, jnp.float32)] * 2,
         scratch_shapes=[field, field, field],
-        compiler_params=pltpu.CompilerParams(vmem_limit_bytes=(14 + 14 * tiles) * MIB),
+        compiler_params=pltpu.CompilerParams(vmem_limit_bytes=(6 + 17 * tiles) * MIB),
         cost_estimate=pl.CostEstimate(flops=60 * cells, bytes_accessed=12 * MIB, transcendentals=0),
         name="both_solves",
-    )(side, coef, own, *messages)
+    )(side, after, coef, own, *messages)
 
 
 def stacked(side, tiles, rows):
@@ -356,66 +489,36 @@
     return value, other
 
 
-def coefficients(side, ext, planes, rows):
-    cut = EDGE - DEPTH
-    k, absorb, sense, weight = ext
-    depth = k.shape[2]
-
-    def shifted(value, dx, dy):
-        return value[1 + dx : value.shape[0] - 1 + dx, cut + dy : value.shape[1] - cut + dy]
-
-    mid = shifted(k, 0, 0)
-    faces = [0.5 * (mid + shifted(k, *d)) for d in ((-1, 0), (1, 0), (0, -1), (0, 1))]
-    zpad = jnp.pad(mid, ((0, 0), (0, 0), (1, 1)))
-    z_low = 0.5 * (mid + zpad[:, :, :-2])
-    z_high = 0.5 * (mid + zpad[:, :, 2:])
-    diag = shifted(absorb, 0, 0) + sum(faces) + z_low + z_high
-
-    def inside(axis, start, total):
-        index = start - DEPTH + lax.broadcasted_iota(jnp.int32, diag.shape, axis)
-        return (index >= 0) & (index < total)
-
-    gx, gy = lax.axis_index("gx"), lax.axis_index("gy")
-    here = inside(0, (gx - side) * planes, planes * lax.axis_size("gx"))
-    here = here & inside(1, gy * rows, rows * lax.axis_size("gy"))
-    inv = jnp.where(here, OMEGA / jnp.where(here, diag, 1.0), 0.0)
-    z = lax.broadcasted_iota(jnp.int32, diag.shape, 2)
-    z_low = jnp.where(z == 0, 0.0, z_low)
-    z_high = jnp.where(z == depth - 1, 0.0, z_high)
-    sense, weight = shifted(sense, 0, 0), shifted(weight, 0, 0)
-    return jnp.stack([f * inv for f in faces] + [z_low * inv, z_high * inv, sense * inv, A0 * weight * inv, A0 * sense])
-
-
 def rows_of(*values):
     parts = [v.reshape(-1, v.shape[-1]) for v in values]
     return parts[0] if len(parts) == 1 else jnp.concatenate(parts, axis=0)
 
 
-def fields_of(flat, *shape):
-    size = 1
-    for n in shape[:-1]:
-        size *= n
-    return flat[:size].reshape(shape)
-
-
-def maps_of(flat, skip, *shape):
-    return flat[skip:].reshape(shape)
+def inner_rows(side, recv, size, planes, rows, maps):
+    depth = recv.shape[-1]
+    cells = planes * rows
+    fields = recv[: size * cells * 8].reshape(size, planes, rows * 8, depth)
+    out = [lax.dynamic_slice_in_dim(fields, (1 - side) * (planes - DEPTH), DEPTH, 1)]
+    if maps:
+        extra = recv[size * cells * 8 :].reshape(len(maps), planes, rows, depth)
+        out.append(lax.dynamic_slice_in_dim(extra, (1 - side) * (planes - RING), RING, 1))
+    return rows_of(*out)
 
 
 def body(probes, permeability, absorption, sensitivity, observe_weight):
     count, planes, rows, depth = probes.shape
-    cells = planes * lax.axis_size("gx") * rows * lax.axis_size("gy") * depth
-    side = lax.axis_index("gx") % 2
-    lower = side == 0
+    totals = (planes * lax.axis_size("gx"), rows * lax.axis_size("gy"))
+    gx, gy = lax.axis_index("gx"), lax.axis_index("gy")
+    side = gx % 2
     flag = side.reshape(1).astype(jnp.int32)
+    at = jnp.stack([(gx - side) * planes - RING, gy * rows - EDGE]).astype(jnp.int32)
     maps = (permeability, absorption, sensitivity, observe_weight)
-    tall = 2 * planes + 2 * DEPTH
     assert 16 * sum(GROUPS) == count
 
-    groups = []
+    groups, backs = [], []
     coef = turn = None
     tile = 0
-    for size in GROUPS:
+    for number, size in enumerate(GROUPS):
         mine = maps if tile == 0 else ()
         owns, sends, edges = zip(*[prep(flag, probes, tile + t, mine if t == size - 1 else ()) for t in range(size)])
         tile += size
@@ -425,39 +528,17 @@
         recv = swap(send)
         e1 = outward(edge)
         turn = recv
-        block, halo = (size, planes, rows, 8, depth), (size, DEPTH, rows, 8, depth)
-        recv_f = fields_of(recv, *block)
-        inner = [lax.dynamic_slice_in_dim(recv_f, (1 - side) * (planes - DEPTH), DEPTH, 1)]
+        e2 = inward(inner_rows(side, recv, size, planes, rows, mine))
+        after = backs[number - 2] if number >= 2 else own
+        low, high = border(flag, own, recv, e1, e2, after, mine)
+        ylo, yhi = above(low), below(high)
         if mine:
-            recv_m = maps_of(recv, size * planes * rows * 8, len(maps), planes, rows, depth)
-            inner.append(lax.dynamic_slice_in_dim(recv_m, (1 - side) * (planes - RING), RING, 1))
-        e2 = inward(rows_of(*inner))
-        whole = (own, recv_f, fields_of(e1, *halo), fields_of(e2, *halo))
-        low = [jnp.concatenate([p[:, :, rows - DEPTH :] for p in whole], axis=1)]
-        high = [jnp.concatenate([p[:, :, :DEPTH] for p in whole], axis=1)]
-        if mine:
-            own_m = jnp.stack(maps)
-            skip = size * DEPTH * rows * 8
-            e1_m, e2_m = (maps_of(e, skip, len(maps), RING, rows, depth) for e in (e1, e2))
-            wide = jnp.concatenate(
-                [
-                    jnp.where(lower, e2_m, e1_m),
-                    jnp.where(lower, own_m, recv_m),
-                    jnp.where(lower, recv_m, own_m),
-                    jnp.where(lower, e1_m, e2_m),
-                ],
-                axis=1,
-            )
-            low.append(wide[:, :, rows - EDGE :])
-            high.append(wide[:, :, :EDGE])
-        ylo, yhi = above(rows_of(*low)), below(rows_of(*high))
-        if mine:
-            skip = size * tall * DEPTH * 8
-            ends = [maps_of(y, skip, len(maps), tall + 2, EDGE, depth) for y in (ylo, yhi)]
-            coef = coefficients(side, jnp.concatenate([ends[0], wide, ends[1]], axis=2), planes, rows)
-        keep, back = solve(flag, coef, own, recv, e1, e2, ylo, yhi)
+            coef = coefficients(flag, at, totals, own, recv, e1, e2, ylo, yhi, maps)
+        after = groups[number - 2][1] if number >= 2 else own
+        keep, back = solve(flag, after, coef, own, recv, e1, e2, ylo, yhi)
+        backs.append(back)
         groups.append((keep, swap(back)))
-    a, b = summed(gram_of(flag, groups, cells))
+    a, b = summed(gram_of(flag, groups, totals[0] * totals[1] * depth))
     q, r = basis(flag, a, b, groups)
     return (q, r)
 

time: 219 us -> 210 us (0.959)
  waiting for transfers between devices: 84 us -> 51.7 us
  starting transfers between devices: 32.5 us -> 64.7 us
  other arithmetic: 18.5 us -> 0.14 us
  Pallas kernels: 65 us -> 80.3 us
  local copies, waits for them, and re-layouts: 17 us -> 10.9 us
    ppermute x2 -> x4, waiting for transfers between devices: 30.4 us -> 6.38 us  [inward(): lax.ppermute(value, 'gx', [(i, i + 2 - 4 * (i % 2)) for i in range(n) if...]
    pallas_call x2 -> x9, Pallas kernels: 48.7 us -> 62.9 us  [the longest x4 50.9 us: solve(): pl.pallas_call(solve_kernel, in_specs=[smem(), pl.BlockSpec(memory_space=...]
    ppermute x4 -> x8, waiting for transfers between devices: 42.9 us -> 31.1 us  [swap(): lax.ppermute(value, 'gx', [(i, i ^ 1) for i in range(lax.axis_size('gx'))])]
    concatenate x7 -> x1, other arithmetic: 10.3 us -> 0.04 us  [rows_of(): return parts[0] if len(parts) == 1 else jnp.concatenate(parts, axis=0)]
    ppermute x2 -> x4, starting transfers between devices: 8.25 us -> 17.2 us  [inward(): lax.ppermute(value, 'gx', [(i, i + 2 - 4 * (i % 2)) for i in range(n) if...]
    ppermute x4 -> x8, starting transfers between devices: 5.57 us -> 14.1 us  [swap(): lax.ppermute(value, 'gx', [(i, i ^ 1) for i in range(lax.axis_size('gx'))])]
    ppermute x2 -> x4, starting transfers between devices: 5.79 us -> 12.8 us  [above(): return lax.ppermute(value, 'gy', [(i, i + 1) for i in range(n - 1)])]
    ppermute x2 -> x4, waiting for transfers between devices: 0.01 us -> 5.73 us  [outward(): lax.ppermute(value, 'gx', [(i, i + 2 * (i % 2) * 2 - 2) for i in range(n)...]
  transfers between devices with their start and end apart: 17 -> 29, of which waited for: 9 -> 12; matrix products, arithmetic and copies ran while one was open for 10% -> 1% of each run, Pallas kernels for 23% -> 31%
where the time goes in v4:
time: 210 us; the launch traced here: 209 us
  Pallas kernels  80.3 us (38%)
  starting transfers between devices  64.7 us (31%)
  waiting for transfers between devices  51.7 us (25%)
  local copies, waits for them, and re-layouts  10.9 us (5%)
    pallas_call x4, Pallas kernels, solve(): pl.pallas_call(solve_kernel, in_specs=[smem(), pl.BlockSpec(memory_space=...  50.9 us
    ppermute x8, waiting for transfers between devices, swap(): lax.ppermute(value, 'gx', [(i, i ^ 1) for i in range(lax.axis_size('gx'))])  31.1 us
    ppermute x4, starting transfers between devices, inward(): lax.ppermute(value, 'gx', [(i, i + 2 - 4 * (i % 2)) for i in range(n) if...  17.2 us
    ppermute x8, starting transfers between devices, swap(): lax.ppermute(value, 'gx', [(i, i ^ 1) for i in range(lax.axis_size('gx'))])  14.1 us
    ppermute x4, starting transfers between devices, above(): return lax.ppermute(value, 'gy', [(i, i + 1) for i in range(n - 1)])  12.8 us
    pallas_call x1, Pallas kernels, basis(): pl.pallas_call(basis_kernel, grid=(planes,), in_specs=[smem(), full, full...  10.4 us
    ppermute x5, starting transfers between devices, summed(): other = lax.ppermute(value, axis, [(i, i ^ shift) for i in range(n)])  10.2 us
    unnamed x68, local copies, waits for them, and re-layouts  9.95 us
  transfers between devices with their start and end apart: 29, of which 12 were waited for; matrix products, arithmetic and copies ran while one was open for 1% of the time, Pallas kernels for 31%

profile of v4, /device:TPU:0, one launch (start us, length us, event | category | flops | bytes accessed | tf_op | source)
XLA Modules:
  0.0 209.0 jit_solution(6322455918778872829)
XLA Ops:
  7.6 2.9 %collective-permute-start = (f32[1536,128]{1,0:T(8,128)}, f32[1536,128]{1,0:T(8,128)S(1)}, u32[]{:S(2)}, u32[]{:S(2)}) collective-permute-start(f32[1536,128]{1,0:T(8,128)} %get-tuple-element.37), channel_id=1, source_target_pairs={{0,4},{4,0},{8,12},{12,8},{16,20},{20,16},{24,28},{28,24},{1,5},{5... | collective-permute-start | bytes 2359304 | tf_op jit(solution)/shard_map/ppermute | solution.py:452
  15.1 13.2 %collective-permute-done.recv = f32[1536,128]{1,0:T(8,128)S(1)} collective-permute-done((f32[1536,128]{1,0:T(8,128)}, f32[1536,128]{1,0:T(8,128)S(1)}, u32[]{:S(2)}, u32[]{:S(2)}) %collective-permute-start) | collective-permute-done | bytes 786464 | tf_op jit(solution)/shard_map/ppermute | solution.py:452
  30.2 3.7 %collective-permute-start.2 = (f32[1216,128]{1,0:T(8,128)S(1)}, f32[1216,128]{1,0:T(8,128)S(1)}, u32[]{:S(2)}, u32[]{:S(2)}) collective-permute-start(f32[1216,128]{1,0:T(8,128)S(1)} %pad_maximum_fusion), channel_id=1, source_target_pairs={{0,8},{8,16},{12,4},{16,24},{20,12},{28,20},{1,9},{9,17},{13,5},{1... | collective-permute-start | bytes 1867784 | tf_op jit(solution)/shard_map/ppermute | solution.py:462
  35.5 6.1 %collective-permute-done.6.recv = f32[1024,128]{1,0:T(8,128)S(1)} collective-permute-done((f32[1024,128]{1,0:T(8,128)}, f32[1024,128]{1,0:T(8,128)S(1)}, u32[]{:S(2)}, u32[]{:S(2)}) %collective-permute-start.6) | collective-permute-done | bytes 524320 | tf_op jit(solution)/shard_map/ppermute | solution.py:452
  43.0 3.0 %collective-permute-done.2.e2 = f32[1216,128]{1,0:T(8,128)S(1)} collective-permute-done((f32[1216,128]{1,0:T(8,128)S(1)}, f32[1216,128]{1,0:T(8,128)S(1)}, u32[]{:S(2)}, u32[]{:S(2)}) %collective-permute-start.2) | collective-permute-done | bytes 622624 | tf_op jit(solution)/shard_map/ppermute | solution.py:462
  46.0 2.9 %border_rows.4 = (f32[2304,128]{1,0:T(8,128)}, f32[2304,128]{1,0:T(8,128)}) custom-call(s32[1]{0:T(128)} %bitcast.h_ref, f32[1,8,16,8,128]{4,3,2,1,0:T(8,128)S(1)} %bitcast.17, f32[1536,128]{1,0:T(8,128)S(1)} %collective-permute-done.recv, f32[1216,128]{1,0:T(8,128)} %collective-permute-done.1.e1, f32[1216,128]{1,0:T(8,128)S(1)} %collective-permute-done.2.e2, ...), custom_call_target="tpu_custom_call" | custom-call | bytes 2097152 | tf_op jit(solution)/shard_map/border_rows/pallas_call | solution.py:140
  54.7 3.8 %collective-permute-start.18 = (f32[1024,128]{1,0:T(8,128)S(1)}, f32[1024,128]{1,0:T(8,128)S(1)}, u32[]{:S(2)}, u32[]{:S(2)}) collective-permute-start(f32[1024,128]{1,0:T(8,128)S(1)} %get-tuple-element.64), channel_id=1, source_target_pairs={{0,4},{4,0},{8,12},{12,8},{16,20},{20,16},{24,28},{28,24},{1,5},{5... | collective-permute-start | bytes 1572872 | tf_op jit(solution)/shard_map/ppermute | solution.py:452
  58.6 3.5 %collective-permute-start.8 = (f32[768,128]{1,0:T(8,128)S(1)}, f32[768,128]{1,0:T(8,128)S(1)}, u32[]{:S(2)}, u32[]{:S(2)}) collective-permute-start(f32[768,128]{1,0:T(8,128)S(1)} %bitcast.37), channel_id=1, source_target_pairs={{0,8},{8,16},{12,4},{16,24},{20,12},{28,20},{1,9},{9,17},{13,5},{1... | collective-permute-start | bytes 1179656 | tf_op jit(solution)/shard_map/ppermute | solution.py:462
  62.1 3.7 %collective-permute-done.7.e1 = f32[768,128]{1,0:T(8,128)S(1)} collective-permute-done((f32[768,128]{1,0:T(8,128)S(1)}, f32[768,128]{1,0:T(8,128)S(1)}, u32[]{:S(2)}, u32[]{:S(2)}) %collective-permute-start.7) | collective-permute-done | bytes 393248 | tf_op jit(solution)/shard_map/ppermute | solution.py:457
  67.8 3.4 %collective-permute-done.8.e2 = f32[768,128]{1,0:T(8,128)S(1)} collective-permute-done((f32[768,128]{1,0:T(8,128)S(1)}, f32[768,128]{1,0:T(8,128)S(1)}, u32[]{:S(2)}, u32[]{:S(2)}) %collective-permute-start.8) | collective-permute-done | bytes 393248 | tf_op jit(solution)/shard_map/ppermute | solution.py:462
  71.2 5.1 %collective-permute-start.14 = (f32[768,128]{1,0:T(8,128)}, f32[768,128]{1,0:T(8,128)}, u32[]{:S(2)}, u32[]{:S(2)}) collective-permute-start(f32[768,128]{1,0:T(8,128)} %bitcast.13), channel_id=1, source_target_pairs={{0,8},{8,16},{12,4},{16,24},{20,12},{28,20},{1,9},{9,17},{13,5},{1... | collective-permute-start | bytes 1179656 | tf_op jit(solution)/shard_map/ppermute | solution.py:462
  79.6 2.9 %collective-permute-start.9 = (f32[1344,128]{1,0:T(8,128)}, f32[1344,128]{1,0:T(8,128)}, u32[]{:S(2)}, u32[]{:S(2)}) collective-permute-start(f32[1344,128]{1,0:T(8,128)} %get-tuple-element.48), channel_id=1, source_target_pairs={{0,1},{1,2},{2,3},{4,5},{5,6},{6,7},{8,9},{9,10},{10,11},{12,13},{... | collective-permute-start | bytes 2064392 | tf_op jit(solution)/shard_map/ppermute | solution.py:467
  85.2 4.9 %collective-permute-start.20 = (f32[768,128]{1,0:T(8,128)S(1)}, f32[768,128]{1,0:T(8,128)S(1)}, u32[]{:S(2)}, u32[]{:S(2)}) collective-permute-start(f32[768,128]{1,0:T(8,128)S(1)} %bitcast.36), channel_id=1, source_target_pairs={{0,8},{8,16},{12,4},{16,24},{20,12},{28,20},{1,9},{9,17},{13,5},{1... | collective-permute-start | bytes 1179656 | tf_op jit(solution)/shard_map/ppermute | solution.py:462
  91.9 6.7 %coefficients.1.coef = f32[6,30,32,128]{3,2,1,0:T(8,128)S(1)} custom-call(s32[1]{0:T(128)} %bitcast.h_ref, s32[2]{0:T(128)S(1)} %pad_add_fusion.at_ref, f32[1536,128]{1,0:T(8,128)S(1)} %collective-permute-done.recv, f32[1216,128]{1,0:T(8,128)} %collective-permute-done.1.e1, f32[1216,128]{1,0:T(8,128)S(1)} %copy-done.5, ...), custom_call_target="tpu_custom_call" | custom-call | bytes 4194304 | tf_op jit(solution)/shard_map/coefficients/pallas_call | solution.py:199
  98.6 13.6 %both_solves.4 = (f32[1,8,16,8,128]{4,3,2,1,0:T(8,128)S(1)}, f32[1,8,16,8,128]{4,3,2,1,0:T(8,128)S(1)}) custom-call(s32[1]{0:T(128)} %bitcast.h_ref, f32[1,8,16,8,128]{4,3,2,1,0:T(8,128)S(1)} %bitcast.19, f32[6,30,32,128]{3,2,1,0:T(8,128)S(1)} %coefficients.1.coef, f32[1,8,16,8,128]{4,3,2,1,0:T(8,128)S(1)} %bitcast.20, ...), custom_call_target="tpu_custom_call" | custom-call | flops 48168960 | bytes 12582912 | tf_op jit(solution)/shard_map/both_solves/pallas_call | solution.py:308
  113.5 2.8 %collective-permute-start.15 = (f32[1344,128]{1,0:T(8,128)S(1)}, f32[1344,128]{1,0:T(8,128)S(1)}, u32[]{:S(2)}, u32[]{:S(2)}) collective-permute-start(f32[1344,128]{1,0:T(8,128)S(1)} %get-tuple-element.57), channel_id=1, source_target_pairs={{0,1},{1,2},{2,3},{4,5},{5,6},{6,7},{8,9},{9,10},{10,11},{12,13},{... | collective-permute-start | bytes 2064392 | tf_op jit(solution)/shard_map/ppermute | solution.py:467
  117.8 13.0 %both_solves.5 = (f32[1,8,16,8,128]{4,3,2,1,0:T(8,128)S(1)}, f32[1,8,16,8,128]{4,3,2,1,0:T(8,128)S(1)}) custom-call(s32[1]{0:T(128)} %bitcast.h_ref, f32[1,8,16,8,128]{4,3,2,1,0:T(8,128)S(1)} %bitcast.23, f32[6,30,32,128]{3,2,1,0:T(8,128)S(1)} %coefficients.1.coef, f32[1,8,16,8,128]{4,3,2,1,0:T(8,128)S(1)} %bitcast.24, f32[1024,128]{1,0:T(8,128)S(1)} %copy-done.11, ...), custom_call_target="tpu_custom_call" | custom-call | flops 48168960 | bytes 12582912 | tf_op jit(solution)/shard_map/both_solves/pallas_call | solution.py:308
  130.9 4.8 %collective-permute-start.21 = (f32[1344,128]{1,0:T(8,128)S(1)}, f32[1344,128]{1,0:T(8,128)S(1)}, u32[]{:S(2)}, u32[]{:S(2)}) collective-permute-start(f32[1344,128]{1,0:T(8,128)S(1)} %get-tuple-element.66), channel_id=1, source_target_pairs={{0,1},{1,2},{2,3},{4,5},{5,6},{6,7},{8,9},{9,10},{10,11},{12,13},{... | collective-permute-start | bytes 2064392 | tf_op jit(solution)/shard_map/ppermute | solution.py:467
  139.1 12.7 %both_solves.6 = (f32[1,8,16,8,128]{4,3,2,1,0:T(8,128)S(1)}, f32[1,8,16,8,128]{4,3,2,1,0:T(8,128)S(1)}) custom-call(s32[1]{0:T(128)} %bitcast.h_ref, f32[1,8,16,8,128]{4,3,2,1,0:T(8,128)S(1)} %collective-permute-done.5.after.refs_1_, f32[6,30,32,128]{3,2,1,0:T(8,128)S(1)} %coefficients.1.coef, f32[1,8,16,8,128]{4,3,2,1,0:T(8,128)S(1)} %bitcast.29, ...), custom_call_target="tpu_custom_call" | custom-call | flops 48168960 | bytes 12582912 | tf_op jit(solution)/shard_map/both_solves/pallas_call | solution.py:308
  151.9 11.7 %both_solves.7 = (f32[1,8,16,8,128]{4,3,2,1,0:T(8,128)S(1)}, f32[1,8,16,8,128]{4,3,2,1,0:T(8,128)S(1)}) custom-call(s32[1]{0:T(128)} %bitcast.h_ref, f32[1,8,16,8,128]{4,3,2,1,0:T(8,128)S(1)} %collective-permute-done.11.after.refs_3_, f32[6,30,32,128]{3,2,1,0:T(8,128)S(1)} %coefficients.1.coef, f32[1,8,16,8,128]{4,3,2,1,0:T(8,128)S(1)} %bitcast.31, ...), custom_call_target="tpu_custom_call" | custom-call | flops 48168960 | bytes 12582912 | tf_op jit(solution)/shard_map/both_solves/pallas_call | solution.py:308
  165.6 11.7 %collective-permute-done.23.refs_7_ = f32[1,8,16,8,128]{4,3,2,1,0:T(8,128)S(1)} collective-permute-done((f32[1,8,16,8,128]{4,3,2,1,0:T(8,128)S(1)}, f32[1,8,16,8,128]{4,3,2,1,0:T(8,128)S(1)}, u32[]{:S(2)}, u32[]{:S(2)}) %collective-permute-start.23) | collective-permute-done | bytes 524320 | tf_op jit(solution)/shard_map/ppermute | solution.py:452
  177.3 2.6 %gram.1 = f32[64,64]{1,0:T(8,128)S(1)} custom-call(s32[1]{0:T(128)} %bitcast.h_ref, f32[1,8,16,8,128]{4,3,2,1,0:T(8,128)S(1)} %get-tuple-element.41.refs_0_, f32[1,8,16,8,128]{4,3,2,1,0:T(8,128)S(1)} %collective-permute-done.5.after.refs_1_, f32[1,8,16,8,128]{4,3,2,1,0:T(8,128)S(1)} %get-tuple-element.50.refs_2_, ...), custom_call_target="tpu_custom_call" | custom-call | bytes 6291456 | tf_op jit(solution)/shard_map/gram/pallas_call | solution.py:370
  193.7 3.1 %collective-permute-start.28 = (f32[64,64]{1,0:T(8,128)S(1)}, f32[64,64]{1,0:T(8,128)S(1)}, u32[]{:S(2)}, u32[]{:S(2)}) collective-permute-start(f32[64,64]{1,0:T(8,128)S(1)} %add.34.a_ref), channel_id=1, source_target_pairs={{0,16},{4,20},{8,24},{12,28},{16,0},{20,4},{24,8},{28,12},{1,17},{... | collective-permute-start | bytes 49160 | tf_op jit(solution)/shard_map/ppermute | solution.py:488
  198.7 10.4 %basis.1 = (f32[64,8,16,128]{3,2,1,0:T(8,128)}, f32[64,64]{1,0:T(8,128)}) custom-call(s32[1]{0:T(128)} %bitcast.h_ref, f32[64,64]{1,0:T(8,128)S(1)} %add.34.a_ref, f32[64,64]{1,0:T(8,128)S(1)} %collective-permute-done.28.b_ref, f32[1,8,16,8,128]{4,3,2,1,0:T(8,128)S(1)} %get-tuple-element.41.refs_0_, ...), custom_call_target="tpu_custom_call" | custom-call | bytes 8388608 | tf_op jit(solution)/shard_map/basis/pallas_call | solution.py:435
  (130 shorter events, 55.8 us)
Async XLA Ops:
  7.6 20.7 %collective-permute-start = (f32[1536,128]{1,0:T(8,128)}, f32[1536,128]{1,0:T(8,128)S(1)}, u32[]{:S(2)}, u32[]{:S(2)}) collective-permute-start(f32[1536,128]{1,0:T(8,128)} %get-tuple-element.37), channel_id=1, source_target_pairs={{0,4},{4,0},{8,12},{12,8},{16,20},{20,16},{24,28},{28,24},{1,5},{5... | collective-permute-start | bytes 2359304 | tf_op jit(solution)/shard_map/ppermute | solution.py:452
  10.5 32.5 %collective-permute-start.1 = (f32[1216,128]{1,0:T(8,128)}, f32[1216,128]{1,0:T(8,128)}, u32[]{:S(2)}, u32[]{:S(2)}) collective-permute-start(f32[1216,128]{1,0:T(8,128)} %get-tuple-element.38), channel_id=1, source_target_pairs={{4,12},{8,0},{12,20},{16,8},{20,28},{24,16},{5,13},{9,1},{13,21},{... | collective-permute-start | bytes 1867784 | tf_op jit(solution)/shard_map/ppermute | solution.py:457
  28.3 13.4 %collective-permute-start.6 = (f32[1024,128]{1,0:T(8,128)}, f32[1024,128]{1,0:T(8,128)S(1)}, u32[]{:S(2)}, u32[]{:S(2)}) collective-permute-start(f32[1024,128]{1,0:T(8,128)} %copy-done.30), channel_id=1, source_target_pairs={{0,4},{4,0},{8,12},{12,8},{16,20},{20,16},{24,28},{28,24},{1,5},{5... | collective-permute-start | bytes 1572872 | tf_op jit(solution)/shard_map/ppermute | solution.py:452
  30.2 15.7 %collective-permute-start.2 = (f32[1216,128]{1,0:T(8,128)S(1)}, f32[1216,128]{1,0:T(8,128)S(1)}, u32[]{:S(2)}, u32[]{:S(2)}) collective-permute-start(f32[1216,128]{1,0:T(8,128)S(1)} %pad_maximum_fusion), channel_id=1, source_target_pairs={{0,8},{8,16},{12,4},{16,24},{20,12},{28,20},{1,9},{9,17},{13,5},{1... | collective-permute-start | bytes 1867784 | tf_op jit(solution)/shard_map/ppermute | solution.py:462
  41.7 13.0 %collective-permute-start.12 = (f32[1024,128]{1,0:T(8,128)S(1)}, f32[1024,128]{1,0:T(8,128)S(1)}, u32[]{:S(2)}, u32[]{:S(2)}) collective-permute-start(f32[1024,128]{1,0:T(8,128)S(1)} %get-tuple-element.55), channel_id=1, source_target_pairs={{0,4},{4,0},{8,12},{12,8},{16,20},{20,16},{24,28},{28,24},{1,5},{5... | collective-permute-start | bytes 1572872 | tf_op jit(solution)/shard_map/ppermute | solution.py:452
  48.9 35.0 %collective-permute-start.3 = (f32[2304,128]{1,0:T(8,128)}, f32[2304,128]{1,0:T(8,128)}, u32[]{:S(2)}, u32[]{:S(2)}) collective-permute-start(f32[2304,128]{1,0:T(8,128)} %get-tuple-element.39), channel_id=1, source_target_pairs={{0,1},{1,2},{2,3},{4,5},{5,6},{6,7},{8,9},{9,10},{10,11},{12,13},{... | collective-permute-start | bytes 3538952 | tf_op jit(solution)/shard_map/ppermute | solution.py:467
  51.2 33.9 %collective-permute-start.4 = (f32[2304,128]{1,0:T(8,128)}, f32[2304,128]{1,0:T(8,128)}, u32[]{:S(2)}, u32[]{:S(2)}) collective-permute-start(f32[2304,128]{1,0:T(8,128)} %get-tuple-element.40), channel_id=1, source_target_pairs={{1,0},{2,1},{3,2},{5,4},{6,5},{7,6},{9,8},{10,9},{11,10},{13,12},{... | collective-permute-start | bytes 3538952 | tf_op jit(solution)/shard_map/ppermute | solution.py:472
  52.5 13.2 %collective-permute-start.7 = (f32[768,128]{1,0:T(8,128)S(1)}, f32[768,128]{1,0:T(8,128)S(1)}, u32[]{:S(2)}, u32[]{:S(2)}) collective-permute-start(f32[768,128]{1,0:T(8,128)S(1)} %copy-done.33), channel_id=1, source_target_pairs={{4,12},{8,0},{12,20},{16,8},{20,28},{24,16},{5,13},{9,1},{13,21},{... | collective-permute-start | bytes 1179656 | tf_op jit(solution)/shard_map/ppermute | solution.py:457
  54.7 27.8 %collective-permute-start.18 = (f32[1024,128]{1,0:T(8,128)S(1)}, f32[1024,128]{1,0:T(8,128)S(1)}, u32[]{:S(2)}, u32[]{:S(2)}) collective-permute-start(f32[1024,128]{1,0:T(8,128)S(1)} %get-tuple-element.64), channel_id=1, source_target_pairs={{0,4},{4,0},{8,12},{12,8},{16,20},{20,16},{24,28},{28,24},{1,5},{5... | collective-permute-start | bytes 1572872 | tf_op jit(solution)/shard_map/ppermute | solution.py:452
  58.6 12.6 %collective-permute-start.8 = (f32[768,128]{1,0:T(8,128)S(1)}, f32[768,128]{1,0:T(8,128)S(1)}, u32[]{:S(2)}, u32[]{:S(2)}) collective-permute-start(f32[768,128]{1,0:T(8,128)S(1)} %bitcast.37), channel_id=1, source_target_pairs={{0,8},{8,16},{12,4},{16,24},{20,12},{28,20},{1,9},{9,17},{13,5},{1... | collective-permute-start | bytes 1179656 | tf_op jit(solution)/shard_map/ppermute | solution.py:462
  65.7 13.9 %collective-permute-start.13 = (f32[768,128]{1,0:T(8,128)S(1)}, f32[768,128]{1,0:T(8,128)S(1)}, u32[]{:S(2)}, u32[]{:S(2)}) collective-permute-start(f32[768,128]{1,0:T(8,128)S(1)} %get-tuple-element.56), channel_id=1, source_target_pairs={{4,12},{8,0},{12,20},{16,8},{20,28},{24,16},{5,13},{9,1},{13,21},{... | collective-permute-start | bytes 1179656 | tf_op jit(solution)/shard_map/ppermute | solution.py:457
  71.2 41.0 %collective-permute-start.14 = (f32[768,128]{1,0:T(8,128)}, f32[768,128]{1,0:T(8,128)}, u32[]{:S(2)}, u32[]{:S(2)}) collective-permute-start(f32[768,128]{1,0:T(8,128)} %bitcast.13), channel_id=1, source_target_pairs={{0,8},{8,16},{12,4},{16,24},{20,12},{28,20},{1,9},{9,17},{13,5},{1... | collective-permute-start | bytes 1179656 | tf_op jit(solution)/shard_map/ppermute | solution.py:462
  79.6 33.9 %collective-permute-start.9 = (f32[1344,128]{1,0:T(8,128)}, f32[1344,128]{1,0:T(8,128)}, u32[]{:S(2)}, u32[]{:S(2)}) collective-permute-start(f32[1344,128]{1,0:T(8,128)} %get-tuple-element.48), channel_id=1, source_target_pairs={{0,1},{1,2},{2,3},{4,5},{5,6},{6,7},{8,9},{9,10},{10,11},{12,13},{... | collective-permute-start | bytes 2064392 | tf_op jit(solution)/shard_map/ppermute | solution.py:467
  82.5 33.8 %collective-permute-start.10 = (f32[1344,128]{1,0:T(8,128)}, f32[1344,128]{1,0:T(8,128)}, u32[]{:S(2)}, u32[]{:S(2)}) collective-permute-start(f32[1344,128]{1,0:T(8,128)} %get-tuple-element.49), channel_id=1, source_target_pairs={{1,0},{2,1},{3,2},{5,4},{6,5},{7,6},{9,8},{10,9},{11,10},{13,12},{... | collective-permute-start | bytes 2064392 | tf_op jit(solution)/shard_map/ppermute | solution.py:472
  83.9 46.9 %collective-permute-start.19 = (f32[768,128]{1,0:T(8,128)}, f32[768,128]{1,0:T(8,128)S(1)}, u32[]{:S(2)}, u32[]{:S(2)}) collective-permute-start(f32[768,128]{1,0:T(8,128)} %copy-done.31), channel_id=1, source_target_pairs={{4,12},{8,0},{12,20},{16,8},{20,28},{24,16},{5,13},{9,1},{13,21},{... | collective-permute-start | bytes 1179656 | tf_op jit(solution)/shard_map/ppermute | solution.py:457
  85.2 45.6 %collective-permute-start.20 = (f32[768,128]{1,0:T(8,128)S(1)}, f32[768,128]{1,0:T(8,128)S(1)}, u32[]{:S(2)}, u32[]{:S(2)}) collective-permute-start(f32[768,128]{1,0:T(8,128)S(1)} %bitcast.36), channel_id=1, source_target_pairs={{0,8},{8,16},{12,4},{16,24},{20,12},{28,20},{1,9},{9,17},{13,5},{1... | collective-permute-start | bytes 1179656 | tf_op jit(solution)/shard_map/ppermute | solution.py:462
  112.2 24.8 %collective-permute-start.5 = (f32[1,8,16,8,128]{4,3,2,1,0:T(8,128)S(1)}, f32[1,8,16,8,128]{4,3,2,1,0:T(8,128)S(1)}, u32[]{:S(2)}, u32[]{:S(2)}) collective-permute-start(f32[1,8,16,8,128]{4,3,2,1,0:T(8,128)S(1)} %get-tuple-element.42.refs_0_), channel_id=1, source_target_pairs={{0,4},{4,0},{8,12},{12,8},{16,20},{20,16},{24,28},{28,24},{1,5},{5... | collective-permute-start | bytes 1572872 | tf_op jit(solution)/shard_map/ppermute | solution.py:452
  113.5 25.6 %collective-permute-start.15 = (f32[1344,128]{1,0:T(8,128)S(1)}, f32[1344,128]{1,0:T(8,128)S(1)}, u32[]{:S(2)}, u32[]{:S(2)}) collective-permute-start(f32[1344,128]{1,0:T(8,128)S(1)} %get-tuple-element.57), channel_id=1, source_target_pairs={{0,1},{1,2},{2,3},{4,5},{5,6},{6,7},{8,9},{9,10},{10,11},{12,13},{... | collective-permute-start | bytes 2064392 | tf_op jit(solution)/shard_map/ppermute | solution.py:467
  116.3 22.7 %collective-permute-start.16 = (f32[1344,128]{1,0:T(8,128)S(1)}, f32[1344,128]{1,0:T(8,128)S(1)}, u32[]{:S(2)}, u32[]{:S(2)}) collective-permute-start(f32[1344,128]{1,0:T(8,128)S(1)} %get-tuple-element.58), channel_id=1, source_target_pairs={{1,0},{2,1},{3,2},{5,4},{6,5},{7,6},{9,8},{10,9},{11,10},{13,12},{... | collective-permute-start | bytes 2064392 | tf_op jit(solution)/shard_map/ppermute | solution.py:472
  130.9 20.9 %collective-permute-start.21 = (f32[1344,128]{1,0:T(8,128)S(1)}, f32[1344,128]{1,0:T(8,128)S(1)}, u32[]{:S(2)}, u32[]{:S(2)}) collective-permute-start(f32[1344,128]{1,0:T(8,128)S(1)} %get-tuple-element.66), channel_id=1, source_target_pairs={{0,1},{1,2},{2,3},{4,5},{5,6},{6,7},{8,9},{9,10},{10,11},{12,13},{... | collective-permute-start | bytes 2064392 | tf_op jit(solution)/shard_map/ppermute | solution.py:467
  135.7 16.1 %collective-permute-start.22 = (f32[1344,128]{1,0:T(8,128)S(1)}, f32[1344,128]{1,0:T(8,128)S(1)}, u32[]{:S(2)}, u32[]{:S(2)}) collective-permute-start(f32[1344,128]{1,0:T(8,128)S(1)} %get-tuple-element.67), channel_id=1, source_target_pairs={{1,0},{2,1},{3,2},{5,4},{6,5},{7,6},{9,8},{10,9},{11,10},{13,12},{... | collective-permute-start | bytes 2064392 | tf_op jit(solution)/shard_map/ppermute | solution.py:472
  137.0 14.8 %collective-permute-start.11 = (f32[1,8,16,8,128]{4,3,2,1,0:T(8,128)S(1)}, f32[1,8,16,8,128]{4,3,2,1,0:T(8,128)S(1)}, u32[]{:S(2)}, u32[]{:S(2)}) collective-permute-start(f32[1,8,16,8,128]{4,3,2,1,0:T(8,128)S(1)} %get-tuple-element.51.refs_0_), channel_id=1, source_target_pairs={{0,4},{4,0},{8,12},{12,8},{16,20},{20,16},{24,28},{28,24},{1,5},{5... | collective-permute-start | bytes 1572872 | tf_op jit(solution)/shard_map/ppermute | solution.py:452
  151.7 13.9 %collective-permute-start.17 = (f32[1,8,16,8,128]{4,3,2,1,0:T(8,128)S(1)}, f32[1,8,16,8,128]{4,3,2,1,0:T(8,128)S(1)}, u32[]{:S(2)}, u32[]{:S(2)}) collective-permute-start(f32[1,8,16,8,128]{4,3,2,1,0:T(8,128)S(1)} %get-tuple-element.60), channel_id=1, source_target_pairs={{0,4},{4,0},{8,12},{12,8},{16,20},{20,16},{24,28},{28,24},{1,5},{5... | collective-permute-start | bytes 1572872 | tf_op jit(solution)/shard_map/ppermute | solution.py:452
  163.5 13.8 %collective-permute-start.23 = (f32[1,8,16,8,128]{4,3,2,1,0:T(8,128)S(1)}, f32[1,8,16,8,128]{4,3,2,1,0:T(8,128)S(1)}, u32[]{:S(2)}, u32[]{:S(2)}) collective-permute-start(f32[1,8,16,8,128]{4,3,2,1,0:T(8,128)S(1)} %get-tuple-element.69), channel_id=1, source_target_pairs={{0,4},{4,0},{8,12},{12,8},{16,20},{20,16},{24,28},{28,24},{1,5},{5... | collective-permute-start | bytes 1572872 | tf_op jit(solution)/shard_map/ppermute | solution.py:452
  (39 other events, 349.7 us)

commit v5 on v4

v5 whole, which is shorter than its diff:
```python
import functools

import jax
import jax.numpy as jnp
from jax import lax
from jax.experimental import pallas as pl
from jax.experimental.pallas import tpu as pltpu
from jax.sharding import PartitionSpec as P

OMEGA = 0.8
KEEP = 1.0 - OMEGA
A0 = 1.0 + KEEP + KEEP**2 + KEEP**3
A1 = 1.0 + 2.0 * KEEP + 3.0 * KEEP**2
A2 = 1.0 + 3.0 * KEEP
A3 = 1.0
DEPTH = 6
RING = DEPTH + 1
EDGE = 8
GROUPS = (2, 2, 2, 1, 1)
AFTER = (None, 0, 1, 1, 2)
MIB = 1 << 20


def smem():
    return pl.BlockSpec(memory_space=pltpu.SMEM)


def vmem():
    return pl.BlockSpec(memory_space=pltpu.VMEM)


def prep_kernel(probes, out, wide):
    many, planes, rows, depth = probes.shape
    cells = planes * rows
    wide[...] = probes[...].astype(jnp.float32).reshape(wide.shape)

    def plane(x, carry):
        at = x * rows
        for y in range(rows):
            out[pl.ds(pl.multiple_of((at + y) * many, many), many), :] = wide[pl.ds(at + y, many, stride=cells), :]
        return carry

    lax.fori_loop(0, planes, plane, 0)


def prep(probes, tile, size, after):
    planes, rows, depth = probes.shape[1:]
    count = planes * rows * 8
    in_specs = [pl.BlockSpec((8, planes, rows, depth), lambda i: (tile + i, 0, 0, 0))]
    kernel, operands = prep_kernel, [probes]
    if after is not None:
        in_specs.insert(0, pl.BlockSpec(memory_space=pl.ANY))
        kernel, operands = (lambda _, *refs: prep_kernel(*refs)), [after, probes]
    return pl.pallas_call(
        kernel,
        grid=(size,),
        in_specs=in_specs,
        out_specs=pl.BlockSpec((count, depth), lambda i: (i, 0)),
        out_shape=jax.ShapeDtypeStruct((size * count, depth), jnp.float32),
        scratch_shapes=[pltpu.VMEM((count, depth), jnp.float32)],
        compiler_params=pltpu.CompilerParams(vmem_limit_bytes=40 * MIB),
        cost_estimate=pl.CostEstimate(flops=0, bytes_accessed=size * MIB, transcendentals=0),
        name="spread_probes",
    )(*operands)


def pieces_of(side, tiles, planes, rows, many, own, recv, outer):
    depth = own.shape[-1]
    own, recv = (ref.reshape(tiles, planes, rows, many, depth) for ref in (own, recv))
    outer = outer.reshape(tiles, DEPTH, rows, many, depth)
    top = DEPTH + planes
    return (
        (own, 0, planes, 0, DEPTH),
        (recv, side * (planes - DEPTH), DEPTH, planes, top * (1 - side)),
        (outer, 0, DEPTH, planes + DEPTH, top * side),
    )


def border_kernel(sizes, h_ref, own, recv, outer, after, low, high):
    tiles, planes, rows, many = sizes
    shape = (tiles, planes + 2 * DEPTH, DEPTH, many, own.shape[-1])
    low, high = low.reshape(shape), high.reshape(shape)
    for piece, first, count, role, _ in pieces_of(h_ref[0], *sizes, own, recv, outer):
        for t in range(tiles):
            for i in range(count):
                low[t, role + i] = piece[t, first + i, rows - DEPTH :]
                high[t, role + i] = piece[t, first + i, :DEPTH]


def border(side, sizes, own, recv, outer, after):
    tiles, planes, rows, many = sizes
    message = jax.ShapeDtypeStruct((tiles * (planes + 2 * DEPTH) * DEPTH * many, own.shape[-1]), jnp.float32)
    return pl.pallas_call(
        functools.partial(border_kernel, sizes),
        in_specs=[smem()] + [vmem()] * 3 + [pl.BlockSpec(memory_space=pl.ANY)],
        out_specs=[vmem(), vmem()],
        out_shape=[message, message],
        compiler_params=pltpu.CompilerParams(vmem_limit_bytes=12 * MIB),
        cost_estimate=pl.CostEstimate(flops=0, bytes_accessed=2 * MIB, transcendentals=0),
        name="border_rows",
    )(side, own, recv, outer, after)


def coef_kernel(total_x, total_y, at_ref, ext, out, root):
    wide_x, wide_y, depth = root.shape
    y = at_ref[1] + lax.broadcasted_iota(jnp.int32, (wide_y, depth), 0)
    z = lax.broadcasted_iota(jnp.int32, (wide_y, depth), 1)
    inside = (y >= 0) & (y < total_y)
    root[0] = jnp.zeros((wide_y, depth), jnp.float32)
    root[wide_x - 1] = jnp.zeros((wide_y, depth), jnp.float32)

    def roots(i, carry):
        for x in (2 * i + 1, 2 * i + 2):
            k = ext[0, x]
            beside = ext[0, x - 1] + ext[0, x + 1] + pltpu.roll(k, 1, 0) + pltpu.roll(k, wide_y - 1, 0)
            beside = beside + jnp.where(z == 0, 0.0, pltpu.roll(k, 1, 1))
            beside = beside + jnp.where(z == depth - 1, 0.0, pltpu.roll(k, depth - 1, 1))
            diag = ext[1, x] + 0.5 * (6.0 * k + beside)
            here = inside & (at_ref[0] + x >= 0) & (at_ref[0] + x < total_x)
            root[x] = jnp.where(here, lax.rsqrt(jnp.where(here, diag, 1.0)), 0.0)
        return carry

    lax.fori_loop(0, (wide_x - 2) // 2, roots, 0)

    def plane(i, carry):
        for x in (2 * i + 1, 2 * i + 2):
            k, inv = ext[0, x], root[x]
            half = 0.5 * OMEGA * inv
            out[0, x] = half * root[x + 1] * (k + ext[0, x + 1])
            out[1, x] = half * pltpu.roll(inv, wide_y - 1, 0) * (k + pltpu.roll(k, wide_y - 1, 0))
            up = half * pltpu.roll(inv, depth - 1, 1) * (k + pltpu.roll(k, depth - 1, 1))
            out[2, x] = jnp.where(z == depth - 1, 0.0, up)
            out[3, x] = OMEGA * inv * ext[2, x]
            out[4, x] = (OMEGA * A0) * inv * inv * ext[3, x]
            out[5, x] = A0 * inv * ext[2, x]
        return carry

    lax.fori_loop(0, (wide_x - 2) // 2, plane, 0)


def coefficients(side, at, totals, maps):
    planes, rows, depth = maps[0].shape
    lower = side == 0
    own = jnp.stack(maps)
    recv = swap(own)
    outer = relay(lax.dynamic_slice_in_dim(recv, (1 - side) * (planes - RING), RING, 1))
    inner = lax.dynamic_slice_in_dim(recv, side * (planes - RING), RING, 1)
    wide = jnp.concatenate([jnp.where(lower, outer, inner), own, jnp.where(lower, inner, outer)], axis=1)
    low, high = above(wide[:, :, rows - EDGE :]), below(wide[:, :, :EDGE])
    ext = jnp.concatenate([low, wide, high], axis=2)
    shape = ext.shape[1:]
    return pl.pallas_call(
        functools.partial(coef_kernel, *totals),
        in_specs=[smem(), vmem()],
        out_specs=vmem(),
        out_shape=jax.ShapeDtypeStruct((6,) + shape, jnp.float32),
        scratch_shapes=[pltpu.VMEM(shape, jnp.float32)],
        compiler_params=pltpu.CompilerParams(vmem_limit_bytes=12 * MIB),
        cost_estimate=pl.CostEstimate(flops=0, bytes_accessed=4 * MIB, transcendentals=0),
        name="coefficients",
    )(at, ext)


def spread(coef, which, x, y, many):
    return coef[which, x, pl.ds(y, many, stride=0), :]


def solve_kernel(sizes, h_ref, coef, own, recv, outer, ylo, yhi, out_ref, r_s, a_s, b_s):
    tiles, planes, rows, many = sizes
    wide_x, wide_y, _, depth = r_s.shape[1:]
    span = range(tiles)
    shape = (tiles, wide_x, DEPTH, many, depth)
    ylo, yhi = ylo.reshape(shape), yhi.reshape(shape)

    def row(which, x, y):
        return spread(coef, which, x + RING - DEPTH, y + EDGE - DEPTH, many)

    for piece, first, count, role, place in pieces_of(h_ref[0], *sizes, own, recv, outer):

        def fill(i, carry, piece=piece, first=first, role=role, place=place):
            x = place + i
            for y in range(wide_y):
                scale = row(3, x, y)
                for t in span:
                    if y < DEPTH:
                        value = ylo[t, role + i, y]
                    elif y < DEPTH + rows:
                        value = piece[t, first + i, y - DEPTH]
                    else:
                        value = yhi[t, role + i, y - DEPTH - rows]
                    r_s[t, x, y] = value * scale
            return carry

        lax.fori_loop(0, count, fill, 0)

    def stencil(src, r, x, low, scale, last=None):
        both = (x, x + 1)
        prev = [[src[t, p, low - 1] for t in span] for p in both]
        here = [[src[t, p, low] for t in span] for p in both]
        cy_prev = [row(1, p, low - 1) for p in both]
        for y in range(low, wide_y - low):
            after = [[src[t, p, y + 1] for t in span] for p in both]
            cx = [row(0, x + k, y) for k in (-1, 0, 1)]
            cy = [row(1, p, y) for p in both]
            values = []
            for k, p in enumerate(both):
                cz = row(2, p, y)
                end = None if last is None else row(last, p, y)
                for t in span:
                    f = here[k][t]
                    before = src[t, x - 1, y] if k == 0 else here[0][t]
                    beyond = here[1][t] if k == 0 else src[t, x + 2, y]
                    total = cx[k] * before + cx[k + 1] * beyond
                    total = total + (cy_prev[k] * prev[k][t] + cy[k] * after[k][t])
                    total = total + (pltpu.roll(cz * f, 1, 1) + cz * pltpu.roll(f, depth - 1, 1))
                    value = r[t, p, y] + scale * total
                    values.append((t, k, value if end is None else value * end))
            yield y, values
            prev, here, cy_prev = here, after, cy

    def sweep(src, dst, r, low, scale, last=None):
        def pair(i, carry):
            x = low + 2 * i
            for y, values in stencil(src, r, x, low, scale, last):
                for t, k, value in values:
                    dst[t, x + k, y] = value
            return carry

        lax.fori_loop(0, (wide_x - 2 * low) // 2, pair, 0)

    sweep(r_s, a_s, r_s, 1, A3 / A2)
    sweep(a_s, b_s, r_s, 2, A2 / A1)
    sweep(b_s, a_s, r_s, 3, A1 / A0, last=4)
    sweep(a_s, b_s, a_s, 4, A3 / A2)
    sweep(b_s, r_s, a_s, 5, A2 / A1)

    def out(i, carry):
        for y, values in stencil(r_s, a_s, DEPTH + 2 * i, DEPTH, A1 / A0, last=5):
            for t, k, value in values:
                out_ref[t, 2 * i + k, y - DEPTH] = value
        return carry

    lax.fori_loop(0, planes // 2, out, 0)


def solve(side, sizes, coef, *messages):
    tiles, planes, rows, many = sizes
    depth = coef.shape[-1]
    wide = (planes + 2 * DEPTH, rows + 2 * DEPTH)
    field = pltpu.VMEM((tiles,) + wide + (many, depth), jnp.float32)
    cells = tiles * wide[0] * wide[1] * many * depth
    return pl.pallas_call(
        functools.partial(solve_kernel, sizes),
        in_specs=[smem()] + [vmem()] * 6,
        out_specs=vmem(),
        out_shape=jax.ShapeDtypeStruct((tiles, planes, rows, many, depth), jnp.float32),
        scratch_shapes=[field, field, field],
        compiler_params=pltpu.CompilerParams(vmem_limit_bytes=(6 + 12 * tiles) * MIB),
        cost_estimate=pl.CostEstimate(flops=60 * cells, bytes_accessed=12 * MIB, transcendentals=0),
        name="both_solves",
    )(side, coef, *messages)


def stacked(tiles, rows):
    columns = [jnp.concatenate([t[0, 0, y] for t in tiles], axis=0) for y in range(rows)]
    return jnp.concatenate(columns, axis=1)


def split(value):
    high = value.astype(jnp.bfloat16)
    return high, (value - high.astype(jnp.float32)).astype(jnp.bfloat16)


def gram_kernel(scale, *refs):
    tiles, out, total = refs[:-2], refs[-2], refs[-1]
    step = pl.program_id(0)

    @pl.when(step == 0)
    def _():
        total[...] = jnp.zeros_like(total)

    both = jnp.concatenate(split(stacked(tiles, tiles[0].shape[2])), axis=0)
    total[...] += lax.dot_general(both, both, (((1,), (1,)), ((), ())), preferred_element_type=jnp.float32)

    @pl.when(step == pl.num_programs(0) - 1)
    def _():
        n = out.shape[0]
        g = total[:n, :n] + total[:n, n:] + total[n:, :n] + total[n:, n:]
        out[...] = g * scale


def tile_specs(groups):
    return [
        pl.BlockSpec((1, 1) + g.shape[2:], lambda i, t=t: (t, i, 0, 0, 0)) for g in groups for t in range(g.shape[0])
    ]


def tile_args(groups):
    return [g for g in groups for t in range(g.shape[0])]


def gram_of(groups, cells):
    tiles = tile_args(groups)
    count = 8 * len(tiles)
    return pl.pallas_call(
        functools.partial(gram_kernel, 1.0 / cells),
        grid=(tiles[0].shape[1],),
        in_specs=tile_specs(groups),
        out_specs=pl.BlockSpec((count, count), lambda i: (0, 0)),
        out_shape=jax.ShapeDtypeStruct((count, count), jnp.float32),
        scratch_shapes=[pltpu.VMEM((2 * count, 2 * count), jnp.float32)],
        compiler_params=pltpu.CompilerParams(vmem_limit_bytes=16 * MIB),
        cost_estimate=pl.CostEstimate(flops=0, bytes_accessed=6 * MIB, transcendentals=0),
        name="gram",
    )(*tiles)


def factor(gram):
    n = gram.shape[0]
    i = lax.broadcasted_iota(jnp.int32, (n, n), 0)
    j = lax.broadcasted_iota(jnp.int32, (n, n), 1)
    both = jnp.concatenate([gram, (i == j).astype(jnp.float32)], axis=1)
    rows = [both[8 * t : 8 * t + 8] for t in range(n // 8)]
    place = lax.broadcasted_iota(jnp.int32, (8, 2 * n), 0)
    for c in range(0, n, 2):
        t, s = divmod(c, 8)
        first, second = rows[t][s : s + 1], rows[t][s + 1 : s + 2]
        a, b, d = first[:, c : c + 1], first[:, c + 1 : c + 2], second[:, c + 1 : c + 2]
        inv = 1.0 / (a * d - b * b)
        w1 = (d * first - b * second) * inv
        w2 = (a * second - b * first) * inv
        fixed = jnp.where(place == s + 1, second - (b / a) * first, rows[t])
        for k in range(t, n // 8):
            new = rows[k] - (rows[k][:, c : c + 1] * w1 + rows[k][:, c + 1 : c + 2] * w2)
            rows[k] = jnp.where(place > s + 1, new, fixed) if k == t else new
    done = jnp.concatenate(rows, axis=0)
    size = jnp.sum(jnp.where(i == j, done[:, :n], 0.0), axis=1, keepdims=True)
    done = done * lax.rsqrt(size)
    return done[:, :n], done[:, n:]


def basis_kernel(a_ref, b_ref, *refs):
    tiles, (q_ref, r_ref, left) = refs[:-3], refs[-3:]
    n = r_ref.shape[0]
    rows = tiles[0].shape[2]

    @pl.when(pl.program_id(0) == 0)
    def _():
        upper, inverse = factor(a_ref[...] + b_ref[...])
        i = lax.broadcasted_iota(jnp.int32, (n, n), 0)
        j = lax.broadcasted_iota(jnp.int32, (n, n), 1)
        r_ref[...] = jnp.where(j >= i, upper, 0.0)
        inverse = jnp.where(j <= i, inverse, 0.0)
        high, low = split(inverse)
        left[...] = jnp.concatenate([high, high, low, low], axis=1)

    high, low = split(stacked(tiles, rows))
    q = jnp.dot(left[...], jnp.concatenate([high, low, high, low], axis=0), preferred_element_type=jnp.float32)
    depth = q.shape[1] // rows
    flat = q_ref.reshape(n * rows, depth)
    for y in range(rows):
        flat[pl.ds(y, n, stride=rows), :] = q[:, y * depth : (y + 1) * depth]


def basis(a, b, groups):
    n = a.shape[0]
    tiles = tile_args(groups)
    _, planes, rows, _, depth = tiles[0].shape
    full = pl.BlockSpec((n, n), lambda i: (0, 0))
    return pl.pallas_call(
        basis_kernel,
        grid=(planes,),
        in_specs=[full, full] + tile_specs(groups),
        out_specs=[pl.BlockSpec((n, 1, rows, depth), lambda i: (0, i, 0, 0)), full],
        out_shape=[
            jax.ShapeDtypeStruct((n, planes, rows, depth), jnp.float32),
            jax.ShapeDtypeStruct((n, n), jnp.float32),
        ],
        scratch_shapes=[pltpu.VMEM((n, 4 * n), jnp.bfloat16)],
        compiler_params=pltpu.CompilerParams(vmem_limit_bytes=24 * MIB),
        cost_estimate=pl.CostEstimate(flops=0, bytes_accessed=8 * MIB, transcendentals=0),
        name="basis",
    )(a, b, *tiles)


def swap(value):
    return lax.ppermute(value, "gx", [(i, i ^ 1) for i in range(lax.axis_size("gx"))])


def relay(value):
    n = lax.axis_size("gx")
    return lax.ppermute(value, "gx", [(i, i + 2 - 4 * (i % 2)) for i in range(n) if 0 <= i + 2 - 4 * (i % 2) < n])


def above(value):
    n = lax.axis_size("gy")
    return lax.ppermute(value, "gy", [(i, i + 1) for i in range(n - 1)])


def below(value):
    n = lax.axis_size("gy")
    return lax.ppermute(value, "gy", [(i + 1, i) for i in range(n - 1)])


def summed(value):
    steps = []
    for axis in ("gy", "gx"):
        n = lax.axis_size(axis)
        assert n & (n - 1) == 0
        shift = 1
        while shift < n:
            steps.append((axis, shift, n))
            shift *= 2
    other = None
    for axis, shift, n in steps:
        if other is not None:
            value = value + other
        other = lax.ppermute(value, axis, [(i, i ^ shift) for i in range(n)])
    return value, other


def relayed(side, recv, size, planes):
    fields = recv.reshape(size, planes, -1, recv.shape[-1])
    part = lax.dynamic_slice_in_dim(fields, (1 - side) * (planes - DEPTH), DEPTH, 1)
    return relay(part.reshape(-1, recv.shape[-1]))


def body(probes, permeability, absorption, sensitivity, observe_weight):
    count, planes, rows, depth = probes.shape
    totals = (planes * lax.axis_size("gx"), rows * lax.axis_size("gy"))
    gx, gy = lax.axis_index("gx"), lax.axis_index("gy")
    side = gx % 2
    flag = side.reshape(1).astype(jnp.int32)
    at = jnp.stack([gx * planes - RING, gy * rows - EDGE]).astype(jnp.int32)
    assert 8 * sum(GROUPS) == count

    groups = []
    coef = recv = None
    tile = 0
    for number, size in enumerate(GROUPS):
        sizes = (size, planes, rows, 8)
        own = prep(probes, tile, size, recv)
        tile += size
        recv = swap(own)
        if coef is None:
            coef = coefficients(side, at, totals, (permeability, absorption, sensitivity, observe_weight))
        outer = relayed(side, recv, size, planes)
        after = AFTER[number]
        low, high = border(flag, sizes, own, recv, outer, own if after is None else groups[after])
        groups.append(solve(flag, sizes, coef, own, recv, outer, above(low), below(high)))
    a, b = summed(gram_of(groups, totals[0] * totals[1] * depth))
    q, r = basis(a, b, groups)
    return (q, r)


def solution(mesh):
    return jax.shard_map(
        body,
        mesh=mesh,
        in_specs=(
            P(None, "gx", "gy", None),
            P("gx", "gy", None),
            P("gx", "gy", None),
            P("gx", "gy", None),
            P("gx", "gy", None),
        ),
        out_specs=(P(None, "gx", "gy", None), P()),
        check_vma=False,
    )
```

time: 210 us -> 246 us (1.17)
  waiting for transfers between devices: 51.7 us -> 83.5 us
  starting transfers between devices: 64.7 us -> 74 us
  Pallas kernels: 80.3 us -> 75.1 us
  other arithmetic: 0.14 us -> 3.49 us
  local copies, waits for them, and re-layouts: 10.9 us -> 7.9 us
    ppermute x8 -> x6, waiting for transfers between devices: 31.1 us -> 62 us  [swap(): lax.ppermute(value, 'gx', [(i, i ^ 1) for i in range(lax.axis_size('gx'))])]
    ppermute x4 -> x6, starting transfers between devices: 12.8 us -> 23.4 us  [above(): return lax.ppermute(value, 'gy', [(i, i + 1) for i in range(n - 1)])]
    ppermute x8 -> x6, starting transfers between devices: 14.1 us -> 7.75 us  [swap(): lax.ppermute(value, 'gx', [(i, i ^ 1) for i in range(lax.axis_size('gx'))])]
    unnamed x68 -> x26, local copies, waits for them, and re-layouts: 9.95 us -> 3.72 us
    pallas_call x14 -> x17, Pallas kernels: 77.7 us -> 72.5 us  [the longest x5 49.8 us: solve(): pl.pallas_call(functools.partial(solve_kernel, sizes), in_specs=[smem()]...]
    ppermute x8 -> x6, waiting for transfers between devices: 12.1 us -> 8.6 us  [relay(): lax.ppermute(value, 'gx', [(i, i + 2 - 4 * (i % 2)) for i in range(n) if...]
    ppermute x4 -> x6, waiting for transfers between devices: 0.01 us -> 3.06 us  [below(): return lax.ppermute(value, 'gy', [(i + 1, i) for i in range(n - 1)])]
    ppermute x4 -> x6, starting transfers between devices: 5.28 us -> 7.91 us  [below(): return lax.ppermute(value, 'gy', [(i + 1, i) for i in range(n - 1)])]
  transfers between devices with their start and end apart: 29 -> 29, of which waited for: 12 -> 11; matrix products, arithmetic and copies ran while one was open for 1% -> 3% of each run, Pallas kernels for 31% -> 22%
where the time goes in v5:
time: 246 us; the launch traced here: 245 us
  waiting for transfers between devices  83.5 us (34%)
  Pallas kernels  75.1 us (31%)
  starting transfers between devices  74 us (30%)
  local copies, waits for them, and re-layouts  7.9 us (3%)
  other arithmetic  3.49 us (1%)
    ppermute x6, waiting for transfers between devices, swap(): lax.ppermute(value, 'gx', [(i, i ^ 1) for i in range(lax.axis_size('gx'))])  62 us
    pallas_call x5, Pallas kernels, solve(): pl.pallas_call(functools.partial(solve_kernel, sizes), in_specs=[smem()]...  49.8 us
    ppermute x6, starting transfers between devices, above(): return lax.ppermute(value, 'gy', [(i, i + 1) for i in range(n - 1)])  23.4 us
    ppermute x6, starting transfers between devices, relay(): lax.ppermute(value, 'gx', [(i, i + 2 - 4 * (i % 2)) for i in range(n) if...  23.1 us
    ppermute x5, starting transfers between devices, summed(): other = lax.ppermute(value, axis, [(i, i ^ shift) for i in range(n)])  11.9 us
    pallas_call x1, Pallas kernels, basis(): pl.pallas_call(basis_kernel, grid=(planes,), in_specs=[full, full] + tile...  10.3 us
    ppermute x5, waiting for transfers between devices, summed(): other = lax.ppermute(value, axis, [(i, i ^ shift) for i in range(n)])  9.85 us
    ppermute x6, waiting for transfers between devices, relay(): lax.ppermute(value, 'gx', [(i, i + 2 - 4 * (i % 2)) for i in range(n) if...  8.6 us
  transfers between devices with their start and end apart: 29, of which 11 were waited for; matrix products, arithmetic and copies ran while one was open for 3% of the time, Pallas kernels for 22%

profile of v5, /device:TPU:0, one launch (start us, length us, event | category | flops | bytes accessed | tf_op | source)
XLA Modules:
  0.0 245.2 jit_solution(15772030621788581862)
XLA Ops:
  3.1 3.0 %collective-permute-start.4 = (f32[2048,128]{1,0:T(8,128)S(1)}, f32[2048,128]{1,0:T(8,128)S(1)}, u32[]{:S(2)}, u32[]{:S(2)}) collective-permute-start(f32[2048,128]{1,0:T(8,128)S(1)} %spread_probes.5.own.after), channel_id=1, source_target_pairs={{0,4},{4,0},{8,12},{12,8},{16,20},{20,16},{24,28},{28,24},{1,5},{5... | collective-permute-start | bytes 3145736 | tf_op jit(solution)/shard_map/ppermute | solution.py:387
  6.1 23.2 %collective-permute-done.4.recv._ = f32[2048,128]{1,0:T(8,128)S(1)} collective-permute-done((f32[2048,128]{1,0:T(8,128)S(1)}, f32[2048,128]{1,0:T(8,128)S(1)}, u32[]{:S(2)}, u32[]{:S(2)}) %collective-permute-start.4) | collective-permute-done | bytes 1048608 | tf_op jit(solution)/shard_map/ppermute | solution.py:387
  33.1 3.8 %collective-permute-start.5 = (f32[1536,128]{1,0:T(8,128)S(1)}, f32[1536,128]{1,0:T(8,128)S(1)}, u32[]{:S(2)}, u32[]{:S(2)}) collective-permute-start(f32[1536,128]{1,0:T(8,128)S(1)} %bitcast.20), channel_id=1, source_target_pairs={{0,8},{8,16},{12,4},{16,24},{20,12},{28,20},{1,9},{9,17},{13,5},{1... | collective-permute-start | bytes 2359304 | tf_op jit(solution)/shard_map/ppermute | solution.py:392
  36.9 24.2 %collective-permute-done = f32[4,8,16,128]{3,2,1,0:T(8,128)S(1)} collective-permute-done((f32[4,8,16,128]{3,2,1,0:T(8,128)S(1)}, f32[4,8,16,128]{3,2,1,0:T(8,128)S(1)}, u32[]{:S(2)}, u32[]{:S(2)}) %collective-permute-start) | collective-permute-done | bytes 262176 | tf_op jit(solution)/shard_map/ppermute | solution.py:387
  61.1 4.1 %collective-permute-start.1 = (f32[4,7,16,128]{3,2,1,0:T(8,128)S(1)}, f32[4,7,16,128]{3,2,1,0:T(8,128)}, u32[]{:S(2)}, u32[]{:S(2)}) collective-permute-start(f32[4,7,16,128]{3,2,1,0:T(8,128)S(1)} %constant_dynamic-slice_fusion.5), channel_id=1, source_target_pairs={{0,8},{8,16},{12,4},{16,24},{20,12},{28,20},{1,9},{9,17},{13,5},{1... | collective-permute-start | bytes 688136 | tf_op jit(solution)/shard_map/ppermute | solution.py:392
  82.1 4.3 %collective-permute-start.2 = (f32[4,22,8,128]{3,2,1,0:T(8,128)S(1)}, f32[4,22,8,128]{3,2,1,0:T(8,128)}, u32[]{:S(2)}, u32[]{:S(2)}) collective-permute-start(f32[4,22,8,128]{3,2,1,0:T(8,128)S(1)} %get-tuple-element.22), channel_id=1, source_target_pairs={{0,1},{1,2},{2,3},{4,5},{5,6},{6,7},{8,9},{9,10},{10,11},{12,13},{... | collective-permute-start | bytes 1081352 | tf_op jit(solution)/shard_map/ppermute | solution.py:397
  88.5 4.4 %collective-permute-start.9 = (f32[1536,128]{1,0:T(8,128)}, f32[1536,128]{1,0:T(8,128)}, u32[]{:S(2)}, u32[]{:S(2)}) collective-permute-start(f32[1536,128]{1,0:T(8,128)} %bitcast.10), channel_id=1, source_target_pairs={{0,8},{8,16},{12,4},{16,24},{20,12},{28,20},{1,9},{9,17},{13,5},{1... | collective-permute-start | bytes 2359304 | tf_op jit(solution)/shard_map/ppermute | solution.py:392
  94.2 3.0 %collective-permute-done.3 = f32[4,22,8,128]{3,2,1,0:T(8,128)} collective-permute-done((f32[4,22,8,128]{3,2,1,0:T(8,128)}, f32[4,22,8,128]{3,2,1,0:T(8,128)}, u32[]{:S(2)}, u32[]{:S(2)}) %collective-permute-start.3) | collective-permute-done | bytes 360480 | tf_op jit(solution)/shard_map/ppermute | solution.py:402
  101.1 12.0 %both_solves.5.after.refs_0_.refs_1_ = f32[2,8,16,8,128]{4,3,2,1,0:T(8,128)S(1)} custom-call(s32[1]{0:T(128)} %bitcast.h_ref, f32[6,22,32,128]{3,2,1,0:T(8,128)S(1)} %coefficients.1.coef, f32[2048,128]{1,0:T(8,128)S(1)} %spread_probes.5.own.after, f32[2048,128]{1,0:T(8,128)S(1)} %copy-done.4, f32[1536,128]{1,0:T(8,128)S(1)} %copy-done.7, ...), custom_call_target="tpu_custom_call" | custom-call | flops 68812800 | bytes 12582912 | tf_op jit(solution)/shard_map/both_solves/pallas_call | solution.py:252
  115.0 7.9 %collective-permute-start.10 = (f32[1920,128]{1,0:T(8,128)S(1)}, f32[1920,128]{1,0:T(8,128)S(1)}, u32[]{:S(2)}, u32[]{:S(2)}) collective-permute-start(f32[1920,128]{1,0:T(8,128)S(1)} %get-tuple-element.14), channel_id=1, source_target_pairs={{0,1},{1,2},{2,3},{4,5},{5,6},{6,7},{8,9},{9,10},{10,11},{12,13},{... | collective-permute-start | bytes 2949128 | tf_op jit(solution)/shard_map/ppermute | solution.py:397
  125.4 3.8 %collective-permute-start.13 = (f32[1536,128]{1,0:T(8,128)S(1)}, f32[1536,128]{1,0:T(8,128)S(1)}, u32[]{:S(2)}, u32[]{:S(2)}) collective-permute-start(f32[1536,128]{1,0:T(8,128)S(1)} %bitcast.21), channel_id=1, source_target_pairs={{0,8},{8,16},{12,4},{16,24},{20,12},{28,20},{1,9},{9,17},{13,5},{1... | collective-permute-start | bytes 2359304 | tf_op jit(solution)/shard_map/ppermute | solution.py:392
  129.7 14.7 %collective-permute-done.16.recv._ = f32[1024,128]{1,0:T(8,128)S(1)} collective-permute-done((f32[1024,128]{1,0:T(8,128)S(1)}, f32[1024,128]{1,0:T(8,128)S(1)}, u32[]{:S(2)}, u32[]{:S(2)}) %collective-permute-start.16) | collective-permute-done | bytes 524320 | tf_op jit(solution)/shard_map/ppermute | solution.py:387
  144.9 12.3 %both_solves.6.after.refs_2_.refs_3_ = f32[2,8,16,8,128]{4,3,2,1,0:T(8,128)S(1)} custom-call(s32[1]{0:T(128)} %bitcast.h_ref, f32[6,22,32,128]{3,2,1,0:T(8,128)S(1)} %coefficients.1.coef, f32[2048,128]{1,0:T(8,128)} %spread_probes.6.own, f32[2048,128]{1,0:T(8,128)} %collective-permute-done.8.recv._, f32[1536,128]{1,0:T(8,128)} %collective-permute-done.9.outer, ...), custom_call_target="tpu_custom_call" | custom-call | flops 68812800 | bytes 12582912 | tf_op jit(solution)/shard_map/both_solves/pallas_call | solution.py:252
  162.1 3.5 %collective-permute-start.17 = (f32[768,128]{1,0:T(8,128)S(1)}, f32[768,128]{1,0:T(8,128)S(1)}, u32[]{:S(2)}, u32[]{:S(2)}) collective-permute-start(f32[768,128]{1,0:T(8,128)S(1)} %bitcast.35), channel_id=1, source_target_pairs={{0,8},{8,16},{12,4},{16,24},{20,12},{28,20},{1,9},{9,17},{13,5},{1... | collective-permute-start | bytes 1179656 | tf_op jit(solution)/shard_map/ppermute | solution.py:392
  165.7 3.5 %collective-permute-start.21 = (f32[768,128]{1,0:T(8,128)S(1)}, f32[768,128]{1,0:T(8,128)S(1)}, u32[]{:S(2)}, u32[]{:S(2)}) collective-permute-start(f32[768,128]{1,0:T(8,128)S(1)} %bitcast.34), channel_id=1, source_target_pairs={{0,8},{8,16},{12,4},{16,24},{20,12},{28,20},{1,9},{9,17},{13,5},{1... | collective-permute-start | bytes 1179656 | tf_op jit(solution)/shard_map/ppermute | solution.py:392
  169.2 5.8 %collective-permute-done.17.outer = f32[768,128]{1,0:T(8,128)S(1)} collective-permute-done((f32[768,128]{1,0:T(8,128)S(1)}, f32[768,128]{1,0:T(8,128)S(1)}, u32[]{:S(2)}, u32[]{:S(2)}) %collective-permute-start.17) | collective-permute-done | bytes 393248 | tf_op jit(solution)/shard_map/ppermute | solution.py:392
  178.7 12.0 %both_solves.7.after.refs_4_.refs_5_ = f32[2,8,16,8,128]{4,3,2,1,0:T(8,128)S(1)} custom-call(s32[1]{0:T(128)} %bitcast.h_ref, f32[6,22,32,128]{3,2,1,0:T(8,128)S(1)} %coefficients.1.coef, f32[2048,128]{1,0:T(8,128)} %spread_probes.7.own, f32[2048,128]{1,0:T(8,128)} %collective-permute-done.12.recv._, f32[1536,128]{1,0:T(8,128)S(1)} %collective-permute-done.13.outer, ...), custom_call_target="tpu_custom_call" | custom-call | flops 68812800 | bytes 12582912 | tf_op jit(solution)/shard_map/both_solves/pallas_call | solution.py:252
  190.9 4.6 %collective-permute-start.22 = (f32[960,128]{1,0:T(8,128)S(1)}, f32[960,128]{1,0:T(8,128)S(1)}, u32[]{:S(2)}, u32[]{:S(2)}) collective-permute-start(f32[960,128]{1,0:T(8,128)S(1)} %get-tuple-element.20), channel_id=1, source_target_pairs={{0,1},{1,2},{2,3},{4,5},{5,6},{6,7},{8,9},{9,10},{10,11},{12,13},{... | collective-permute-start | bytes 1474568 | tf_op jit(solution)/shard_map/ppermute | solution.py:397
  197.0 6.8 %both_solves.8.refs_6_ = f32[1,8,16,8,128]{4,3,2,1,0:T(8,128)S(1)} custom-call(s32[1]{0:T(128)} %bitcast.h_ref, f32[6,22,32,128]{3,2,1,0:T(8,128)S(1)} %coefficients.1.coef, f32[1024,128]{1,0:T(8,128)S(1)} %spread_probes.8.own, f32[1024,128]{1,0:T(8,128)S(1)} %collective-permute-done.16.recv._, f32[768,128]{1,0:T(8,128)S(1)} %collective-permute-done.17.outer, ...), custom_call_target="tpu_custom_call" | custom-call | flops 34406400 | bytes 12582912 | tf_op jit(solution)/shard_map/both_solves/pallas_call | solution.py:252
  203.8 6.8 %both_solves.9.refs_7_ = f32[1,8,16,8,128]{4,3,2,1,0:T(8,128)S(1)} custom-call(s32[1]{0:T(128)} %bitcast.h_ref, f32[6,22,32,128]{3,2,1,0:T(8,128)S(1)} %coefficients.1.coef, f32[1024,128]{1,0:T(8,128)S(1)} %spread_probes.9.own, f32[1024,128]{1,0:T(8,128)S(1)} %collective-permute-done.20.recv, f32[768,128]{1,0:T(8,128)S(1)} %collective-permute-done.21.outer, ...), custom_call_target="tpu_custom_call" | custom-call | flops 34406400 | bytes 12582912 | tf_op jit(solution)/shard_map/both_solves/pallas_call | solution.py:252
  213.2 3.7 %collective-permute-start.24 = (f32[64,64]{1,0:T(8,128)S(1)}, f32[64,64]{1,0:T(8,128)S(1)}, u32[]{:S(2)}, u32[]{:S(2)}) collective-permute-start(f32[64,64]{1,0:T(8,128)S(1)} %gram.1), channel_id=1, source_target_pairs={{0,1},{1,0},{2,3},{3,2},{4,5},{5,4},{6,7},{7,6},{8,9},{9,8},{10,11... | collective-permute-start | bytes 49160 | tf_op jit(solution)/shard_map/ppermute | solution.py:418
  218.5 3.2 %collective-permute-done.25 = f32[64,64]{1,0:T(8,128)S(1)} collective-permute-done((f32[64,64]{1,0:T(8,128)S(1)}, f32[64,64]{1,0:T(8,128)S(1)}, u32[]{:S(2)}, u32[]{:S(2)}) %collective-permute-start.25) | collective-permute-done | bytes 16416 | tf_op jit(solution)/shard_map/ppermute | solution.py:418
  230.0 3.0 %collective-permute-start.28 = (f32[64,64]{1,0:T(8,128)S(1)}, f32[64,64]{1,0:T(8,128)S(1)}, u32[]{:S(2)}, u32[]{:S(2)}) collective-permute-start(f32[64,64]{1,0:T(8,128)S(1)} %add.39.a_ref), channel_id=1, source_target_pairs={{0,16},{4,20},{8,24},{12,28},{16,0},{20,4},{24,8},{28,12},{1,17},{... | collective-permute-start | bytes 49160 | tf_op jit(solution)/shard_map/ppermute | solution.py:418
  234.9 10.3 %basis.1 = (f32[64,8,16,128]{3,2,1,0:T(8,128)}, f32[64,64]{1,0:T(8,128)}) custom-call(f32[64,64]{1,0:T(8,128)S(1)} %add.39.a_ref, f32[64,64]{1,0:T(8,128)S(1)} %collective-permute-done.28.b_ref, f32[2,8,16,8,128]{4,3,2,1,0:T(8,128)S(1)} %both_solves.5.after.refs_0_.refs_1_, f32[2,8,16,8,128]{4,3,2,1,0:T(8,128)S(1)} %both_solves.5.after.refs_0_.refs_1_, ...), custom_call_target="tpu_custom_call" | custom-call | bytes 8388608 | tf_op jit(solution)/shard_map/basis/pallas_call | solution.py:370
  (94 shorter events, 60.4 us)
Async XLA Ops:
  3.1 26.2 %collective-permute-start.4 = (f32[2048,128]{1,0:T(8,128)S(1)}, f32[2048,128]{1,0:T(8,128)S(1)}, u32[]{:S(2)}, u32[]{:S(2)}) collective-permute-start(f32[2048,128]{1,0:T(8,128)S(1)} %spread_probes.5.own.after), channel_id=1, source_target_pairs={{0,4},{4,0},{8,12},{12,8},{16,20},{20,16},{24,28},{28,24},{1,5},{5... | collective-permute-start | bytes 3145736 | tf_op jit(solution)/shard_map/ppermute | solution.py:387
  30.9 46.3 %collective-permute-start.8 = (f32[2048,128]{1,0:T(8,128)}, f32[2048,128]{1,0:T(8,128)}, u32[]{:S(2)}, u32[]{:S(2)}) collective-permute-start(f32[2048,128]{1,0:T(8,128)} %spread_probes.6.own), channel_id=1, source_target_pairs={{0,4},{4,0},{8,12},{12,8},{16,20},{20,16},{24,28},{28,24},{1,5},{5... | collective-permute-start | bytes 3145736 | tf_op jit(solution)/shard_map/ppermute | solution.py:387
  32.7 28.4 %collective-permute-start = (f32[4,8,16,128]{3,2,1,0:T(8,128)S(1)}, f32[4,8,16,128]{3,2,1,0:T(8,128)S(1)}, u32[]{:S(2)}, u32[]{:S(2)}) collective-permute-start(f32[4,8,16,128]{3,2,1,0:T(8,128)S(1)} %pad_maximum_fusion.2), channel_id=1, source_target_pairs={{0,4},{4,0},{8,12},{12,8},{16,20},{20,16},{24,28},{28,24},{1,5},{5... | collective-permute-start | bytes 786440 | tf_op jit(solution)/shard_map/ppermute | solution.py:387
  33.1 37.0 %collective-permute-start.5 = (f32[1536,128]{1,0:T(8,128)S(1)}, f32[1536,128]{1,0:T(8,128)S(1)}, u32[]{:S(2)}, u32[]{:S(2)}) collective-permute-start(f32[1536,128]{1,0:T(8,128)S(1)} %bitcast.20), channel_id=1, source_target_pairs={{0,8},{8,16},{12,4},{16,24},{20,12},{28,20},{1,9},{9,17},{13,5},{1... | collective-permute-start | bytes 2359304 | tf_op jit(solution)/shard_map/ppermute | solution.py:392
  61.1 6.9 %collective-permute-start.1 = (f32[4,7,16,128]{3,2,1,0:T(8,128)S(1)}, f32[4,7,16,128]{3,2,1,0:T(8,128)}, u32[]{:S(2)}, u32[]{:S(2)}) collective-permute-start(f32[4,7,16,128]{3,2,1,0:T(8,128)S(1)} %constant_dynamic-slice_fusion.5), channel_id=1, source_target_pairs={{0,8},{8,16},{12,4},{16,24},{20,12},{28,20},{1,9},{9,17},{13,5},{1... | collective-permute-start | bytes 688136 | tf_op jit(solution)/shard_map/ppermute | solution.py:392
  73.6 27.5 %collective-permute-start.6 = (f32[1920,128]{1,0:T(8,128)}, f32[1920,128]{1,0:T(8,128)}, u32[]{:S(2)}, u32[]{:S(2)}) collective-permute-start(f32[1920,128]{1,0:T(8,128)} %get-tuple-element.12), channel_id=1, source_target_pairs={{0,1},{1,2},{2,3},{4,5},{5,6},{6,7},{8,9},{9,10},{10,11},{12,13},{... | collective-permute-start | bytes 2949128 | tf_op jit(solution)/shard_map/ppermute | solution.py:397
  75.9 25.2 %collective-permute-start.7 = (f32[1920,128]{1,0:T(8,128)}, f32[1920,128]{1,0:T(8,128)}, u32[]{:S(2)}, u32[]{:S(2)}) collective-permute-start(f32[1920,128]{1,0:T(8,128)} %get-tuple-element.13), channel_id=1, source_target_pairs={{1,0},{2,1},{3,2},{5,4},{6,5},{7,6},{9,8},{10,9},{11,10},{13,12},{... | collective-permute-start | bytes 2949128 | tf_op jit(solution)/shard_map/ppermute | solution.py:402
  78.8 45.4 %collective-permute-start.12 = (f32[2048,128]{1,0:T(8,128)}, f32[2048,128]{1,0:T(8,128)}, u32[]{:S(2)}, u32[]{:S(2)}) collective-permute-start(f32[2048,128]{1,0:T(8,128)} %spread_probes.7.own), channel_id=1, source_target_pairs={{0,4},{4,0},{8,12},{12,8},{16,20},{20,16},{24,28},{28,24},{1,5},{5... | collective-permute-start | bytes 3145736 | tf_op jit(solution)/shard_map/ppermute | solution.py:387
  82.1 10.7 %collective-permute-start.2 = (f32[4,22,8,128]{3,2,1,0:T(8,128)S(1)}, f32[4,22,8,128]{3,2,1,0:T(8,128)}, u32[]{:S(2)}, u32[]{:S(2)}) collective-permute-start(f32[4,22,8,128]{3,2,1,0:T(8,128)S(1)} %get-tuple-element.22), channel_id=1, source_target_pairs={{0,1},{1,2},{2,3},{4,5},{5,6},{6,7},{8,9},{9,10},{10,11},{12,13},{... | collective-permute-start | bytes 1081352 | tf_op jit(solution)/shard_map/ppermute | solution.py:397
  88.5 24.7 %collective-permute-start.9 = (f32[1536,128]{1,0:T(8,128)}, f32[1536,128]{1,0:T(8,128)}, u32[]{:S(2)}, u32[]{:S(2)}) collective-permute-start(f32[1536,128]{1,0:T(8,128)} %bitcast.10), channel_id=1, source_target_pairs={{0,8},{8,16},{12,4},{16,24},{20,12},{28,20},{1,9},{9,17},{13,5},{1... | collective-permute-start | bytes 2359304 | tf_op jit(solution)/shard_map/ppermute | solution.py:392
  115.0 29.8 %collective-permute-start.10 = (f32[1920,128]{1,0:T(8,128)S(1)}, f32[1920,128]{1,0:T(8,128)S(1)}, u32[]{:S(2)}, u32[]{:S(2)}) collective-permute-start(f32[1920,128]{1,0:T(8,128)S(1)} %get-tuple-element.14), channel_id=1, source_target_pairs={{0,1},{1,2},{2,3},{4,5},{5,6},{6,7},{8,9},{9,10},{10,11},{12,13},{... | collective-permute-start | bytes 2949128 | tf_op jit(solution)/shard_map/ppermute | solution.py:397
  122.9 21.9 %collective-permute-start.11 = (f32[1920,128]{1,0:T(8,128)S(1)}, f32[1920,128]{1,0:T(8,128)S(1)}, u32[]{:S(2)}, u32[]{:S(2)}) collective-permute-start(f32[1920,128]{1,0:T(8,128)S(1)} %get-tuple-element.15), channel_id=1, source_target_pairs={{1,0},{2,1},{3,2},{5,4},{6,5},{7,6},{9,8},{10,9},{11,10},{13,12},{... | collective-permute-start | bytes 2949128 | tf_op jit(solution)/shard_map/ppermute | solution.py:402
  125.4 31.7 %collective-permute-start.13 = (f32[1536,128]{1,0:T(8,128)S(1)}, f32[1536,128]{1,0:T(8,128)S(1)}, u32[]{:S(2)}, u32[]{:S(2)}) collective-permute-start(f32[1536,128]{1,0:T(8,128)S(1)} %bitcast.21), channel_id=1, source_target_pairs={{0,8},{8,16},{12,4},{16,24},{20,12},{28,20},{1,9},{9,17},{13,5},{1... | collective-permute-start | bytes 2359304 | tf_op jit(solution)/shard_map/ppermute | solution.py:392
  129.6 14.7 %collective-permute-start.16 = (f32[1024,128]{1,0:T(8,128)S(1)}, f32[1024,128]{1,0:T(8,128)S(1)}, u32[]{:S(2)}, u32[]{:S(2)}) collective-permute-start(f32[1024,128]{1,0:T(8,128)S(1)} %spread_probes.8.own), channel_id=1, source_target_pairs={{0,4},{4,0},{8,12},{12,8},{16,20},{20,16},{24,28},{28,24},{1,5},{5... | collective-permute-start | bytes 1572872 | tf_op jit(solution)/shard_map/ppermute | solution.py:387
  144.8 20.9 %collective-permute-start.20 = (f32[1024,128]{1,0:T(8,128)S(1)}, f32[1024,128]{1,0:T(8,128)S(1)}, u32[]{:S(2)}, u32[]{:S(2)}) collective-permute-start(f32[1024,128]{1,0:T(8,128)S(1)} %spread_probes.9.own), channel_id=1, source_target_pairs={{0,4},{4,0},{8,12},{12,8},{16,20},{20,16},{24,28},{28,24},{1,5},{5... | collective-permute-start | bytes 1572872 | tf_op jit(solution)/shard_map/ppermute | solution.py:387
  158.8 19.9 %collective-permute-start.14 = (f32[1920,128]{1,0:T(8,128)S(1)}, f32[1920,128]{1,0:T(8,128)S(1)}, u32[]{:S(2)}, u32[]{:S(2)}) collective-permute-start(f32[1920,128]{1,0:T(8,128)S(1)} %get-tuple-element.16), channel_id=1, source_target_pairs={{0,1},{1,2},{2,3},{4,5},{5,6},{6,7},{8,9},{9,10},{10,11},{12,13},{... | collective-permute-start | bytes 2949128 | tf_op jit(solution)/shard_map/ppermute | solution.py:397
  160.8 17.9 %collective-permute-start.15 = (f32[1920,128]{1,0:T(8,128)S(1)}, f32[1920,128]{1,0:T(8,128)S(1)}, u32[]{:S(2)}, u32[]{:S(2)}) collective-permute-start(f32[1920,128]{1,0:T(8,128)S(1)} %get-tuple-element.17), channel_id=1, source_target_pairs={{1,0},{2,1},{3,2},{5,4},{6,5},{7,6},{9,8},{10,9},{11,10},{13,12},{... | collective-permute-start | bytes 2949128 | tf_op jit(solution)/shard_map/ppermute | solution.py:402
  162.1 12.8 %collective-permute-start.17 = (f32[768,128]{1,0:T(8,128)S(1)}, f32[768,128]{1,0:T(8,128)S(1)}, u32[]{:S(2)}, u32[]{:S(2)}) collective-permute-start(f32[768,128]{1,0:T(8,128)S(1)} %bitcast.35), channel_id=1, source_target_pairs={{0,8},{8,16},{12,4},{16,24},{20,12},{28,20},{1,9},{9,17},{13,5},{1... | collective-permute-start | bytes 1179656 | tf_op jit(solution)/shard_map/ppermute | solution.py:392
  165.7 25.1 %collective-permute-start.21 = (f32[768,128]{1,0:T(8,128)S(1)}, f32[768,128]{1,0:T(8,128)S(1)}, u32[]{:S(2)}, u32[]{:S(2)}) collective-permute-start(f32[768,128]{1,0:T(8,128)S(1)} %bitcast.34), channel_id=1, source_target_pairs={{0,8},{8,16},{12,4},{16,24},{20,12},{28,20},{1,9},{9,17},{13,5},{1... | collective-permute-start | bytes 1179656 | tf_op jit(solution)/shard_map/ppermute | solution.py:392
  175.0 22.0 %collective-permute-start.18 = (f32[960,128]{1,0:T(8,128)S(1)}, f32[960,128]{1,0:T(8,128)S(1)}, u32[]{:S(2)}, u32[]{:S(2)}) collective-permute-start(f32[960,128]{1,0:T(8,128)S(1)} %get-tuple-element.18), channel_id=1, source_target_pairs={{0,1},{1,2},{2,3},{4,5},{5,6},{6,7},{8,9},{9,10},{10,11},{12,13},{... | collective-permute-start | bytes 1474568 | tf_op jit(solution)/shard_map/ppermute | solution.py:397
  177.4 19.6 %collective-permute-start.19 = (f32[960,128]{1,0:T(8,128)S(1)}, f32[960,128]{1,0:T(8,128)S(1)}, u32[]{:S(2)}, u32[]{:S(2)}) collective-permute-start(f32[960,128]{1,0:T(8,128)S(1)} %get-tuple-element.19), channel_id=1, source_target_pairs={{1,0},{2,1},{3,2},{5,4},{6,5},{7,6},{9,8},{10,9},{11,10},{13,12},{... | collective-permute-start | bytes 1474568 | tf_op jit(solution)/shard_map/ppermute | solution.py:402
  190.9 12.9 %collective-permute-start.22 = (f32[960,128]{1,0:T(8,128)S(1)}, f32[960,128]{1,0:T(8,128)S(1)}, u32[]{:S(2)}, u32[]{:S(2)}) collective-permute-start(f32[960,128]{1,0:T(8,128)S(1)} %get-tuple-element.20), channel_id=1, source_target_pairs={{0,1},{1,2},{2,3},{4,5},{5,6},{6,7},{8,9},{9,10},{10,11},{12,13},{... | collective-permute-start | bytes 1474568 | tf_op jit(solution)/shard_map/ppermute | solution.py:397
  195.5 8.3 %collective-permute-start.23 = (f32[960,128]{1,0:T(8,128)S(1)}, f32[960,128]{1,0:T(8,128)S(1)}, u32[]{:S(2)}, u32[]{:S(2)}) collective-permute-start(f32[960,128]{1,0:T(8,128)S(1)} %get-tuple-element.21), channel_id=1, source_target_pairs={{1,0},{2,1},{3,2},{5,4},{6,5},{7,6},{9,8},{10,9},{11,10},{13,12},{... | collective-permute-start | bytes 1474568 | tf_op jit(solution)/shard_map/ppermute | solution.py:402
  230.0 4.9 %collective-permute-start.28 = (f32[64,64]{1,0:T(8,128)S(1)}, f32[64,64]{1,0:T(8,128)S(1)}, u32[]{:S(2)}, u32[]{:S(2)}) collective-permute-start(f32[64,64]{1,0:T(8,128)S(1)} %add.39.a_ref), channel_id=1, source_target_pairs={{0,16},{4,20},{8,24},{12,28},{16,0},{20,4},{24,8},{28,12},{1,17},{... | collective-permute-start | bytes 49160 | tf_op jit(solution)/shard_map/ppermute | solution.py:418
  (18 other events, 163.8 us)

commit v6 on v5

--- a/solution.py
+++ b/solution.py
@@ -16,8 +16,9 @@
 DEPTH = 6
 RING = DEPTH + 1
 EDGE = 8
-GROUPS = (2, 2, 2, 1, 1)
+GROUPS = (1, 2, 2, 2, 1)
 AFTER = (None, 0, 1, 1, 2)
+BLOCK = 4
 MIB = 1 << 20
 
 
@@ -43,25 +44,20 @@
     lax.fori_loop(0, planes, plane, 0)
 
 
-def prep(probes, tile, size, after):
+def prep(probes, tile, size):
     planes, rows, depth = probes.shape[1:]
     count = planes * rows * 8
-    in_specs = [pl.BlockSpec((8, planes, rows, depth), lambda i: (tile + i, 0, 0, 0))]
-    kernel, operands = prep_kernel, [probes]
-    if after is not None:
-        in_specs.insert(0, pl.BlockSpec(memory_space=pl.ANY))
-        kernel, operands = (lambda _, *refs: prep_kernel(*refs)), [after, probes]
-    return pl.pallas_call(
-        kernel,
+    return pl.pallas_call(
+        prep_kernel,
         grid=(size,),
-        in_specs=in_specs,
+        in_specs=[pl.BlockSpec((8, planes, rows, depth), lambda i: (tile + i, 0, 0, 0))],
         out_specs=pl.BlockSpec((count, depth), lambda i: (i, 0)),
         out_shape=jax.ShapeDtypeStruct((size * count, depth), jnp.float32),
         scratch_shapes=[pltpu.VMEM((count, depth), jnp.float32)],
         compiler_params=pltpu.CompilerParams(vmem_limit_bytes=40 * MIB),
         cost_estimate=pl.CostEstimate(flops=0, bytes_accessed=size * MIB, transcendentals=0),
         name="spread_probes",
-    )(*operands)
+    )(probes)
 
 
 def pieces_of(side, tiles, planes, rows, many, own, recv, outer):
@@ -138,16 +134,19 @@
     lax.fori_loop(0, (wide_x - 2) // 2, plane, 0)
 
 
-def coefficients(side, at, totals, maps):
+def widened(side, maps, after):
     planes, rows, depth = maps[0].shape
     lower = side == 0
-    own = jnp.stack(maps)
+    own = once(jnp.stack(maps), after)
     recv = swap(own)
     outer = relay(lax.dynamic_slice_in_dim(recv, (1 - side) * (planes - RING), RING, 1))
     inner = lax.dynamic_slice_in_dim(recv, side * (planes - RING), RING, 1)
     wide = jnp.concatenate([jnp.where(lower, outer, inner), own, jnp.where(lower, inner, outer)], axis=1)
     low, high = above(wide[:, :, rows - EDGE :]), below(wide[:, :, :EDGE])
-    ext = jnp.concatenate([low, wide, high], axis=2)
+    return jnp.concatenate([low, wide, high], axis=2), recv, wide
+
+
+def coefficients(at, totals, ext):
     shape = ext.shape[1:]
     return pl.pallas_call(
         functools.partial(coef_kernel, *totals),
@@ -193,40 +192,45 @@
 
         lax.fori_loop(0, count, fill, 0)
 
-    def stencil(src, r, x, low, scale, last=None):
-        both = (x, x + 1)
-        prev = [[src[t, p, low - 1] for t in span] for p in both]
-        here = [[src[t, p, low] for t in span] for p in both]
-        cy_prev = [row(1, p, low - 1) for p in both]
+    def stencil(src, r, x, block, low, scale, last=None):
+        inner = range(block)
+        prev = [[src[t, x + k, low - 1] for t in span] for k in inner]
+        here = [[src[t, x + k, low] for t in span] for k in inner]
+        cy_prev = [row(1, x + k, low - 1) for k in inner]
         for y in range(low, wide_y - low):
-            after = [[src[t, p, y + 1] for t in span] for p in both]
-            cx = [row(0, x + k, y) for k in (-1, 0, 1)]
-            cy = [row(1, p, y) for p in both]
+            after = [[src[t, x + k, y + 1] for t in span] for k in inner]
+            cx = [row(0, x + k, y) for k in range(-1, block)]
+            cy = [row(1, x + k, y) for k in inner]
             values = []
-            for k, p in enumerate(both):
-                cz = row(2, p, y)
-                end = None if last is None else row(last, p, y)
+            for k in inner:
+                cz = row(2, x + k, y)
+                end = None if last is None else row(last, x + k, y)
                 for t in span:
                     f = here[k][t]
-                    before = src[t, x - 1, y] if k == 0 else here[0][t]
-                    beyond = here[1][t] if k == 0 else src[t, x + 2, y]
+                    before = here[k - 1][t] if k else src[t, x - 1, y]
+                    beyond = here[k + 1][t] if k + 1 < block else src[t, x + block, y]
                     total = cx[k] * before + cx[k + 1] * beyond
                     total = total + (cy_prev[k] * prev[k][t] + cy[k] * after[k][t])
                     total = total + (pltpu.roll(cz * f, 1, 1) + cz * pltpu.roll(f, depth - 1, 1))
-                    value = r[t, p, y] + scale * total
+                    value = r[t, x + k, y] + scale * total
                     values.append((t, k, value if end is None else value * end))
             yield y, values
             prev, here, cy_prev = here, after, cy
 
     def sweep(src, dst, r, low, scale, last=None):
-        def pair(i, carry):
-            x = low + 2 * i
-            for y, values in stencil(src, r, x, low, scale, last):
+        def planes_at(x, block):
+            for y, values in stencil(src, r, x, block, low, scale, last):
                 for t, k, value in values:
                     dst[t, x + k, y] = value
+
+        def step(i, carry):
+            planes_at(low + BLOCK * i, BLOCK)
             return carry
 
-        lax.fori_loop(0, (wide_x - 2 * low) // 2, pair, 0)
+        full, rest = divmod(wide_x - 2 * low, BLOCK)
+        lax.fori_loop(0, full, step, 0)
+        if rest:
+            planes_at(low + BLOCK * full, rest)
 
     sweep(r_s, a_s, r_s, 1, A3 / A2)
     sweep(a_s, b_s, r_s, 2, A2 / A1)
@@ -235,12 +239,12 @@
     sweep(b_s, r_s, a_s, 5, A2 / A1)
 
     def out(i, carry):
-        for y, values in stencil(r_s, a_s, DEPTH + 2 * i, DEPTH, A1 / A0, last=5):
+        for y, values in stencil(r_s, a_s, DEPTH + BLOCK * i, BLOCK, DEPTH, A1 / A0, last=5):
             for t, k, value in values:
-                out_ref[t, 2 * i + k, y - DEPTH] = value
+                out_ref[t, BLOCK * i + k, y - DEPTH] = value
         return carry
 
-    lax.fori_loop(0, planes // 2, out, 0)
+    lax.fori_loop(0, planes // BLOCK, out, 0)
 
 
 def solve(side, sizes, coef, *messages):
@@ -419,10 +423,14 @@
     return value, other
 
 
-def relayed(side, recv, size, planes):
+def part_to_relay(side, recv, size, planes):
     fields = recv.reshape(size, planes, -1, recv.shape[-1])
     part = lax.dynamic_slice_in_dim(fields, (1 - side) * (planes - DEPTH), DEPTH, 1)
-    return relay(part.reshape(-1, recv.shape[-1]))
+    return part.reshape(-1, recv.shape[-1])
+
+
+def once(value, after):
+    return value if after is None else lax.optimization_barrier((value, after))[0]
 
 
 def body(probes, permeability, absorption, sensitivity, observe_weight):
@@ -434,20 +442,27 @@
     at = jnp.stack([gx * planes - RING, gy * rows - EDGE]).astype(jnp.int32)
     assert 8 * sum(GROUPS) == count
 
-    groups = []
-    coef = recv = None
+    coef, parts = None, []
+    groups, low = [], None
     tile = 0
     for number, size in enumerate(GROUPS):
         sizes = (size, planes, rows, 8)
-        own = prep(probes, tile, size, recv)
+        own = once(prep(probes, tile, size), parts[-2] if len(parts) > 1 else None)
         tile += size
         recv = swap(own)
-        if coef is None:
-            coef = coefficients(side, at, totals, (permeability, absorption, sensitivity, observe_weight))
-        outer = relayed(side, recv, size, planes)
+        if number == 0:
+            ext, first, wide = widened(side, (permeability, absorption, sensitivity, observe_weight), own)
+            parts.append(first)
+        part = part_to_relay(side, once(recv, (ylo, yhi, coef) if number == 1 else low), size, planes)
+        parts.append(part)
+        outer = relay(part)
         after = AFTER[number]
-        low, high = border(flag, sizes, own, recv, outer, own if after is None else groups[after])
-        groups.append(solve(flag, sizes, coef, own, recv, outer, above(low), below(high)))
+        low, high = border(flag, sizes, own, recv, outer, wide if after is None else groups[after])
+        ylo, yhi = above(low), below(high)
+        if number == 0:
+            coef = coefficients(at, totals, once(ext, low))
+        here = coef if number == 0 else once(coef, groups[-1])
+        groups.append(solve(flag, sizes, here, own, recv, outer, ylo, yhi))
     a, b = summed(gram_of(groups, totals[0] * totals[1] * depth))
     q, r = basis(a, b, groups)
     return (q, r)

time: 246 us -> 191 us (0.78)
  waiting for transfers between devices: 83.5 us -> 38.4 us
  Pallas kernels: 75.1 us -> 64.3 us
    ppermute x6, waiting for transfers between devices: 62 us -> 8.82 us  [swap(): lax.ppermute(value, 'gx', [(i, i ^ 1) for i in range(lax.axis_size('gx'))])]
    ppermute x6, waiting for transfers between devices: 8.6 us -> 19 us  [relay(): lax.ppermute(value, 'gx', [(i, i + 2 - 4 * (i % 2)) for i in range(n) if...]
    pallas_call x5, Pallas kernels: 49.8 us -> 41 us  [solve(): pl.pallas_call(functools.partial(solve_kernel, sizes), in_specs=[smem()]...]
    ppermute x6, starting transfers between devices: 23.4 us -> 29.2 us  [above(): return lax.ppermute(value, 'gy', [(i, i + 1) for i in range(n - 1)])]
    ppermute x6, starting transfers between devices: 7.75 us -> 4.2 us  [swap(): lax.ppermute(value, 'gx', [(i, i ^ 1) for i in range(lax.axis_size('gx'))])]
    ppermute x6, waiting for transfers between devices: 3.06 us -> 0.02 us  [below(): return lax.ppermute(value, 'gy', [(i + 1, i) for i in range(n - 1)])]
    ppermute x6, starting transfers between devices: 23.1 us -> 25.6 us  [relay(): lax.ppermute(value, 'gx', [(i, i + 2 - 4 * (i % 2)) for i in range(n) if...]
  transfers between devices with their start and end apart: 29 -> 29, of which waited for: 11 -> 11; matrix products, arithmetic and copies ran while one was open for 3% -> 4% of each run, Pallas kernels for 22% -> 23%
where the time goes in v6:
time: 191 us; the launch traced here: 190 us
  starting transfers between devices  76.3 us (40%)
  Pallas kernels  64.3 us (34%)
  waiting for transfers between devices  38.4 us (20%)
  local copies, waits for them, and re-layouts  6.62 us (3%)
  other arithmetic  3.59 us (2%)
    pallas_call x5, Pallas kernels, solve(): pl.pallas_call(functools.partial(solve_kernel, sizes), in_specs=[smem()]...  41 us
    ppermute x6, starting transfers between devices, above(): return lax.ppermute(value, 'gy', [(i, i + 1) for i in range(n - 1)])  29.2 us
    ppermute x6, starting transfers between devices, relay(): lax.ppermute(value, 'gx', [(i, i + 2 - 4 * (i % 2)) for i in range(n) if...  25.6 us
    ppermute x6, waiting for transfers between devices, relay(): lax.ppermute(value, 'gx', [(i, i + 2 - 4 * (i % 2)) for i in range(n) if...  19 us
    ppermute x5, waiting for transfers between devices, summed(): other = lax.ppermute(value, axis, [(i, i ^ shift) for i in range(n)])  10.6 us
    pallas_call x1, Pallas kernels, basis(): pl.pallas_call(basis_kernel, grid=(planes,), in_specs=[full, full] + tile...  10.3 us
    ppermute x5, starting transfers between devices, summed(): other = lax.ppermute(value, axis, [(i, i ^ shift) for i in range(n)])  9.53 us
    ppermute x6, waiting for transfers between devices, swap(): lax.ppermute(value, 'gx', [(i, i ^ 1) for i in range(lax.axis_size('gx'))])  8.82 us
  transfers between devices with their start and end apart: 29, of which 11 were waited for; matrix products, arithmetic and copies ran while one was open for 4% of the time, Pallas kernels for 23%

profile of v6, /device:TPU:0, one launch (start us, length us, event | category | flops | bytes accessed | tf_op | source)
XLA Modules:
  0.0 190.3 jit_solution(10862948558411354634)
XLA Ops:
  3.5 3.0 %collective-permute-start = (f32[4,8,16,128]{3,2,1,0:T(8,128)S(1)}, f32[4,8,16,128]{3,2,1,0:T(8,128)S(1)}, u32[]{:S(2)}, u32[]{:S(2)}) collective-permute-start(f32[4,8,16,128]{3,2,1,0:T(8,128)S(1)} %pad_maximum_fusion.2), channel_id=1, source_target_pairs={{0,4},{4,0},{8,12},{12,8},{16,20},{20,16},{24,28},{28,24},{1,5},{5... | collective-permute-start | bytes 786440 | tf_op jit(solution)/shard_map/ppermute | solution.py:391
  6.6 7.1 %collective-permute-done = f32[4,8,16,128]{3,2,1,0:T(8,128)S(1)} collective-permute-done((f32[4,8,16,128]{3,2,1,0:T(8,128)S(1)}, f32[4,8,16,128]{3,2,1,0:T(8,128)S(1)}, u32[]{:S(2)}, u32[]{:S(2)}) %collective-permute-start) | collective-permute-done | bytes 262176 | tf_op jit(solution)/shard_map/ppermute | solution.py:391
  14.3 4.7 %collective-permute-start.1 = (f32[4,7,16,128]{3,2,1,0:T(8,128)}, f32[4,7,16,128]{3,2,1,0:T(8,128)}, u32[]{:S(2)}, u32[]{:S(2)}) collective-permute-start(f32[4,7,16,128]{3,2,1,0:T(8,128)} %constant_dynamic-slice_fusion.5), channel_id=1, source_target_pairs={{0,8},{8,16},{12,4},{16,24},{20,12},{28,20},{1,9},{9,17},{13,5},{1... | collective-permute-start | bytes 688136 | tf_op jit(solution)/shard_map/ppermute | solution.py:396
  26.0 4.1 %collective-permute-start.5 = (f32[768,128]{1,0:T(8,128)S(1)}, f32[768,128]{1,0:T(8,128)S(1)}, u32[]{:S(2)}, u32[]{:S(2)}) collective-permute-start(f32[768,128]{1,0:T(8,128)S(1)} %bitcast.24), channel_id=1, source_target_pairs={{0,8},{8,16},{12,4},{16,24},{20,12},{28,20},{1,9},{9,17},{13,5},{1... | collective-permute-start | bytes 1179656 | tf_op jit(solution)/shard_map/ppermute | solution.py:396
  33.3 3.8 %collective-permute-start.2 = (f32[4,22,8,128]{3,2,1,0:T(8,128)}, f32[4,22,8,128]{3,2,1,0:T(8,128)}, u32[]{:S(2)}, u32[]{:S(2)}) collective-permute-start(f32[4,22,8,128]{3,2,1,0:T(8,128)} %get-tuple-element.50), channel_id=1, source_target_pairs={{0,1},{1,2},{2,3},{4,5},{5,6},{6,7},{8,9},{9,10},{10,11},{12,13},{... | collective-permute-start | bytes 1081352 | tf_op jit(solution)/shard_map/ppermute | solution.py:401
  39.4 3.1 %collective-permute-start.6 = (f32[960,128]{1,0:T(8,128)}, f32[960,128]{1,0:T(8,128)}, u32[]{:S(2)}, u32[]{:S(2)}) collective-permute-start(f32[960,128]{1,0:T(8,128)} %get-tuple-element.27), channel_id=1, source_target_pairs={{0,1},{1,2},{2,3},{4,5},{5,6},{6,7},{8,9},{9,10},{10,11},{12,13},{... | collective-permute-start | bytes 1474568 | tf_op jit(solution)/shard_map/ppermute | solution.py:401
  51.4 3.5 %collective-permute-start.9 = (f32[1536,128]{1,0:T(8,128)S(1)}, f32[1536,128]{1,0:T(8,128)S(1)}, u32[]{:S(2)}, u32[]{:S(2)}) collective-permute-start(f32[1536,128]{1,0:T(8,128)S(1)} %bitcast.22), channel_id=1, source_target_pairs={{0,8},{8,16},{12,4},{16,24},{20,12},{28,20},{1,9},{9,17},{13,5},{1... | collective-permute-start | bytes 2359304 | tf_op jit(solution)/shard_map/ppermute | solution.py:396
  55.8 6.9 %both_solves.5.after.refs_0_ = f32[1,8,16,8,128]{4,3,2,1,0:T(8,128)S(1)} custom-call(s32[1]{0:T(128)} %bitcast.h_ref, f32[6,22,32,128]{3,2,1,0:T(8,128)S(1)} %coefficients.1.coef, f32[1024,128]{1,0:T(8,128)} %spread_probes.5.own, f32[1024,128]{1,0:T(8,128)} %collective-permute-done.4.recv, f32[768,128]{1,0:T(8,128)S(1)} %collective-permute-done.5.outer, ...), custom_call_target="tpu_custom_call" | custom-call | flops 34406400 | bytes 12582912 | tf_op jit(solution)/shard_map/both_solves/pallas_call | solution.py:256
  62.7 7.5 %collective-permute-done.9.outer = f32[1536,128]{1,0:T(8,128)S(1)} collective-permute-done((f32[1536,128]{1,0:T(8,128)S(1)}, f32[1536,128]{1,0:T(8,128)S(1)}, u32[]{:S(2)}, u32[]{:S(2)}) %collective-permute-start.9) | collective-permute-done | bytes 786464 | tf_op jit(solution)/shard_map/ppermute | solution.py:396
  71.6 4.7 %collective-permute-start.10 = (f32[1920,128]{1,0:T(8,128)S(1)}, f32[1920,128]{1,0:T(8,128)S(1)}, u32[]{:S(2)}, u32[]{:S(2)}) collective-permute-start(f32[1920,128]{1,0:T(8,128)S(1)} %get-tuple-element.33), channel_id=1, source_target_pairs={{0,1},{1,2},{2,3},{4,5},{5,6},{6,7},{8,9},{9,10},{10,11},{12,13},{... | collective-permute-start | bytes 2949128 | tf_op jit(solution)/shard_map/ppermute | solution.py:401
  77.6 4.6 %collective-permute-start.13 = (f32[1536,128]{1,0:T(8,128)S(1)}, f32[1536,128]{1,0:T(8,128)S(1)}, u32[]{:S(2)}, u32[]{:S(2)}) collective-permute-start(f32[1536,128]{1,0:T(8,128)S(1)} %bitcast.20), channel_id=1, source_target_pairs={{0,8},{8,16},{12,4},{16,24},{20,12},{28,20},{1,9},{9,17},{13,5},{1... | collective-permute-start | bytes 2359304 | tf_op jit(solution)/shard_map/ppermute | solution.py:396
  82.2 10.4 %both_solves.6.after.refs_1_.refs_2_ = f32[2,8,16,8,128]{4,3,2,1,0:T(8,128)S(1)} custom-call(s32[1]{0:T(128)} %bitcast.h_ref, f32[6,22,32,128]{3,2,1,0:T(8,128)S(1)} %coefficients.1.coef, f32[2048,128]{1,0:T(8,128)S(1)} %spread_probes.6.own, f32[2048,128]{1,0:T(8,128)} %collective-permute-done.8.recv, f32[1536,128]{1,0:T(8,128)S(1)} %collective-permute-done.9.outer, ...), custom_call_target="tpu_custom_call" | custom-call | flops 68812800 | bytes 12582912 | tf_op jit(solution)/shard_map/both_solves/pallas_call | solution.py:256
  92.6 5.8 %collective-permute-done.13.outer = f32[1536,128]{1,0:T(8,128)S(1)} collective-permute-done((f32[1536,128]{1,0:T(8,128)S(1)}, f32[1536,128]{1,0:T(8,128)S(1)}, u32[]{:S(2)}, u32[]{:S(2)}) %collective-permute-start.13) | collective-permute-done | bytes 786464 | tf_op jit(solution)/shard_map/ppermute | solution.py:396
  98.6 4.4 %collective-permute-start.17 = (f32[1536,128]{1,0:T(8,128)S(1)}, f32[1536,128]{1,0:T(8,128)S(1)}, u32[]{:S(2)}, u32[]{:S(2)}) collective-permute-start(f32[1536,128]{1,0:T(8,128)S(1)} %bitcast.21), channel_id=1, source_target_pairs={{0,8},{8,16},{12,4},{16,24},{20,12},{28,20},{1,9},{9,17},{13,5},{1... | collective-permute-start | bytes 2359304 | tf_op jit(solution)/shard_map/ppermute | solution.py:396
  103.8 7.3 %collective-permute-start.14 = (f32[1920,128]{1,0:T(8,128)S(1)}, f32[1920,128]{1,0:T(8,128)S(1)}, u32[]{:S(2)}, u32[]{:S(2)}) collective-permute-start(f32[1920,128]{1,0:T(8,128)S(1)} %get-tuple-element.38), channel_id=1, source_target_pairs={{0,1},{1,2},{2,3},{4,5},{5,6},{6,7},{8,9},{9,10},{10,11},{12,13},{... | collective-permute-start | bytes 2949128 | tf_op jit(solution)/shard_map/ppermute | solution.py:401
  112.4 3.5 %collective-permute-done.17.outer = f32[1536,128]{1,0:T(8,128)S(1)} collective-permute-done((f32[1536,128]{1,0:T(8,128)S(1)}, f32[1536,128]{1,0:T(8,128)S(1)}, u32[]{:S(2)}, u32[]{:S(2)}) %collective-permute-start.17) | collective-permute-done | bytes 786464 | tf_op jit(solution)/shard_map/ppermute | solution.py:396
  116.1 7.1 %collective-permute-start.18 = (f32[1920,128]{1,0:T(8,128)S(1)}, f32[1920,128]{1,0:T(8,128)S(1)}, u32[]{:S(2)}, u32[]{:S(2)}) collective-permute-start(f32[1920,128]{1,0:T(8,128)S(1)} %get-tuple-element.43), channel_id=1, source_target_pairs={{0,1},{1,2},{2,3},{4,5},{5,6},{6,7},{8,9},{9,10},{10,11},{12,13},{... | collective-permute-start | bytes 2949128 | tf_op jit(solution)/shard_map/ppermute | solution.py:401
  124.5 4.3 %collective-permute-start.21 = (f32[768,128]{1,0:T(8,128)S(1)}, f32[768,128]{1,0:T(8,128)S(1)}, u32[]{:S(2)}, u32[]{:S(2)}) collective-permute-start(f32[768,128]{1,0:T(8,128)S(1)} %bitcast.23), channel_id=1, source_target_pairs={{0,8},{8,16},{12,4},{16,24},{20,12},{28,20},{1,9},{9,17},{13,5},{1... | collective-permute-start | bytes 1179656 | tf_op jit(solution)/shard_map/ppermute | solution.py:396
  128.8 9.2 %both_solves.7.after.refs_3_.refs_4_ = f32[2,8,16,8,128]{4,3,2,1,0:T(8,128)S(1)} custom-call(s32[1]{0:T(128)} %bitcast.h_ref, f32[6,22,32,128]{3,2,1,0:T(8,128)S(1)} %coefficients.1.coef, f32[2048,128]{1,0:T(8,128)S(1)} %copy-done.3, f32[2048,128]{1,0:T(8,128)S(1)} %collective-permute-done.12.recv, f32[1536,128]{1,0:T(8,128)S(1)} %collective-permute-done.13.outer, ...), custom_call_target="tpu_custom_call" | custom-call | flops 68812800 | bytes 12582912 | tf_op jit(solution)/shard_map/both_solves/pallas_call | solution.py:256
  138.1 3.2 %collective-permute-start.22 = (f32[960,128]{1,0:T(8,128)S(1)}, f32[960,128]{1,0:T(8,128)S(1)}, u32[]{:S(2)}, u32[]{:S(2)}) collective-permute-start(f32[960,128]{1,0:T(8,128)S(1)} %get-tuple-element.48), channel_id=1, source_target_pairs={{0,1},{1,2},{2,3},{4,5},{5,6},{6,7},{8,9},{9,10},{10,11},{12,13},{... | collective-permute-start | bytes 1474568 | tf_op jit(solution)/shard_map/ppermute | solution.py:401
  142.6 9.2 %both_solves.8.refs_5_.refs_6_ = f32[2,8,16,8,128]{4,3,2,1,0:T(8,128)S(1)} custom-call(s32[1]{0:T(128)} %bitcast.h_ref, f32[6,22,32,128]{3,2,1,0:T(8,128)S(1)} %coefficients.1.coef, f32[2048,128]{1,0:T(8,128)S(1)} %spread_probes.8.own, f32[2048,128]{1,0:T(8,128)S(1)} %collective-permute-done.16.recv, f32[1536,128]{1,0:T(8,128)S(1)} %collective-permute-done.17.outer, ...), custom_call_target="tpu_custom_call" | custom-call | flops 68812800 | bytes 12582912 | tf_op jit(solution)/shard_map/both_solves/pallas_call | solution.py:256
  151.8 5.4 %both_solves.9.refs_7_ = f32[1,8,16,8,128]{4,3,2,1,0:T(8,128)S(1)} custom-call(s32[1]{0:T(128)} %bitcast.h_ref, f32[6,22,32,128]{3,2,1,0:T(8,128)S(1)} %coefficients.1.coef, f32[1024,128]{1,0:T(8,128)S(1)} %spread_probes.9.own, f32[1024,128]{1,0:T(8,128)S(1)} %collective-permute-done.20.recv, f32[768,128]{1,0:T(8,128)S(1)} %collective-permute-done.21.outer, ...), custom_call_target="tpu_custom_call" | custom-call | flops 34406400 | bytes 12582912 | tf_op jit(solution)/shard_map/both_solves/pallas_call | solution.py:256
  168.0 3.2 %collective-permute-done.26 = f32[64,64]{1,0:T(8,128)S(1)} collective-permute-done((f32[64,64]{1,0:T(8,128)S(1)}, f32[64,64]{1,0:T(8,128)S(1)}, u32[]{:S(2)}, u32[]{:S(2)}) %collective-permute-start.26) | collective-permute-done | bytes 16416 | tf_op jit(solution)/shard_map/ppermute | solution.py:422
  180.0 10.3 %basis.1 = (f32[64,8,16,128]{3,2,1,0:T(8,128)}, f32[64,64]{1,0:T(8,128)}) custom-call(f32[64,64]{1,0:T(8,128)S(1)} %add.39.a_ref, f32[64,64]{1,0:T(8,128)S(1)} %collective-permute-done.28.b_ref, f32[1,8,16,8,128]{4,3,2,1,0:T(8,128)S(1)} %both_solves.5.after.refs_0_, f32[2,8,16,8,128]{4,3,2,1,0:T(8,128)S(1)} %both_solves.6.after.refs_1_.refs_2_, ...), custom_call_target="tpu_custom_call" | custom-call | bytes 8388608 | tf_op jit(solution)/shard_map/basis/pallas_call | solution.py:374
  (90 shorter events, 53.0 us)
Async XLA Ops:
  3.5 10.1 %collective-permute-start = (f32[4,8,16,128]{3,2,1,0:T(8,128)S(1)}, f32[4,8,16,128]{3,2,1,0:T(8,128)S(1)}, u32[]{:S(2)}, u32[]{:S(2)}) collective-permute-start(f32[4,8,16,128]{3,2,1,0:T(8,128)S(1)} %pad_maximum_fusion.2), channel_id=1, source_target_pairs={{0,4},{4,0},{8,12},{12,8},{16,20},{20,16},{24,28},{28,24},{1,5},{5... | collective-permute-start | bytes 786440 | tf_op jit(solution)/shard_map/ppermute | solution.py:391
  6.5 18.5 %collective-permute-start.4 = (f32[1024,128]{1,0:T(8,128)}, f32[1024,128]{1,0:T(8,128)}, u32[]{:S(2)}, u32[]{:S(2)}) collective-permute-start(f32[1024,128]{1,0:T(8,128)} %spread_probes.5.own), channel_id=1, source_target_pairs={{0,4},{4,0},{8,12},{12,8},{16,20},{20,16},{24,28},{28,24},{1,5},{5... | collective-permute-start | bytes 1572872 | tf_op jit(solution)/shard_map/ppermute | solution.py:391
  14.3 7.9 %collective-permute-start.1 = (f32[4,7,16,128]{3,2,1,0:T(8,128)}, f32[4,7,16,128]{3,2,1,0:T(8,128)}, u32[]{:S(2)}, u32[]{:S(2)}) collective-permute-start(f32[4,7,16,128]{3,2,1,0:T(8,128)} %constant_dynamic-slice_fusion.5), channel_id=1, source_target_pairs={{0,8},{8,16},{12,4},{16,24},{20,12},{28,20},{1,9},{9,17},{13,5},{1... | collective-permute-start | bytes 688136 | tf_op jit(solution)/shard_map/ppermute | solution.py:396
  19.9 30.3 %collective-permute-start.8 = (f32[2048,128]{1,0:T(8,128)S(1)}, f32[2048,128]{1,0:T(8,128)}, u32[]{:S(2)}, u32[]{:S(2)}) collective-permute-start(f32[2048,128]{1,0:T(8,128)S(1)} %spread_probes.6.own), channel_id=1, source_target_pairs={{0,4},{4,0},{8,12},{12,8},{16,20},{20,16},{24,28},{28,24},{1,5},{5... | collective-permute-start | bytes 3145736 | tf_op jit(solution)/shard_map/ppermute | solution.py:391
  26.0 11.1 %collective-permute-start.5 = (f32[768,128]{1,0:T(8,128)S(1)}, f32[768,128]{1,0:T(8,128)S(1)}, u32[]{:S(2)}, u32[]{:S(2)}) collective-permute-start(f32[768,128]{1,0:T(8,128)S(1)} %bitcast.24), channel_id=1, source_target_pairs={{0,8},{8,16},{12,4},{16,24},{20,12},{28,20},{1,9},{9,17},{13,5},{1... | collective-permute-start | bytes 1179656 | tf_op jit(solution)/shard_map/ppermute | solution.py:396
  32.1 13.6 %collective-permute-start.3 = (f32[4,22,8,128]{3,2,1,0:T(8,128)}, f32[4,22,8,128]{3,2,1,0:T(8,128)}, u32[]{:S(2)}, u32[]{:S(2)}) collective-permute-start(f32[4,22,8,128]{3,2,1,0:T(8,128)} %get-tuple-element.51), channel_id=1, source_target_pairs={{1,0},{2,1},{3,2},{5,4},{6,5},{7,6},{9,8},{10,9},{11,10},{13,12},{... | collective-permute-start | bytes 1081352 | tf_op jit(solution)/shard_map/ppermute | solution.py:406
  33.3 12.9 %collective-permute-start.2 = (f32[4,22,8,128]{3,2,1,0:T(8,128)}, f32[4,22,8,128]{3,2,1,0:T(8,128)}, u32[]{:S(2)}, u32[]{:S(2)}) collective-permute-start(f32[4,22,8,128]{3,2,1,0:T(8,128)} %get-tuple-element.50), channel_id=1, source_target_pairs={{0,1},{1,2},{2,3},{4,5},{5,6},{6,7},{8,9},{9,10},{10,11},{12,13},{... | collective-permute-start | bytes 1081352 | tf_op jit(solution)/shard_map/ppermute | solution.py:401
  39.4 10.8 %collective-permute-start.6 = (f32[960,128]{1,0:T(8,128)}, f32[960,128]{1,0:T(8,128)}, u32[]{:S(2)}, u32[]{:S(2)}) collective-permute-start(f32[960,128]{1,0:T(8,128)} %get-tuple-element.27), channel_id=1, source_target_pairs={{0,1},{1,2},{2,3},{4,5},{5,6},{6,7},{8,9},{9,10},{10,11},{12,13},{... | collective-permute-start | bytes 1474568 | tf_op jit(solution)/shard_map/ppermute | solution.py:401
  42.5 7.7 %collective-permute-start.7 = (f32[960,128]{1,0:T(8,128)}, f32[960,128]{1,0:T(8,128)}, u32[]{:S(2)}, u32[]{:S(2)}) collective-permute-start(f32[960,128]{1,0:T(8,128)} %get-tuple-element.29), channel_id=1, source_target_pairs={{1,0},{2,1},{3,2},{5,4},{6,5},{7,6},{9,8},{10,9},{11,10},{13,12},{... | collective-permute-start | bytes 1474568 | tf_op jit(solution)/shard_map/ppermute | solution.py:406
  45.6 31.9 %collective-permute-start.12 = (f32[2048,128]{1,0:T(8,128)}, f32[2048,128]{1,0:T(8,128)S(1)}, u32[]{:S(2)}, u32[]{:S(2)}) collective-permute-start(f32[2048,128]{1,0:T(8,128)} %copy-done.2), channel_id=1, source_target_pairs={{0,4},{4,0},{8,12},{12,8},{16,20},{20,16},{24,28},{28,24},{1,5},{5... | collective-permute-start | bytes 3145736 | tf_op jit(solution)/shard_map/ppermute | solution.py:391
  51.4 18.8 %collective-permute-start.9 = (f32[1536,128]{1,0:T(8,128)S(1)}, f32[1536,128]{1,0:T(8,128)S(1)}, u32[]{:S(2)}, u32[]{:S(2)}) collective-permute-start(f32[1536,128]{1,0:T(8,128)S(1)} %bitcast.22), channel_id=1, source_target_pairs={{0,8},{8,16},{12,4},{16,24},{20,12},{28,20},{1,9},{9,17},{13,5},{1... | collective-permute-start | bytes 2359304 | tf_op jit(solution)/shard_map/ppermute | solution.py:396
  55.8 42.8 %collective-permute-start.16 = (f32[2048,128]{1,0:T(8,128)S(1)}, f32[2048,128]{1,0:T(8,128)S(1)}, u32[]{:S(2)}, u32[]{:S(2)}) collective-permute-start(f32[2048,128]{1,0:T(8,128)S(1)} %spread_probes.8.own), channel_id=1, source_target_pairs={{0,4},{4,0},{8,12},{12,8},{16,20},{20,16},{24,28},{28,24},{1,5},{5... | collective-permute-start | bytes 3145736 | tf_op jit(solution)/shard_map/ppermute | solution.py:391
  71.6 10.7 %collective-permute-start.10 = (f32[1920,128]{1,0:T(8,128)S(1)}, f32[1920,128]{1,0:T(8,128)S(1)}, u32[]{:S(2)}, u32[]{:S(2)}) collective-permute-start(f32[1920,128]{1,0:T(8,128)S(1)} %get-tuple-element.33), channel_id=1, source_target_pairs={{0,1},{1,2},{2,3},{4,5},{5,6},{6,7},{8,9},{9,10},{10,11},{12,13},{... | collective-permute-start | bytes 2949128 | tf_op jit(solution)/shard_map/ppermute | solution.py:401
  76.2 6.0 %collective-permute-start.11 = (f32[1920,128]{1,0:T(8,128)S(1)}, f32[1920,128]{1,0:T(8,128)S(1)}, u32[]{:S(2)}, u32[]{:S(2)}) collective-permute-start(f32[1920,128]{1,0:T(8,128)S(1)} %get-tuple-element.34), channel_id=1, source_target_pairs={{1,0},{2,1},{3,2},{5,4},{6,5},{7,6},{9,8},{10,9},{11,10},{13,12},{... | collective-permute-start | bytes 2949128 | tf_op jit(solution)/shard_map/ppermute | solution.py:406
  77.6 20.8 %collective-permute-start.13 = (f32[1536,128]{1,0:T(8,128)S(1)}, f32[1536,128]{1,0:T(8,128)S(1)}, u32[]{:S(2)}, u32[]{:S(2)}) collective-permute-start(f32[1536,128]{1,0:T(8,128)S(1)} %bitcast.20), channel_id=1, source_target_pairs={{0,8},{8,16},{12,4},{16,24},{20,12},{28,20},{1,9},{9,17},{13,5},{1... | collective-permute-start | bytes 2359304 | tf_op jit(solution)/shard_map/ppermute | solution.py:396
  98.6 17.3 %collective-permute-start.17 = (f32[1536,128]{1,0:T(8,128)S(1)}, f32[1536,128]{1,0:T(8,128)S(1)}, u32[]{:S(2)}, u32[]{:S(2)}) collective-permute-start(f32[1536,128]{1,0:T(8,128)S(1)} %bitcast.21), channel_id=1, source_target_pairs={{0,8},{8,16},{12,4},{16,24},{20,12},{28,20},{1,9},{9,17},{13,5},{1... | collective-permute-start | bytes 2359304 | tf_op jit(solution)/shard_map/ppermute | solution.py:396
  103.5 21.0 %collective-permute-start.20 = (f32[1024,128]{1,0:T(8,128)S(1)}, f32[1024,128]{1,0:T(8,128)S(1)}, u32[]{:S(2)}, u32[]{:S(2)}) collective-permute-start(f32[1024,128]{1,0:T(8,128)S(1)} %spread_probes.9.own), channel_id=1, source_target_pairs={{0,4},{4,0},{8,12},{12,8},{16,20},{20,16},{24,28},{28,24},{1,5},{5... | collective-permute-start | bytes 1572872 | tf_op jit(solution)/shard_map/ppermute | solution.py:391
  103.8 25.0 %collective-permute-start.14 = (f32[1920,128]{1,0:T(8,128)S(1)}, f32[1920,128]{1,0:T(8,128)S(1)}, u32[]{:S(2)}, u32[]{:S(2)}) collective-permute-start(f32[1920,128]{1,0:T(8,128)S(1)} %get-tuple-element.38), channel_id=1, source_target_pairs={{0,1},{1,2},{2,3},{4,5},{5,6},{6,7},{8,9},{9,10},{10,11},{12,13},{... | collective-permute-start | bytes 2949128 | tf_op jit(solution)/shard_map/ppermute | solution.py:401
  111.1 17.7 %collective-permute-start.15 = (f32[1920,128]{1,0:T(8,128)S(1)}, f32[1920,128]{1,0:T(8,128)S(1)}, u32[]{:S(2)}, u32[]{:S(2)}) collective-permute-start(f32[1920,128]{1,0:T(8,128)S(1)} %get-tuple-element.39), channel_id=1, source_target_pairs={{1,0},{2,1},{3,2},{5,4},{6,5},{7,6},{9,8},{10,9},{11,10},{13,12},{... | collective-permute-start | bytes 2949128 | tf_op jit(solution)/shard_map/ppermute | solution.py:406
  116.1 26.5 %collective-permute-start.18 = (f32[1920,128]{1,0:T(8,128)S(1)}, f32[1920,128]{1,0:T(8,128)S(1)}, u32[]{:S(2)}, u32[]{:S(2)}) collective-permute-start(f32[1920,128]{1,0:T(8,128)S(1)} %get-tuple-element.43), channel_id=1, source_target_pairs={{0,1},{1,2},{2,3},{4,5},{5,6},{6,7},{8,9},{9,10},{10,11},{12,13},{... | collective-permute-start | bytes 2949128 | tf_op jit(solution)/shard_map/ppermute | solution.py:401
  123.1 19.4 %collective-permute-start.19 = (f32[1920,128]{1,0:T(8,128)S(1)}, f32[1920,128]{1,0:T(8,128)S(1)}, u32[]{:S(2)}, u32[]{:S(2)}) collective-permute-start(f32[1920,128]{1,0:T(8,128)S(1)} %get-tuple-element.44), channel_id=1, source_target_pairs={{1,0},{2,1},{3,2},{5,4},{6,5},{7,6},{9,8},{10,9},{11,10},{13,12},{... | collective-permute-start | bytes 2949128 | tf_op jit(solution)/shard_map/ppermute | solution.py:406
  124.5 13.5 %collective-permute-start.21 = (f32[768,128]{1,0:T(8,128)S(1)}, f32[768,128]{1,0:T(8,128)S(1)}, u32[]{:S(2)}, u32[]{:S(2)}) collective-permute-start(f32[768,128]{1,0:T(8,128)S(1)} %bitcast.23), channel_id=1, source_target_pairs={{0,8},{8,16},{12,4},{16,24},{20,12},{28,20},{1,9},{9,17},{13,5},{1... | collective-permute-start | bytes 1179656 | tf_op jit(solution)/shard_map/ppermute | solution.py:396
  138.1 13.7 %collective-permute-start.22 = (f32[960,128]{1,0:T(8,128)S(1)}, f32[960,128]{1,0:T(8,128)S(1)}, u32[]{:S(2)}, u32[]{:S(2)}) collective-permute-start(f32[960,128]{1,0:T(8,128)S(1)} %get-tuple-element.48), channel_id=1, source_target_pairs={{0,1},{1,2},{2,3},{4,5},{5,6},{6,7},{8,9},{9,10},{10,11},{12,13},{... | collective-permute-start | bytes 1474568 | tf_op jit(solution)/shard_map/ppermute | solution.py:401
  141.3 10.5 %collective-permute-start.23 = (f32[960,128]{1,0:T(8,128)S(1)}, f32[960,128]{1,0:T(8,128)S(1)}, u32[]{:S(2)}, u32[]{:S(2)}) collective-permute-start(f32[960,128]{1,0:T(8,128)S(1)} %get-tuple-element.49), channel_id=1, source_target_pairs={{1,0},{2,1},{3,2},{5,4},{6,5},{7,6},{9,8},{10,9},{11,10},{13,12},{... | collective-permute-start | bytes 1474568 | tf_op jit(solution)/shard_map/ppermute | solution.py:406
  (16 other events, 98.4 us)

commit v7 on v6

--- a/solution.py
+++ b/solution.py
@@ -443,7 +443,7 @@
     assert 8 * sum(GROUPS) == count
 
     coef, parts = None, []
-    groups, low = [], None
+    groups, low, ylo, yhi = [], None, None, None
     tile = 0
     for number, size in enumerate(GROUPS):
         sizes = (size, planes, rows, 8)
@@ -453,7 +453,8 @@
         if number == 0:
             ext, first, wide = widened(side, (permeability, absorption, sensitivity, observe_weight), own)
             parts.append(first)
-        part = part_to_relay(side, once(recv, (ylo, yhi, coef) if number == 1 else low), size, planes)
+        before = {1: (ylo, yhi, coef), 3: groups[1] if number == 3 else None}.get(number, low)
+        part = part_to_relay(side, once(recv, before), size, planes)
         parts.append(part)
         outer = relay(part)
         after = AFTER[number]

time: 191 us -> 189 us (0.990)
    ppermute x6, waiting for transfers between devices: 19 us -> 9.7 us  [relay(): lax.ppermute(value, 'gx', [(i, i + 2 - 4 * (i % 2)) for i in range(n) if...]
    ppermute x6, waiting for transfers between devices: 8.82 us -> 16.1 us  [swap(): lax.ppermute(value, 'gx', [(i, i ^ 1) for i in range(lax.axis_size('gx'))])]
  transfers between devices with their start and end apart: 29 -> 29, of which waited for: 11 -> 11; matrix products, arithmetic and copies ran while one was open for 4% -> 3% of each run, Pallas kernels for 23% -> 24%
where the time goes in v7:
time: 189 us; the launch traced here: 188 us
  starting transfers between devices  75.1 us (40%)
  Pallas kernels  64.3 us (34%)
  waiting for transfers between devices  38.3 us (20%)
  local copies, waits for them, and re-layouts  5.61 us (3%)
  other arithmetic  3.59 us (2%)
    pallas_call x5, Pallas kernels, solve(): pl.pallas_call(functools.partial(solve_kernel, sizes), in_specs=[smem()]...  41 us
    ppermute x6, starting transfers between devices, above(): return lax.ppermute(value, 'gy', [(i, i + 1) for i in range(n - 1)])  29.8 us
    ppermute x6, starting transfers between devices, relay(): lax.ppermute(value, 'gx', [(i, i + 2 - 4 * (i % 2)) for i in range(n) if...  24.5 us
    ppermute x6, waiting for transfers between devices, swap(): lax.ppermute(value, 'gx', [(i, i ^ 1) for i in range(lax.axis_size('gx'))])  16.1 us
    ppermute x5, waiting for transfers between devices, summed(): other = lax.ppermute(value, axis, [(i, i ^ shift) for i in range(n)])  12.5 us
    pallas_call x1, Pallas kernels, basis(): pl.pallas_call(basis_kernel, grid=(planes,), in_specs=[full, full] + tile...  10.3 us
    ppermute x6, waiting for transfers between devices, relay(): lax.ppermute(value, 'gx', [(i, i + 2 - 4 * (i % 2)) for i in range(n) if...  9.7 us
    ppermute x6, starting transfers between devices, below(): return lax.ppermute(value, 'gy', [(i + 1, i) for i in range(n - 1)])  7.73 us
  transfers between devices with their start and end apart: 29, of which 11 were waited for; matrix products, arithmetic and copies ran while one was open for 3% of the time, Pallas kernels for 24%

profile of v7, /device:TPU:0, one launch (start us, length us, event | category | flops | bytes accessed | tf_op | source)
XLA Modules:
  0.0 188.0 jit_solution(13318094035089458360)
XLA Ops:
  3.5 3.0 %collective-permute-start = (f32[4,8,16,128]{3,2,1,0:T(8,128)S(1)}, f32[4,8,16,128]{3,2,1,0:T(8,128)S(1)}, u32[]{:S(2)}, u32[]{:S(2)}) collective-permute-start(f32[4,8,16,128]{3,2,1,0:T(8,128)S(1)} %pad_maximum_fusion.2), channel_id=1, source_target_pairs={{0,4},{4,0},{8,12},{12,8},{16,20},{20,16},{24,28},{28,24},{1,5},{5... | collective-permute-start | bytes 786440 | tf_op jit(solution)/shard_map/ppermute | solution.py:391
  6.6 7.1 %collective-permute-done = f32[4,8,16,128]{3,2,1,0:T(8,128)S(1)} collective-permute-done((f32[4,8,16,128]{3,2,1,0:T(8,128)S(1)}, f32[4,8,16,128]{3,2,1,0:T(8,128)S(1)}, u32[]{:S(2)}, u32[]{:S(2)}) %collective-permute-start) | collective-permute-done | bytes 262176 | tf_op jit(solution)/shard_map/ppermute | solution.py:391
  14.3 4.7 %collective-permute-start.1 = (f32[4,7,16,128]{3,2,1,0:T(8,128)}, f32[4,7,16,128]{3,2,1,0:T(8,128)}, u32[]{:S(2)}, u32[]{:S(2)}) collective-permute-start(f32[4,7,16,128]{3,2,1,0:T(8,128)} %constant_dynamic-slice_fusion.5), channel_id=1, source_target_pairs={{0,8},{8,16},{12,4},{16,24},{20,12},{28,20},{1,9},{9,17},{13,5},{1... | collective-permute-start | bytes 688136 | tf_op jit(solution)/shard_map/ppermute | solution.py:396
  26.0 4.1 %collective-permute-start.5 = (f32[768,128]{1,0:T(8,128)S(1)}, f32[768,128]{1,0:T(8,128)S(1)}, u32[]{:S(2)}, u32[]{:S(2)}) collective-permute-start(f32[768,128]{1,0:T(8,128)S(1)} %bitcast.24), channel_id=1, source_target_pairs={{0,8},{8,16},{12,4},{16,24},{20,12},{28,20},{1,9},{9,17},{13,5},{1... | collective-permute-start | bytes 1179656 | tf_op jit(solution)/shard_map/ppermute | solution.py:396
  33.3 3.8 %collective-permute-start.2 = (f32[4,22,8,128]{3,2,1,0:T(8,128)}, f32[4,22,8,128]{3,2,1,0:T(8,128)}, u32[]{:S(2)}, u32[]{:S(2)}) collective-permute-start(f32[4,22,8,128]{3,2,1,0:T(8,128)} %get-tuple-element.50), channel_id=1, source_target_pairs={{0,1},{1,2},{2,3},{4,5},{5,6},{6,7},{8,9},{9,10},{10,11},{12,13},{... | collective-permute-start | bytes 1081352 | tf_op jit(solution)/shard_map/ppermute | solution.py:401
  39.3 3.1 %collective-permute-start.6 = (f32[960,128]{1,0:T(8,128)}, f32[960,128]{1,0:T(8,128)}, u32[]{:S(2)}, u32[]{:S(2)}) collective-permute-start(f32[960,128]{1,0:T(8,128)} %get-tuple-element.27), channel_id=1, source_target_pairs={{0,1},{1,2},{2,3},{4,5},{5,6},{6,7},{8,9},{9,10},{10,11},{12,13},{... | collective-permute-start | bytes 1474568 | tf_op jit(solution)/shard_map/ppermute | solution.py:401
  49.0 3.5 %collective-permute-start.9 = (f32[1536,128]{1,0:T(8,128)S(1)}, f32[1536,128]{1,0:T(8,128)S(1)}, u32[]{:S(2)}, u32[]{:S(2)}) collective-permute-start(f32[1536,128]{1,0:T(8,128)S(1)} %bitcast.22), channel_id=1, source_target_pairs={{0,8},{8,16},{12,4},{16,24},{20,12},{28,20},{1,9},{9,17},{13,5},{1... | collective-permute-start | bytes 2359304 | tf_op jit(solution)/shard_map/ppermute | solution.py:396
  56.3 6.9 %both_solves.5.after.refs_0_ = f32[1,8,16,8,128]{4,3,2,1,0:T(8,128)S(1)} custom-call(s32[1]{0:T(128)} %bitcast.h_ref, f32[6,22,32,128]{3,2,1,0:T(8,128)S(1)} %coefficients.1.coef, f32[1024,128]{1,0:T(8,128)} %spread_probes.5.own, f32[1024,128]{1,0:T(8,128)} %collective-permute-done.4.recv, f32[768,128]{1,0:T(8,128)S(1)} %collective-permute-done.5.outer, ...), custom_call_target="tpu_custom_call" | custom-call | flops 34406400 | bytes 12582912 | tf_op jit(solution)/shard_map/both_solves/pallas_call | solution.py:256
  66.8 7.0 %collective-permute-start.10 = (f32[1920,128]{1,0:T(8,128)S(1)}, f32[1920,128]{1,0:T(8,128)S(1)}, u32[]{:S(2)}, u32[]{:S(2)}) collective-permute-start(f32[1920,128]{1,0:T(8,128)S(1)} %get-tuple-element.33), channel_id=1, source_target_pairs={{0,1},{1,2},{2,3},{4,5},{5,6},{6,7},{8,9},{9,10},{10,11},{12,13},{... | collective-permute-start | bytes 2949128 | tf_op jit(solution)/shard_map/ppermute | solution.py:401
  75.2 4.4 %collective-permute-start.13 = (f32[1536,128]{1,0:T(8,128)S(1)}, f32[1536,128]{1,0:T(8,128)S(1)}, u32[]{:S(2)}, u32[]{:S(2)}) collective-permute-start(f32[1536,128]{1,0:T(8,128)S(1)} %bitcast.20), channel_id=1, source_target_pairs={{0,8},{8,16},{12,4},{16,24},{20,12},{28,20},{1,9},{9,17},{13,5},{1... | collective-permute-start | bytes 2359304 | tf_op jit(solution)/shard_map/ppermute | solution.py:396
  79.6 10.4 %both_solves.6.after.refs_1_.refs_2_ = f32[2,8,16,8,128]{4,3,2,1,0:T(8,128)S(1)} custom-call(s32[1]{0:T(128)} %bitcast.h_ref, f32[6,22,32,128]{3,2,1,0:T(8,128)S(1)} %coefficients.1.coef, f32[2048,128]{1,0:T(8,128)S(1)} %spread_probes.6.own, f32[2048,128]{1,0:T(8,128)} %collective-permute-done.8.recv, f32[1536,128]{1,0:T(8,128)S(1)} %collective-permute-done.9.outer, ...), custom_call_target="tpu_custom_call" | custom-call | flops 68812800 | bytes 12582912 | tf_op jit(solution)/shard_map/both_solves/pallas_call | solution.py:256
  90.0 7.3 %collective-permute-done.16.recv = f32[2048,128]{1,0:T(8,128)S(1)} collective-permute-done((f32[2048,128]{1,0:T(8,128)S(1)}, f32[2048,128]{1,0:T(8,128)S(1)}, u32[]{:S(2)}, u32[]{:S(2)}) %collective-permute-start.16) | collective-permute-done | bytes 1048608 | tf_op jit(solution)/shard_map/ppermute | solution.py:391
  97.3 3.5 %collective-permute-start.17 = (f32[1536,128]{1,0:T(8,128)S(1)}, f32[1536,128]{1,0:T(8,128)S(1)}, u32[]{:S(2)}, u32[]{:S(2)}) collective-permute-start(f32[1536,128]{1,0:T(8,128)S(1)} %bitcast.21), channel_id=1, source_target_pairs={{0,8},{8,16},{12,4},{16,24},{20,12},{28,20},{1,9},{9,17},{13,5},{1... | collective-permute-start | bytes 2359304 | tf_op jit(solution)/shard_map/ppermute | solution.py:396
  101.4 6.7 %collective-permute-start.14 = (f32[1920,128]{1,0:T(8,128)S(1)}, f32[1920,128]{1,0:T(8,128)S(1)}, u32[]{:S(2)}, u32[]{:S(2)}) collective-permute-start(f32[1920,128]{1,0:T(8,128)S(1)} %get-tuple-element.38), channel_id=1, source_target_pairs={{0,1},{1,2},{2,3},{4,5},{5,6},{6,7},{8,9},{9,10},{10,11},{12,13},{... | collective-permute-start | bytes 2949128 | tf_op jit(solution)/shard_map/ppermute | solution.py:401
  109.4 5.1 %collective-permute-done.17.outer = f32[1536,128]{1,0:T(8,128)S(1)} collective-permute-done((f32[1536,128]{1,0:T(8,128)S(1)}, f32[1536,128]{1,0:T(8,128)S(1)}, u32[]{:S(2)}, u32[]{:S(2)}) %collective-permute-start.17) | collective-permute-done | bytes 786464 | tf_op jit(solution)/shard_map/ppermute | solution.py:396
  114.7 6.2 %collective-permute-start.18 = (f32[1920,128]{1,0:T(8,128)S(1)}, f32[1920,128]{1,0:T(8,128)S(1)}, u32[]{:S(2)}, u32[]{:S(2)}) collective-permute-start(f32[1920,128]{1,0:T(8,128)S(1)} %get-tuple-element.43), channel_id=1, source_target_pairs={{0,1},{1,2},{2,3},{4,5},{5,6},{6,7},{8,9},{9,10},{10,11},{12,13},{... | collective-permute-start | bytes 2949128 | tf_op jit(solution)/shard_map/ppermute | solution.py:401
  122.3 4.3 %collective-permute-start.21 = (f32[768,128]{1,0:T(8,128)S(1)}, f32[768,128]{1,0:T(8,128)S(1)}, u32[]{:S(2)}, u32[]{:S(2)}) collective-permute-start(f32[768,128]{1,0:T(8,128)S(1)} %bitcast.23), channel_id=1, source_target_pairs={{0,8},{8,16},{12,4},{16,24},{20,12},{28,20},{1,9},{9,17},{13,5},{1... | collective-permute-start | bytes 1179656 | tf_op jit(solution)/shard_map/ppermute | solution.py:396
  126.6 9.2 %both_solves.7.after.refs_3_.refs_4_ = f32[2,8,16,8,128]{4,3,2,1,0:T(8,128)S(1)} custom-call(s32[1]{0:T(128)} %bitcast.h_ref, f32[6,22,32,128]{3,2,1,0:T(8,128)S(1)} %coefficients.1.coef, f32[2048,128]{1,0:T(8,128)S(1)} %spread_probes.7.own, f32[2048,128]{1,0:T(8,128)S(1)} %collective-permute-done.12.recv, f32[1536,128]{1,0:T(8,128)S(1)} %collective-permute-done.13.outer, ...), custom_call_target="tpu_custom_call" | custom-call | flops 68812800 | bytes 12582912 | tf_op jit(solution)/shard_map/both_solves/pallas_call | solution.py:256
  135.8 3.1 %collective-permute-start.22 = (f32[960,128]{1,0:T(8,128)S(1)}, f32[960,128]{1,0:T(8,128)S(1)}, u32[]{:S(2)}, u32[]{:S(2)}) collective-permute-start(f32[960,128]{1,0:T(8,128)S(1)} %get-tuple-element.48), channel_id=1, source_target_pairs={{0,1},{1,2},{2,3},{4,5},{5,6},{6,7},{8,9},{9,10},{10,11},{12,13},{... | collective-permute-start | bytes 1474568 | tf_op jit(solution)/shard_map/ppermute | solution.py:401
  140.3 9.2 %both_solves.8.refs_5_.refs_6_ = f32[2,8,16,8,128]{4,3,2,1,0:T(8,128)S(1)} custom-call(s32[1]{0:T(128)} %bitcast.h_ref, f32[6,22,32,128]{3,2,1,0:T(8,128)S(1)} %coefficients.1.coef, f32[2048,128]{1,0:T(8,128)S(1)} %spread_probes.8.own, f32[2048,128]{1,0:T(8,128)S(1)} %collective-permute-done.16.recv, f32[1536,128]{1,0:T(8,128)S(1)} %collective-permute-done.17.outer, ...), custom_call_target="tpu_custom_call" | custom-call | flops 68812800 | bytes 12582912 | tf_op jit(solution)/shard_map/both_solves/pallas_call | solution.py:256
  149.5 5.4 %both_solves.9.refs_7_ = f32[1,8,16,8,128]{4,3,2,1,0:T(8,128)S(1)} custom-call(s32[1]{0:T(128)} %bitcast.h_ref, f32[6,22,32,128]{3,2,1,0:T(8,128)S(1)} %coefficients.1.coef, f32[1024,128]{1,0:T(8,128)S(1)} %spread_probes.9.own, f32[1024,128]{1,0:T(8,128)S(1)} %collective-permute-done.20.recv, f32[768,128]{1,0:T(8,128)S(1)} %collective-permute-done.21.outer, ...), custom_call_target="tpu_custom_call" | custom-call | flops 34406400 | bytes 12582912 | tf_op jit(solution)/shard_map/both_solves/pallas_call | solution.py:256
  165.0 3.9 %collective-permute-done.26 = f32[64,64]{1,0:T(8,128)S(1)} collective-permute-done((f32[64,64]{1,0:T(8,128)S(1)}, f32[64,64]{1,0:T(8,128)S(1)}, u32[]{:S(2)}, u32[]{:S(2)}) %collective-permute-start.26) | collective-permute-done | bytes 16416 | tf_op jit(solution)/shard_map/ppermute | solution.py:422
  174.3 3.3 %collective-permute-done.28.b_ref = f32[64,64]{1,0:T(8,128)S(1)} collective-permute-done((f32[64,64]{1,0:T(8,128)S(1)}, f32[64,64]{1,0:T(8,128)S(1)}, u32[]{:S(2)}, u32[]{:S(2)}) %collective-permute-start.28) | collective-permute-done | bytes 16416 | tf_op jit(solution)/shard_map/ppermute | solution.py:422
  177.7 10.3 %basis.1 = (f32[64,8,16,128]{3,2,1,0:T(8,128)}, f32[64,64]{1,0:T(8,128)}) custom-call(f32[64,64]{1,0:T(8,128)S(1)} %add.39.a_ref, f32[64,64]{1,0:T(8,128)S(1)} %collective-permute-done.28.b_ref, f32[1,8,16,8,128]{4,3,2,1,0:T(8,128)S(1)} %both_solves.5.after.refs_0_, f32[2,8,16,8,128]{4,3,2,1,0:T(8,128)S(1)} %both_solves.6.after.refs_1_.refs_2_, ...), custom_call_target="tpu_custom_call" | custom-call | bytes 8388608 | tf_op jit(solution)/shard_map/basis/pallas_call | solution.py:374
  (86 shorter events, 51.5 us)
Async XLA Ops:
  3.5 10.1 %collective-permute-start = (f32[4,8,16,128]{3,2,1,0:T(8,128)S(1)}, f32[4,8,16,128]{3,2,1,0:T(8,128)S(1)}, u32[]{:S(2)}, u32[]{:S(2)}) collective-permute-start(f32[4,8,16,128]{3,2,1,0:T(8,128)S(1)} %pad_maximum_fusion.2), channel_id=1, source_target_pairs={{0,4},{4,0},{8,12},{12,8},{16,20},{20,16},{24,28},{28,24},{1,5},{5... | collective-permute-start | bytes 786440 | tf_op jit(solution)/shard_map/ppermute | solution.py:391
  6.5 18.5 %collective-permute-start.4 = (f32[1024,128]{1,0:T(8,128)}, f32[1024,128]{1,0:T(8,128)}, u32[]{:S(2)}, u32[]{:S(2)}) collective-permute-start(f32[1024,128]{1,0:T(8,128)} %spread_probes.5.own), channel_id=1, source_target_pairs={{0,4},{4,0},{8,12},{12,8},{16,20},{20,16},{24,28},{28,24},{1,5},{5... | collective-permute-start | bytes 1572872 | tf_op jit(solution)/shard_map/ppermute | solution.py:391
  14.3 7.9 %collective-permute-start.1 = (f32[4,7,16,128]{3,2,1,0:T(8,128)}, f32[4,7,16,128]{3,2,1,0:T(8,128)}, u32[]{:S(2)}, u32[]{:S(2)}) collective-permute-start(f32[4,7,16,128]{3,2,1,0:T(8,128)} %constant_dynamic-slice_fusion.5), channel_id=1, source_target_pairs={{0,8},{8,16},{12,4},{16,24},{20,12},{28,20},{1,9},{9,17},{13,5},{1... | collective-permute-start | bytes 688136 | tf_op jit(solution)/shard_map/ppermute | solution.py:396
  19.9 27.8 %collective-permute-start.8 = (f32[2048,128]{1,0:T(8,128)S(1)}, f32[2048,128]{1,0:T(8,128)}, u32[]{:S(2)}, u32[]{:S(2)}) collective-permute-start(f32[2048,128]{1,0:T(8,128)S(1)} %spread_probes.6.own), channel_id=1, source_target_pairs={{0,4},{4,0},{8,12},{12,8},{16,20},{20,16},{24,28},{28,24},{1,5},{5... | collective-permute-start | bytes 3145736 | tf_op jit(solution)/shard_map/ppermute | solution.py:391
  26.0 11.1 %collective-permute-start.5 = (f32[768,128]{1,0:T(8,128)S(1)}, f32[768,128]{1,0:T(8,128)S(1)}, u32[]{:S(2)}, u32[]{:S(2)}) collective-permute-start(f32[768,128]{1,0:T(8,128)S(1)} %bitcast.24), channel_id=1, source_target_pairs={{0,8},{8,16},{12,4},{16,24},{20,12},{28,20},{1,9},{9,17},{13,5},{1... | collective-permute-start | bytes 1179656 | tf_op jit(solution)/shard_map/ppermute | solution.py:396
  32.0 11.8 %collective-permute-start.3 = (f32[4,22,8,128]{3,2,1,0:T(8,128)}, f32[4,22,8,128]{3,2,1,0:T(8,128)}, u32[]{:S(2)}, u32[]{:S(2)}) collective-permute-start(f32[4,22,8,128]{3,2,1,0:T(8,128)} %get-tuple-element.51), channel_id=1, source_target_pairs={{1,0},{2,1},{3,2},{5,4},{6,5},{7,6},{9,8},{10,9},{11,10},{13,12},{... | collective-permute-start | bytes 1081352 | tf_op jit(solution)/shard_map/ppermute | solution.py:406
  33.3 10.5 %collective-permute-start.2 = (f32[4,22,8,128]{3,2,1,0:T(8,128)}, f32[4,22,8,128]{3,2,1,0:T(8,128)}, u32[]{:S(2)}, u32[]{:S(2)}) collective-permute-start(f32[4,22,8,128]{3,2,1,0:T(8,128)} %get-tuple-element.50), channel_id=1, source_target_pairs={{0,1},{1,2},{2,3},{4,5},{5,6},{6,7},{8,9},{9,10},{10,11},{12,13},{... | collective-permute-start | bytes 1081352 | tf_op jit(solution)/shard_map/ppermute | solution.py:401
  39.3 8.4 %collective-permute-start.6 = (f32[960,128]{1,0:T(8,128)}, f32[960,128]{1,0:T(8,128)}, u32[]{:S(2)}, u32[]{:S(2)}) collective-permute-start(f32[960,128]{1,0:T(8,128)} %get-tuple-element.27), channel_id=1, source_target_pairs={{0,1},{1,2},{2,3},{4,5},{5,6},{6,7},{8,9},{9,10},{10,11},{12,13},{... | collective-permute-start | bytes 1474568 | tf_op jit(solution)/shard_map/ppermute | solution.py:401
  42.4 5.3 %collective-permute-start.7 = (f32[960,128]{1,0:T(8,128)}, f32[960,128]{1,0:T(8,128)}, u32[]{:S(2)}, u32[]{:S(2)}) collective-permute-start(f32[960,128]{1,0:T(8,128)} %get-tuple-element.29), channel_id=1, source_target_pairs={{1,0},{2,1},{3,2},{5,4},{6,5},{7,6},{9,8},{10,9},{11,10},{13,12},{... | collective-permute-start | bytes 1474568 | tf_op jit(solution)/shard_map/ppermute | solution.py:406
  49.0 16.5 %collective-permute-start.9 = (f32[1536,128]{1,0:T(8,128)S(1)}, f32[1536,128]{1,0:T(8,128)S(1)}, u32[]{:S(2)}, u32[]{:S(2)}) collective-permute-start(f32[1536,128]{1,0:T(8,128)S(1)} %bitcast.22), channel_id=1, source_target_pairs={{0,8},{8,16},{12,4},{16,24},{20,12},{28,20},{1,9},{9,17},{13,5},{1... | collective-permute-start | bytes 2359304 | tf_op jit(solution)/shard_map/ppermute | solution.py:396
  53.3 21.8 %collective-permute-start.12 = (f32[2048,128]{1,0:T(8,128)S(1)}, f32[2048,128]{1,0:T(8,128)S(1)}, u32[]{:S(2)}, u32[]{:S(2)}) collective-permute-start(f32[2048,128]{1,0:T(8,128)S(1)} %spread_probes.7.own), channel_id=1, source_target_pairs={{0,4},{4,0},{8,12},{12,8},{16,20},{20,16},{24,28},{28,24},{1,5},{5... | collective-permute-start | bytes 3145736 | tf_op jit(solution)/shard_map/ppermute | solution.py:391
  54.2 43.1 %collective-permute-start.16 = (f32[2048,128]{1,0:T(8,128)S(1)}, f32[2048,128]{1,0:T(8,128)S(1)}, u32[]{:S(2)}, u32[]{:S(2)}) collective-permute-start(f32[2048,128]{1,0:T(8,128)S(1)} %spread_probes.8.own), channel_id=1, source_target_pairs={{0,4},{4,0},{8,12},{12,8},{16,20},{20,16},{24,28},{28,24},{1,5},{5... | collective-permute-start | bytes 3145736 | tf_op jit(solution)/shard_map/ppermute | solution.py:391
  66.8 12.8 %collective-permute-start.10 = (f32[1920,128]{1,0:T(8,128)S(1)}, f32[1920,128]{1,0:T(8,128)S(1)}, u32[]{:S(2)}, u32[]{:S(2)}) collective-permute-start(f32[1920,128]{1,0:T(8,128)S(1)} %get-tuple-element.33), channel_id=1, source_target_pairs={{0,1},{1,2},{2,3},{4,5},{5,6},{6,7},{8,9},{9,10},{10,11},{12,13},{... | collective-permute-start | bytes 2949128 | tf_op jit(solution)/shard_map/ppermute | solution.py:401
  73.8 5.8 %collective-permute-start.11 = (f32[1920,128]{1,0:T(8,128)S(1)}, f32[1920,128]{1,0:T(8,128)S(1)}, u32[]{:S(2)}, u32[]{:S(2)}) collective-permute-start(f32[1920,128]{1,0:T(8,128)S(1)} %get-tuple-element.34), channel_id=1, source_target_pairs={{1,0},{2,1},{3,2},{5,4},{6,5},{7,6},{9,8},{10,9},{11,10},{13,12},{... | collective-permute-start | bytes 2949128 | tf_op jit(solution)/shard_map/ppermute | solution.py:406
  75.2 26.1 %collective-permute-start.13 = (f32[1536,128]{1,0:T(8,128)S(1)}, f32[1536,128]{1,0:T(8,128)S(1)}, u32[]{:S(2)}, u32[]{:S(2)}) collective-permute-start(f32[1536,128]{1,0:T(8,128)S(1)} %bitcast.20), channel_id=1, source_target_pairs={{0,8},{8,16},{12,4},{16,24},{20,12},{28,20},{1,9},{9,17},{13,5},{1... | collective-permute-start | bytes 2359304 | tf_op jit(solution)/shard_map/ppermute | solution.py:396
  97.3 17.3 %collective-permute-start.17 = (f32[1536,128]{1,0:T(8,128)S(1)}, f32[1536,128]{1,0:T(8,128)S(1)}, u32[]{:S(2)}, u32[]{:S(2)}) collective-permute-start(f32[1536,128]{1,0:T(8,128)S(1)} %bitcast.21), channel_id=1, source_target_pairs={{0,8},{8,16},{12,4},{16,24},{20,12},{28,20},{1,9},{9,17},{13,5},{1... | collective-permute-start | bytes 2359304 | tf_op jit(solution)/shard_map/ppermute | solution.py:396
  101.2 21.0 %collective-permute-start.20 = (f32[1024,128]{1,0:T(8,128)S(1)}, f32[1024,128]{1,0:T(8,128)S(1)}, u32[]{:S(2)}, u32[]{:S(2)}) collective-permute-start(f32[1024,128]{1,0:T(8,128)S(1)} %spread_probes.9.own), channel_id=1, source_target_pairs={{0,4},{4,0},{8,12},{12,8},{16,20},{20,16},{24,28},{28,24},{1,5},{5... | collective-permute-start | bytes 1572872 | tf_op jit(solution)/shard_map/ppermute | solution.py:391
  101.4 25.1 %collective-permute-start.14 = (f32[1920,128]{1,0:T(8,128)S(1)}, f32[1920,128]{1,0:T(8,128)S(1)}, u32[]{:S(2)}, u32[]{:S(2)}) collective-permute-start(f32[1920,128]{1,0:T(8,128)S(1)} %get-tuple-element.38), channel_id=1, source_target_pairs={{0,1},{1,2},{2,3},{4,5},{5,6},{6,7},{8,9},{9,10},{10,11},{12,13},{... | collective-permute-start | bytes 2949128 | tf_op jit(solution)/shard_map/ppermute | solution.py:401
  108.1 18.4 %collective-permute-start.15 = (f32[1920,128]{1,0:T(8,128)S(1)}, f32[1920,128]{1,0:T(8,128)S(1)}, u32[]{:S(2)}, u32[]{:S(2)}) collective-permute-start(f32[1920,128]{1,0:T(8,128)S(1)} %get-tuple-element.39), channel_id=1, source_target_pairs={{1,0},{2,1},{3,2},{5,4},{6,5},{7,6},{9,8},{10,9},{11,10},{13,12},{... | collective-permute-start | bytes 2949128 | tf_op jit(solution)/shard_map/ppermute | solution.py:406
  114.7 25.6 %collective-permute-start.18 = (f32[1920,128]{1,0:T(8,128)S(1)}, f32[1920,128]{1,0:T(8,128)S(1)}, u32[]{:S(2)}, u32[]{:S(2)}) collective-permute-start(f32[1920,128]{1,0:T(8,128)S(1)} %get-tuple-element.43), channel_id=1, source_target_pairs={{0,1},{1,2},{2,3},{4,5},{5,6},{6,7},{8,9},{9,10},{10,11},{12,13},{... | collective-permute-start | bytes 2949128 | tf_op jit(solution)/shard_map/ppermute | solution.py:401
  120.9 19.4 %collective-permute-start.19 = (f32[1920,128]{1,0:T(8,128)S(1)}, f32[1920,128]{1,0:T(8,128)S(1)}, u32[]{:S(2)}, u32[]{:S(2)}) collective-permute-start(f32[1920,128]{1,0:T(8,128)S(1)} %get-tuple-element.44), channel_id=1, source_target_pairs={{1,0},{2,1},{3,2},{5,4},{6,5},{7,6},{9,8},{10,9},{11,10},{13,12},{... | collective-permute-start | bytes 2949128 | tf_op jit(solution)/shard_map/ppermute | solution.py:406
  122.3 13.5 %collective-permute-start.21 = (f32[768,128]{1,0:T(8,128)S(1)}, f32[768,128]{1,0:T(8,128)S(1)}, u32[]{:S(2)}, u32[]{:S(2)}) collective-permute-start(f32[768,128]{1,0:T(8,128)S(1)} %bitcast.23), channel_id=1, source_target_pairs={{0,8},{8,16},{12,4},{16,24},{20,12},{28,20},{1,9},{9,17},{13,5},{1... | collective-permute-start | bytes 1179656 | tf_op jit(solution)/shard_map/ppermute | solution.py:396
  135.8 13.6 %collective-permute-start.22 = (f32[960,128]{1,0:T(8,128)S(1)}, f32[960,128]{1,0:T(8,128)S(1)}, u32[]{:S(2)}, u32[]{:S(2)}) collective-permute-start(f32[960,128]{1,0:T(8,128)S(1)} %get-tuple-element.48), channel_id=1, source_target_pairs={{0,1},{1,2},{2,3},{4,5},{5,6},{6,7},{8,9},{9,10},{10,11},{12,13},{... | collective-permute-start | bytes 1474568 | tf_op jit(solution)/shard_map/ppermute | solution.py:401
  139.0 10.5 %collective-permute-start.23 = (f32[960,128]{1,0:T(8,128)S(1)}, f32[960,128]{1,0:T(8,128)S(1)}, u32[]{:S(2)}, u32[]{:S(2)}) collective-permute-start(f32[960,128]{1,0:T(8,128)S(1)} %get-tuple-element.49), channel_id=1, source_target_pairs={{1,0},{2,1},{3,2},{5,4},{6,5},{7,6},{9,8},{10,9},{11,10},{13,12},{... | collective-permute-start | bytes 1474568 | tf_op jit(solution)/shard_map/ppermute | solution.py:406
  (14 other events, 76.6 us)
